TPU v7x, 32 devices: a whole 2x2x4 slice. The times are simulated.
32 devices in a mesh: rep: 8 (over y, x, core), tp: 4 (over z).
Axes of the slice: x: 2, y: 2, z: 4, core: 2. Of those that a mesh axis runs over, the one named last changes fastest.
Arguments:
- hidden_in: bfloat16 [768, 8192], P('rep', 'tp'), may hold values from -6 to 6
- queries: bfloat16 [768, 8192], P('rep', 'tp'), may hold values from -20 to 20
- cache_keys: bfloat16 [768, 128, 1024], P('rep', None, 'tp'), may hold values from -6 to 6
- cached_value_rows: bfloat16 [768, 128, 1024], P('rep', None, 'tp'), may hold values from -6 to 6
- cache_lengths: int32 [768], P('rep'), may hold values from 1 to 128, 24576 in all
- base_key_matrix: bfloat16 [8192, 1024], P(None, 'tp'), may hold values from -0.0625 to 0.0625
- base_value_matrix: bfloat16 [8192, 1024], P(None, 'tp'), may hold values from -0.0625 to 0.0625
- shrink_weights: bfloat16 [32, 8192, 128], P('rep', 'tp'), may hold values from -0.0625 to 0.0625
- pooled_up_weights: bfloat16 [32, 2, 64, 1024], P('rep', None, None, 'tp'), may hold values from -0.75 to 0.75
- block_owner: int32 [192, 1], P('rep'), may hold values from 0 to 7; in each aligned block of 24 rows (0 to 23, 24 to 47, ...) at most 6 rows name the same one
- block_slot: int32 [192], P('rep'), may hold values from 0 to 3
Outputs:
- new_keys: bfloat16 [768, 1024], P('rep', 'tp')
- new_values: bfloat16 [768, 1024], P('rep', 'tp')
- context: bfloat16 [768, 8192], P('rep', 'tp')
Inputs may be any that keep to these rules, and one draw needn't show every extreme that they name: `block_owner`: among the 24 blocks of one replica group at most 6 name the same owner, and some group in every draw has 6 blocks with one owner.
All inputs are finite; a program needn't handle non-finite values. No bound on the sum of `cache_lengths` on one device may be relied on, other than what follows from the above.
Results may differ from a plain program's by a relative error of at most 0.0055.
Values may be sent and summed in bfloat16 or wider, within the bound.
No kernel may reach another device: no remote copies, remote signals or barrier semaphores. Data moves between devices by JAX's collectives and lax.ppermute only.
A program may use at most 128 MiB of HBM per device.

v0:
```python
import jax
import jax.numpy as jnp
from jax import lax
from jax.sharding import PartitionSpec as P

HEAD_SIZE = 128
BLK = 4


adapter_scale = 0.5
masked_score = -1e30


def attend(group_queries, key_cache, value_cache, lengths, fresh_keys, fresh_values):
    rows_here = group_queries.shape[0]
    head_groups = key_cache.shape[2] // HEAD_SIZE
    group_size = group_queries.shape[1] // (head_groups * HEAD_SIZE)
    window = key_cache.shape[1]
    inverse_root = HEAD_SIZE ** (-0.5)
    query_heads = group_queries.reshape(rows_here, head_groups, group_size, HEAD_SIZE)
    key_heads = key_cache.reshape(rows_here, window, head_groups, HEAD_SIZE)
    value_heads = value_cache.reshape(rows_here, window, head_groups, HEAD_SIZE)
    scores = (
        jnp.einsum("rkgd,rtkd->rkgt", query_heads, key_heads, preferred_element_type=jnp.float32)
        * inverse_root
    )
    own_score = (
        jnp.einsum(
            "rkgd,rkd->rkg",
            query_heads,
            fresh_keys.reshape(rows_here, head_groups, HEAD_SIZE),
            preferred_element_type=jnp.float32,
        )
        * inverse_root
    )
    visible = (jnp.arange(window, dtype=jnp.int32)[None, :] < lengths[:, None])[:, None, None, :]
    highest = jnp.maximum(jnp.max(jnp.where(visible, scores, masked_score), axis=-1), own_score)
    exp_terms = jnp.where(visible, jnp.exp(scores - highest[..., None]), 0.0)
    own_term = jnp.exp(own_score - highest)
    denominator = jnp.sum(exp_terms, axis=-1) + own_term
    weights = (exp_terms / denominator[..., None]).astype(jnp.bfloat16)
    own_weight = (own_term / denominator).astype(jnp.bfloat16)
    context = jnp.einsum(
        "rkgt,rtkd->rkgd", weights, value_heads, preferred_element_type=jnp.float32
    )
    context = context + own_weight.astype(jnp.float32)[..., None] * fresh_values.reshape(
        rows_here, head_groups, 1, HEAD_SIZE
    ).astype(jnp.float32)
    return context.reshape(rows_here, -1).astype(jnp.bfloat16)


def earlier_ranks(owners):
    span_count = owners.shape[-1]
    matching = owners[..., :, None] == owners[..., None, :]
    before = jnp.arange(span_count)[:, None] > jnp.arange(span_count)[None, :]
    return jnp.sum((matching & before).astype(jnp.int32), axis=-1)


def slot_layout(owners_all, slots_all, myself, replicas, blocks_here, capacity):
    owners_grid = owners_all.reshape(replicas, blocks_here)
    slots_grid = slots_all.reshape(replicas, blocks_here)
    ranks_grid = earlier_ranks(owners_grid)
    placed = (owners_grid == myself)[:, :, None] & (
        ranks_grid[:, :, None] == jnp.arange(capacity, dtype=jnp.int32)[None, None, :]
    )
    placed_int = placed.astype(jnp.int32)
    slot_index = jnp.sum(placed_int * slots_grid[:, :, None], axis=1).reshape(replicas * capacity)
    return (placed, slot_index)


def adapter_pass(slot_rows, slot_index, shrink_weights, pooled_up_weights, site_sum):
    chosen_shrink = jnp.take(shrink_weights, slot_index, axis=0)
    selected_expand = jnp.take(pooled_up_weights, slot_index, axis=0)
    partial_value = jnp.einsum(
        "snd,sdr->snr", slot_rows, chosen_shrink, preferred_element_type=jnp.float32
    )
    shrunk = site_sum(partial_value).astype(jnp.bfloat16)
    split_halves = shrunk.reshape(shrunk.shape[0], shrunk.shape[1], 2, shrunk.shape[2] // 2)
    summed_terms = jnp.einsum(
        "snkr,skrw->snkw", split_halves, selected_expand, preferred_element_type=jnp.float32
    )
    return (adapter_scale * summed_terms).astype(jnp.bfloat16)


def shards(
    hidden_in,
    queries,
    cache_keys,
    cached_value_rows,
    cache_lengths,
    base_key_matrix,
    base_value_matrix,
    shrink_weights,
    pooled_up_weights,
    block_owner,
    block_slot,
):
    rows_here = hidden_in.shape[0]
    shard_width = hidden_in.shape[1]
    replicas = lax.axis_size("rep")
    myself = lax.axis_index("rep")
    blocks_here = rows_here // BLK
    capacity = max(2, (2 * blocks_here + replicas - 1) // replicas)
    key_row_width = base_key_matrix.shape[1]
    gathered = lax.all_gather(hidden_in, "tp", axis=1, tiled=True)
    base_keys = jnp.dot(gathered, base_key_matrix, preferred_element_type=jnp.float32)
    base_values = jnp.dot(gathered, base_value_matrix, preferred_element_type=jnp.float32)
    owners_all, slots_all = (
        lax.all_gather(block_owner[:, 0], "rep", axis=0, tiled=True),
        lax.all_gather(block_slot, "rep", axis=0, tiled=True),
    )
    placed, slot_index = slot_layout(owners_all, slots_all, myself, replicas, blocks_here, capacity)
    my_owners = block_owner[:, 0]
    targets = my_owners * capacity + earlier_ranks(my_owners)
    picker = (jnp.arange(replicas * capacity, dtype=jnp.int32)[:, None] == targets[None, :]).astype(
        jnp.bfloat16
    )
    outgoing = jnp.dot(
        picker,
        hidden_in.reshape(blocks_here, BLK * shard_width),
        preferred_element_type=jnp.float32,
    ).astype(jnp.bfloat16)
    arrived = lax.all_to_all(
        outgoing.reshape(replicas, capacity * BLK, shard_width),
        "rep",
        split_axis=0,
        concat_axis=0,
        tiled=True,
    )
    slot_rows = arrived.reshape(replicas * capacity, BLK, shard_width)

    def sum_sent(partial_value):
        return lax.psum(partial_value, "tp")

    deltas = adapter_pass(slot_rows, slot_index, shrink_weights, pooled_up_weights, sum_sent)
    returned = lax.all_to_all(
        deltas.reshape(replicas, capacity * BLK, 2 * key_row_width),
        "rep",
        split_axis=0,
        concat_axis=0,
        tiled=True,
    )
    own_rows = jnp.einsum(
        "qb,qx->bx",
        picker,
        returned.reshape(replicas * capacity, BLK * 2 * key_row_width),
        preferred_element_type=jnp.float32,
    )
    per_row_delta = own_rows.reshape(rows_here, 2, key_row_width)
    fresh_keys = (base_keys + per_row_delta[:, 0]).astype(jnp.bfloat16)
    fresh_values = (base_values + per_row_delta[:, 1]).astype(jnp.bfloat16)
    context = attend(
        queries, cache_keys, cached_value_rows, cache_lengths, fresh_keys, fresh_values
    )
    return (fresh_keys, fresh_values, context)


def solution(mesh):
    return jax.shard_map(
        shards,
        mesh=mesh,
        in_specs=(
            P("rep", "tp"),
            P("rep", "tp"),
            P("rep", None, "tp"),
            P("rep", None, "tp"),
            P("rep"),
            P(None, "tp"),
            P(None, "tp"),
            P("rep", "tp", None),
            P("rep", None, None, "tp"),
            P("rep", None),
            P("rep"),
        ),
        out_specs=(P("rep", "tp"), P("rep", "tp"), P("rep", "tp")),
        check_vma=False,
    )
```

profile of v0, /device:TPU:0, one launch (start us, length us, event | category | flops | bytes accessed | tf_op | source)
XLA Modules:
  0.0 123.8 jit_solution(11313989197408413024)
XLA Ops:
  7.2 0.7 all-gather.3.cloned.1.call-update
  7.9 1.3 %reshape.146 = bf16[24,8192]{1,0:T(8,128)(2,1)S(1)} reshape(bf16[96,2048]{1,0:T(8,128)(2,1)} %param.11) | data formatting | bytes 786432 | tf_op jit(solution)/shard_map/reshape | solution.py:120
  9.2 0.9 convert_reduce_fusion.1
  10.2 1.2 %dynamic-slice = u32[1]{0:T(128)} dynamic-slice(u32[32]{0:T(128)} %constant.53, u32[]{:T(128)S(6)} %add.55), dynamic_slice_sizes={1} | dynamic-slice | bytes 12
  12.1 0.7 multiply_add_fusion
  12.8 0.3 convolution_convert_fusion
  13.2 1.5 %reshape.147 = bf16[8,24,2048]{2,1,0:T(8,128)(2,1)} reshape(bf16[48,8192]{1,0:T(8,128)(2,1)S(1)} %convolution_convert_fusion) | data formatting | bytes 1572864 | tf_op jit(solution)/shard_map/reshape | solution.py:124
  14.7 5.2 %all-to-all-start = ((bf16[8,24,2048]{2,1,0:T(8,128)(2,1)}), bf16[8,24,2048]{2,1,0:T(8,128)(2,1)S(1)}, u32[]{:S(2)}, u32[]{:S(2)}) async-start(bf16[8,24,2048]{2,1,0:T(8,128)(2,1)} %reshape.147), calls=%async_computation | async-start | bytes 1572864 | tf_op jit(solution)/shard_map/all_to_all | solution.py:123
  19.9 0.2 dynamic-update-slice.1
  20.1 14.6 %all-reduce.2 = (s32[192]{0:T(256)S(1)}, s32[192]{0:T(256)S(1)}) all-reduce(s32[192]{0:T(256)S(1)} %dynamic-update-slice.1, s32[192]{0:T(256)S(1)} %get-tuple-element.10), channel_id=1, replica_groups=mesh['rep'=8,'tp'=4] {'rep'}, use_global_device_ids=true, to_apply=%add.1 | all-reduce | flops 384 | bytes 3072
  34.7 0.1 reshape.143
  34.8 0.3 convert_reduce_fusion
  35.1 0.1 mul.50
  35.2 0.2 select_reduce_fusion.1
  35.4 0.1 copy.42
  35.5 0.1 reshape.145
  35.5 0.1 reshape.144
  35.7 9.6 %gather_fusion.1 = bf16[48,2048,128]{2,1,0:T(8,128)(2,1)} fusion(bf16[4,2048,128]{2,1,0:T(8,128)(2,1)S(1)} %copy-done, s32[1024]{0:T(1024)S(1)} %pad_clamp_fusion), kind=kCustom, calls=%fused_computation.1 | custom fusion | bytes 50331840 | tf_op jit(solution)/shard_map/jit(_take)/gather | solution.py:72
  45.3 2.6 %gather_fusion = bf16[48,2,64,256]{3,2,1,0:T(8,128)(2,1)} fusion(bf16[4,2,64,256]{3,2,1,0:T(8,128)(2,1)S(1)} %copy-done.1, s32[1024]{0:T(1024)S(1)} %pad_clamp_fusion), kind=kCustom, calls=%fused_computation | custom fusion | bytes 6291648 | tf_op jit(solution)/shard_map/jit(_take)/gather | solution.py:73
  47.9 1.1 copy.61
  49.0 0.7 iota_compare_fusion
  49.7 1.2 reshape.148
  50.9 10.4 %fusion = f32[48,4,128]{2,1,0:T(4,128)S(1)} fusion(bf16[48,4,2048]{2,1,0:T(4,128)(2,1)} %reshape.148, bf16[48,2048,128]{2,1,0:T(8,128)(2,1)} %gather_fusion.1, pred[48]{0:T(512)(128)(4,1)S(1)} %compare_and_fusion), kind=kOutput, calls=%fused_computation.2 | convolution fusion | flops 113246208 | bytes 26050608 | tf_op jit(solution)/shard_map/snd,sdr->snr/dot_general | solution.py:74
  61.4 20.4 %psum.7 = bf16[48,4,128]{2,1,0:T(4,128)(2,1)S(1)} all-reduce(f32[48,4,128]{2,1,0:T(4,128)S(1)} %fusion), channel_id=1, replica_groups=mesh['rep'=8,'tp'=4] {'tp'}, use_global_device_ids=true, to_apply=%region_3.4 | all-reduce | flops 24576 | bytes 147456 | tf_op jit(solution)/shard_map/psum | solution.py:133
  81.8 0.1 reshape.149
  81.9 2.5 %fusion.29 = bf16[48,4,2,256]{3,1,2,0:T(4,128)(2,1)S(1)} fusion(bf16[48,2,64,256]{3,2,1,0:T(8,128)(2,1)} %gather_fusion, pred[48]{0:T(512)(128)(4,1)S(1)} %compare_and_fusion, bf16[48,4,2,64]{3,2,1,0:T(2,128)(2,1)S(1)} %reshape.149), kind=kOutput, calls=%fused_computation.22 | convolution fusion | flops 14352384 | bytes 3391536 | tf_op jit(solution)/shard_map/snkr,skrw->snkw/dot_general | solution.py:79
  84.4 0.2 copy.45
  84.6 0.8 reshape.150
  85.4 3.6 %all-to-all-start.1 = ((bf16[8,24,512]{2,1,0:T(8,128)(2,1)}), bf16[8,24,512]{2,1,0:T(8,128)(2,1)S(1)}, u32[]{:S(2)}, u32[]{:S(2)}) async-start(bf16[8,24,512]{2,1,0:T(8,128)(2,1)} %reshape.150), calls=%async_computation.1 | async-start | bytes 393216 | tf_op jit(solution)/shard_map/all_to_all | solution.py:136
  89.0 6.2 %select_reduce_fusion = (f32[96,2,8]{2,1,0:T(2,128)}, f32[96,2,8,128]{3,2,1,0:T(8,128)S(1)}) fusion(pred[96,128]{1,0:T(8,128)(4,1)S(1)} %iota_compare_fusion, bf16[96,2,8,128]{3,2,1,0:T(8,128)(2,1)S(1)} %bitcast.72, bf16[96,128,256]{2,1,0:T(8,128)(2,1)} %param.13), kind=kOutput, calls=%fused_computation.29 | convolution fusion | flops 50919936 | bytes 7489536 | tf_op jit(solution)/shard_map/rkgd,rtkd->rkgt/dot_general | solution.py:24
  95.2 0.9 copy.49
  96.1 0.8 reshape.151
  96.9 1.8 %fusion.40 = f32[24,2048]{1,0:T(8,128)} fusion(bf16[48,2048]{1,0:T(8,128)(2,1)} %reshape.151, s32[24]{0:T(128)S(1)} %get-tuple-element.9), kind=kOutput, calls=%fused_computation.44 | convolution fusion | flops 4719744 | bytes 393312 | tf_op jit(solution)/shard_map/qb,qx->bx/dot_general | solution.py:143
  98.8 1.1 reshape.152
  99.8 0.8 fusion.51
  100.7 3.5 %fusion.32 = bf16[96,256]{1,0:T(8,128)(2,1)S(1)} fusion(bf16[96,8192]{1,0:T(8,128)(2,1)} %all-gather.3.cloned.1.call-done, bf16[8192,256]{1,0:T(8,128)(2,1)} %param.16, f32[96,1,256]{2,1,0:T(1,128)} %get-tuple-element.6), kind=kOutput, calls=%fused_computation.25 | convolution fusion | flops 402702336 | bytes 5914624 | tf_op jit(solution)/shard_map/dot_general | solution.py:106
  104.2 1.0 fusion.52
  105.2 0.9 copy.56
  106.2 0.1 copy.50
  106.3 0.6 fusion.34
  106.9 0.1 copy.51
  107.0 0.7 fusion.46
  107.7 0.1 copy.52
  107.8 0.1 copy.54
  108.0 3.5 %fusion.33 = bf16[96,256]{1,0:T(8,128)(2,1)S(1)} fusion(bf16[96,8192]{1,0:T(8,128)(2,1)} %all-gather.3.cloned.1.call-done, bf16[8192,256]{1,0:T(8,128)(2,1)} %param.17, f32[96,1,256]{2,1,0:T(1,128)S(1)} %copy-done.2), kind=kOutput, calls=%fused_computation.26 | convolution fusion | flops 402702336 | bytes 5914624 | tf_op jit(solution)/shard_map/dot_general | solution.py:107
  111.5 0.1 reshape.157
  111.5 4.6 %fusion.20 = bf16[96,2,8,128]{3,2,1,0:T(8,128)(2,1)S(1)} fusion(f32[96,2,8,128]{3,2,1,0:T(8,128)S(1)} %get-tuple-element.12, f32[96,2,128]{2,1,0:T(2,128)S(1)} %reshape.157, f32[96,2,8]{2,1,0:T(2,128)S(1)} %copy.54, f32[96,2,8]{2,1,0:T(2,128)S(1)} %copy.52, f32[96,2,8]{2,1,0:T(2,128)S(1)} %copy.50, pred[96,128]{1,0:T(8,128)(4,1)S(1)} %iota_compare_fusion, ...), kind=kOutput, calls=%fused_computation.19 | convolution fusion | flops 51707904 | bytes 7600128 | tf_op jit(solution)/shard_map/rkgt,rtkd->rkgd/dot_general | solution.py:43
  116.1 0.9 copy.88
  (27 shorter events, 0.2 us)
Async XLA Ops:
  7.2 28.5 %copy-start = (bf16[4,2048,128]{2,1,0:T(8,128)(2,1)S(1)}, bf16[4,2048,128]{2,1,0:T(8,128)(2,1)}, u32[]{:S(2)}) copy-start(bf16[4,2048,128]{2,1,0:T(8,128)(2,1)} %param.18) | copy-start | bytes 6291460
  7.2 12.7 %copy-start.6 = (s32[24]{0:T(128)S(1)}, s32[24]{0:T(128)}, u32[]{:S(2)}) copy-start(s32[24]{0:T(128)} %param.21) | copy-start | bytes 292
  7.2 93.5 %all-gather.3.cloned.1.call-start = ((), (), s32[]{:S(2)}) async-start(), calls=%async_computation.2 | async-start | bytes 1966080 | tf_op jit(solution)/shard_map/all_gather | solution.py:105
  14.7 35.0 %all-to-all-start = ((bf16[8,24,2048]{2,1,0:T(8,128)(2,1)}), bf16[8,24,2048]{2,1,0:T(8,128)(2,1)S(1)}, u32[]{:S(2)}, u32[]{:S(2)}) async-start(bf16[8,24,2048]{2,1,0:T(8,128)(2,1)} %reshape.147), calls=%async_computation | async-start | bytes 1572864 | tf_op jit(solution)/shard_map/all_to_all | solution.py:123
  35.7 9.6 %copy-start.1 = (bf16[4,2,64,256]{3,2,1,0:T(8,128)(2,1)S(1)}, bf16[4,2,64,256]{3,2,1,0:T(8,128)(2,1)}, u32[]{:S(2)}) copy-start(bf16[4,2,64,256]{3,2,1,0:T(8,128)(2,1)} %param.19) | copy-start | bytes 786436
  85.4 10.7 %all-to-all-start.1 = ((bf16[8,24,512]{2,1,0:T(8,128)(2,1)}), bf16[8,24,512]{2,1,0:T(8,128)(2,1)S(1)}, u32[]{:S(2)}, u32[]{:S(2)}) async-start(bf16[8,24,512]{2,1,0:T(8,128)(2,1)} %reshape.150), calls=%async_computation.1 | async-start | bytes 393216 | tf_op jit(solution)/shard_map/all_to_all | solution.py:136
  96.1 10.0 %copy-start.5 = (f32[96,2,8]{0,2,1:T(8,128)}, f32[96,2,8]{0,2,1:T(8,128)S(1)}, u32[]{:S(2)}) copy-start(f32[96,2,8]{0,2,1:T(8,128)S(1)} %copy.49) | copy-start | bytes 18436
  100.7 7.3 %copy-start.2 = (f32[96,1,256]{2,1,0:T(1,128)S(1)}, f32[96,1,256]{2,1,0:T(1,128)}, u32[]{:S(2)}) copy-start(f32[96,1,256]{2,1,0:T(1,128)} %get-tuple-element.5) | copy-start | bytes 294916
  104.2 2.0 %copy-start.3 = (bf16[96,256]{1,0:T(8,128)(2,1)}, bf16[96,256]{1,0:T(8,128)(2,1)S(1)}, u32[]{:S(2)}) copy-start(bf16[96,256]{1,0:T(8,128)(2,1)S(1)} %fusion.32) | copy-start | bytes 147460
  111.5 4.7 %copy-start.4 = (bf16[96,256]{1,0:T(8,128)(2,1)}, bf16[96,256]{1,0:T(8,128)(2,1)S(1)}, u32[]{:S(2)}) copy-start(bf16[96,256]{1,0:T(8,128)(2,1)S(1)} %fusion.33) | copy-start | bytes 147460
Sparse Core Ops, SparseCore 0:
  9.6 39.7 all-gather.2
where the time goes:
time: 125 us; the launch traced here: 124 us
  blocking collectives  35 us (28%)
  matrix products  33.8 us (27%)
  local copies, waits for them, and re-layouts  26.3 us (21%)
  between operations  14.9 us (12%)
  starting transfers between devices  8.78 us (7%)
  other arithmetic  4.25 us (3%)
    psum x1, blocking collectives, sum_sent(): return lax.psum(partial_value, 'tp')  20.4 us
    unnamed x1, blocking collectives  14.6 us
    dot_general x1, matrix products, adapter_pass(): jnp.einsum('snd,sdr->snr', slot_rows, chosen_shrink, preferred_element_ty...  10.4 us
    gather x1, local copies, waits for them, and re-layouts, adapter_pass(): chosen_shrink = jnp.take(shrink_weights, slot_index, axis=0)  9.59 us
    dot_general x1, matrix products, attend(): jnp.einsum('rkgd,rtkd->rkgt', query_heads, key_heads, preferred_element_t...  6.21 us
    all_to_all x1, starting transfers between devices, shards(): lax.all_to_all(outgoing.reshape(replicas, capacity * BLK, shard_width), '...  5.17 us
    dot_general x1, matrix products, attend(): jnp.einsum('rkgt,rtkd->rkgd', weights, value_heads, preferred_element_typ...  4.58 us
    all_to_all x1, starting transfers between devices, shards(): lax.all_to_all(deltas.reshape(replicas, capacity * BLK, 2 * key_row_width...  3.57 us
  transfers between devices with their start and end apart: 3, of which 0 were waited for; matrix products, arithmetic and copies ran while one was open for 39% of the time, Pallas kernels for 0%

commit v1 on v0

v1 whole, which is shorter than its diff:
```python
import functools

import jax
import jax.numpy as jnp
from jax import lax
from jax.experimental import pallas as pl
from jax.experimental.pallas import tpu as pltpu
from jax.sharding import PartitionSpec as P

HEAD_SIZE = 128
BLK = 4
LANES = 128
MIB = 1 << 20

adapter_scale = 0.5
masked_score = -1e30


def params(mib):
    return pltpu.CompilerParams(vmem_limit_bytes=mib * MIB)


def cost(flops, moved, exps=0):
    return pl.CostEstimate(flops=flops, bytes_accessed=moved, transcendentals=exps)


def iota(shape, dim):
    return lax.broadcasted_iota(jnp.int32, shape, dim)


def pack_kernel(capacity, owner_ref, slot_ref, hidden_ref, out_ref, pick_ref):
    blocks = owner_ref.shape[0]
    rows, width = hidden_ref.shape
    places = out_ref.shape[0]
    square = (blocks, blocks)
    down, across = iota(square, 0), iota(square, 1)
    owner_down = jnp.broadcast_to(owner_ref[...].astype(jnp.float32), square)
    slot_down = jnp.broadcast_to(slot_ref[...].astype(jnp.float32), square)
    owner_across = jnp.sum(jnp.where(down == across, owner_down, 0.0), axis=0, keepdims=True)
    slot_across = jnp.sum(jnp.where(down == across, slot_down, 0.0), axis=0, keepdims=True)
    same = (owner_down == owner_across) & (across < down)
    rank = jnp.sum(jnp.where(same, 1.0, 0.0), axis=1, keepdims=True)
    target = owner_ref[...].astype(jnp.float32) * capacity + rank
    spread = iota((blocks, rows), 0) == iota((blocks, rows), 1) // BLK
    row_target = jnp.sum(jnp.where(spread, jnp.broadcast_to(target, (blocks, rows)), 0.0), axis=0, keepdims=True)
    row_target = row_target.astype(jnp.int32) * BLK + iota((1, rows), 1) % BLK
    pick = jnp.where(iota((places, rows), 0) == row_target, 1.0, 0.0).astype(jnp.bfloat16)
    pick_ref[...] = pick
    gather = iota((rows, blocks), 1) == iota((rows, blocks), 0) // BLK
    row_slot = jnp.sum(jnp.where(gather, jnp.broadcast_to(slot_across, (rows, blocks)), 0.0), axis=1, keepdims=True)
    flags = jnp.where(iota((rows, LANES), 1) == row_slot.astype(jnp.int32), 1.0, 0.0).astype(jnp.bfloat16)
    out_ref[:, :width] = jnp.dot(pick, hidden_ref[...], preferred_element_type=jnp.float32).astype(jnp.bfloat16)
    out_ref[:, width:] = jnp.dot(pick, flags, preferred_element_type=jnp.float32).astype(jnp.bfloat16)


def pack(block_owner, block_slot, hidden, replicas, capacity):
    rows, width = hidden.shape
    places = replicas * capacity * BLK
    return pl.pallas_call(
        functools.partial(pack_kernel, capacity),
        name="pack_rows",
        out_shape=(
            jax.ShapeDtypeStruct((places, width + LANES), jnp.bfloat16),
            jax.ShapeDtypeStruct((places, rows), jnp.bfloat16),
        ),
        compiler_params=params(24),
        cost_estimate=cost(2 * places * rows * width, 2 * (places + rows) * width),
    )(block_owner, block_slot[:, None], hidden)


def shrink_kernel(rows_ref, shrink_ref, out_ref):
    pool, width, rank = shrink_ref.shape
    rows = rows_ref[:, :width]
    total = jnp.zeros(out_ref.shape, jnp.float32)
    for a in range(pool):
        part = jnp.dot(rows, shrink_ref[a], preferred_element_type=jnp.float32)
        total += part * rows_ref[:, width + a : width + a + 1].astype(jnp.float32)
    out_ref[...] = total.astype(out_ref.dtype)


def shrink(arrived, weights):
    places = arrived.shape[0]
    pool, width, rank = weights.shape
    return pl.pallas_call(
        shrink_kernel,
        name="shrink_rows",
        out_shape=jax.ShapeDtypeStruct((places, rank), jnp.bfloat16),
        compiler_params=params(24),
        cost_estimate=cost(2 * places * width * rank * pool, 2 * (places * width + weights.size)),
    )(arrived, weights)


def expand_kernel(count, *refs):
    parts, flag_ref, up_ref, out_ref = refs[:count], refs[count], refs[count + 1], refs[count + 2]
    pool, halves, rank, width = up_ref.shape
    total = parts[0][...].astype(jnp.float32)
    for part in parts[1:]:
        total += part[...].astype(jnp.float32)
    shrunk = total.astype(jnp.bfloat16)
    for half in range(halves):
        mine = shrunk[:, half * rank : (half + 1) * rank]
        wide = jnp.concatenate([mine * flag_ref[:, a : a + 1] for a in range(pool)], axis=1)
        table = up_ref[:, half].reshape(pool * rank, width)
        product = jnp.dot(wide, table, preferred_element_type=jnp.float32)
        out_ref[:, half * width : (half + 1) * width] = (adapter_scale * product).astype(jnp.bfloat16)


def expand(parts, arrived, up):
    places, rank2 = parts[0].shape
    pool, halves, rank, width = up.shape
    last = arrived.shape[1] // LANES - 1
    return pl.pallas_call(
        functools.partial(expand_kernel, len(parts)),
        name="expand_rows",
        grid=(1,),
        in_specs=[pl.BlockSpec((places, rank2), lambda i: (0, 0))] * len(parts)
        + [
            pl.BlockSpec((places, LANES), lambda i: (0, last)),
            pl.BlockSpec(up.shape, lambda i: (0, 0, 0, 0)),
        ],
        out_specs=pl.BlockSpec((places, halves * width), lambda i: (0, 0)),
        out_shape=jax.ShapeDtypeStruct((places, halves * width), jnp.bfloat16),
        compiler_params=params(16),
        cost_estimate=cost(2 * places * up.size, 2 * up.size + 2 * places * halves * width),
    )(*parts, arrived, up)


def cached_kernel(heads, length_ref, query_ref, key_ref, value_ref, mean_ref, lse_ref, wide_q, wide_o, wide_l):
    step = pl.program_id(0)
    rows, window, width = key_ref.shape
    groups = width // HEAD_SIZE
    each = heads // groups
    inverse_root = HEAD_SIZE ** (-0.5)

    @pl.when(step == 0)
    def _():
        wide_q[...] = jnp.zeros_like(wide_q)

    for h in range(heads):
        wide_q[h // each, pl.ds(h, rows, stride=heads), :] = query_ref[:, h * HEAD_SIZE : (h + 1) * HEAD_SIZE].astype(jnp.float32)
    lane = iota((heads, window), 1)
    for r in range(rows):
        here = pl.ds(r * heads, heads)
        query = jnp.concatenate([wide_q[k, here, :] for k in range(groups)], axis=1).astype(jnp.bfloat16)
        scores = lax.dot_general(query, key_ref[r], (((1,), (1,)), ((), ())), preferred_element_type=jnp.float32)
        scores = jnp.where(lane < length_ref[step * rows + r], scores * inverse_root, masked_score)
        highest = jnp.max(scores, axis=1, keepdims=True)
        terms = jnp.exp(scores - highest)
        total = jnp.sum(terms, axis=1, keepdims=True)
        mixed = jnp.dot(terms.astype(jnp.bfloat16), value_ref[r], preferred_element_type=jnp.float32)
        mixed = jnp.concatenate(
            [mixed[k * each : (k + 1) * each, k * HEAD_SIZE : (k + 1) * HEAD_SIZE] for k in range(groups)], axis=0
        )
        wide_o[here, :] = mixed / total
        wide_l[here, :] = jnp.broadcast_to(highest + jnp.log(total), (heads, LANES))
    place = iota((rows, LANES), 1)
    logs = jnp.zeros((rows, LANES), jnp.float32)
    for h in range(heads):
        mean_ref[:, h * HEAD_SIZE : (h + 1) * HEAD_SIZE] = wide_o[pl.ds(h, rows, stride=heads), :]
        logs = jnp.where(place == h, wide_l[pl.ds(h, rows, stride=heads), :], logs)
    lse_ref[...] = logs


def cached_attention(lengths, queries, keys, values):
    rows, window, width = keys.shape
    wide = queries.shape[1]
    heads = wide // HEAD_SIZE
    group = 16
    row_block = pl.BlockSpec((group, wide), lambda i, n: (i, 0))
    cache_block = pl.BlockSpec((group, window, width), lambda i, n: (i, 0, 0))
    return pl.pallas_call(
        functools.partial(cached_kernel, heads),
        name="cached_attention",
        grid_spec=pltpu.PrefetchScalarGridSpec(
            num_scalar_prefetch=1,
            grid=(rows // group,),
            in_specs=[row_block, cache_block, cache_block],
            out_specs=[row_block, pl.BlockSpec((group, LANES), lambda i, n: (i, 0))],
            scratch_shapes=[
                pltpu.VMEM((width // HEAD_SIZE, group * heads, HEAD_SIZE), jnp.float32),
                pltpu.VMEM((group * heads, HEAD_SIZE), jnp.float32),
                pltpu.VMEM((group * heads, LANES), jnp.float32),
            ],
        ),
        out_shape=(
            jax.ShapeDtypeStruct((rows, wide), jnp.float32),
            jax.ShapeDtypeStruct((rows, LANES), jnp.float32),
        ),
        compiler_params=params(24),
        cost_estimate=cost(4 * rows * heads * window * width, 4 * keys.size + 6 * rows * wide, rows * heads * window),
    )(lengths, queries, keys, values)


def base_kernel(count, index_ref, *refs):
    pieces, key_ref, value_ref, out_ref = refs[:count], refs[count], refs[count + 1], refs[count + 2]
    piece, step = pl.program_id(0), pl.program_id(1)
    depth, width = key_ref.shape

    @pl.when((piece == 0) & (step == 0))
    def _():
        out_ref[...] = jnp.zeros_like(out_ref)

    for p in range(count):

        @pl.when(piece == p)
        def _():
            rows = pieces[p][:, pl.ds(pl.multiple_of(step * depth, depth), depth)]
            out_ref[:, :width] += jnp.dot(rows, key_ref[...], preferred_element_type=jnp.float32)
            out_ref[:, width:] += jnp.dot(rows, value_ref[...], preferred_element_type=jnp.float32)


def base_products(pieces, index, key_matrix, value_matrix):
    rows, shard = pieces[0].shape
    width = key_matrix.shape[1]
    depth = min(1024, shard)
    steps = shard // depth
    weight = pl.BlockSpec((depth, width), lambda p, k, n: (n[p] * steps + k, 0))
    return pl.pallas_call(
        functools.partial(base_kernel, len(pieces)),
        name="base_products",
        grid_spec=pltpu.PrefetchScalarGridSpec(
            num_scalar_prefetch=1,
            grid=(len(pieces), steps),
            in_specs=[pl.BlockSpec((rows, shard), lambda p, k, n: (0, 0))] * len(pieces) + [weight, weight],
            out_specs=pl.BlockSpec((rows, 2 * width), lambda p, k, n: (0, 0)),
        ),
        out_shape=jax.ShapeDtypeStruct((rows, 2 * width), jnp.float32),
        compiler_params=params(24),
        cost_estimate=cost(4 * len(pieces) * rows * shard * width, len(pieces) * (4 * shard * width + 2 * rows * shard)),
    )(index, *pieces, key_matrix, value_matrix)


def finish_kernel(count, info_ref, *refs):
    late = refs[:count]
    key_ref, value_ref, base_ref, back_ref, pick_ref, query_ref, mean_ref, lse_ref = refs[count : count + 8]
    new_key_ref, new_value_ref, context_ref = refs[count + 8 :]
    rows, wide = query_ref.shape
    width = key_ref.shape[1]
    heads = wide // HEAD_SIZE
    each = heads // (width // HEAD_SIZE)
    inverse_root = HEAD_SIZE ** (-0.5)
    piece = late[0][...]
    for other in range(1, count):
        piece = jnp.where(info_ref[1] == other, late[other][...], piece)
    delta = lax.dot_general(pick_ref[...], back_ref[...], (((0,), (0,)), ((), ())), preferred_element_type=jnp.float32)
    base = base_ref[...] + delta
    keys = base[:, :width] + jnp.dot(piece, key_ref[...], preferred_element_type=jnp.float32)
    keys = keys.astype(jnp.bfloat16)
    new_key_ref[...] = keys
    values = base[:, width:] + jnp.dot(piece, value_ref[...], preferred_element_type=jnp.float32)
    values = values.astype(jnp.bfloat16)
    new_value_ref[...] = values
    keys, values = keys.astype(jnp.float32), values.astype(jnp.float32)
    place = iota((rows, LANES), 1)
    own = jnp.zeros((rows, LANES), jnp.float32)
    for h in range(heads):
        k = h // each
        query = query_ref[:, h * HEAD_SIZE : (h + 1) * HEAD_SIZE].astype(jnp.float32)
        score = jnp.sum(query * keys[:, k * HEAD_SIZE : (k + 1) * HEAD_SIZE], axis=1, keepdims=True)
        own = jnp.where(place == h, score * inverse_root, own)
    share = 1.0 / (1.0 + jnp.exp(lse_ref[...] - own))
    for h in range(heads):
        k = h // each
        mean = mean_ref[:, h * HEAD_SIZE : (h + 1) * HEAD_SIZE]
        mixed = mean + share[:, h : h + 1] * (values[:, k * HEAD_SIZE : (k + 1) * HEAD_SIZE] - mean)
        context_ref[:, h * HEAD_SIZE : (h + 1) * HEAD_SIZE] = mixed.astype(jnp.bfloat16)


def finish(late, info, key_matrix, value_matrix, base, back, pick, queries, mean, lse):
    rows, wide = queries.shape
    shard = late[0].shape[1]
    width = key_matrix.shape[1]

    def whole(array):
        return pl.BlockSpec(array.shape, lambda i, n: (0, 0))

    weight = pl.BlockSpec((shard, width), lambda i, n: (n[0], 0))
    rest = [base, back, pick, queries, mean, lse]
    outs = (
        jax.ShapeDtypeStruct((rows, width), jnp.bfloat16),
        jax.ShapeDtypeStruct((rows, width), jnp.bfloat16),
        jax.ShapeDtypeStruct((rows, wide), jnp.bfloat16),
    )
    return pl.pallas_call(
        functools.partial(finish_kernel, len(late)),
        name="finish_rows",
        grid_spec=pltpu.PrefetchScalarGridSpec(
            num_scalar_prefetch=1,
            grid=(1,),
            in_specs=[whole(a) for a in late] + [weight, weight] + [whole(a) for a in rest],
            out_specs=[whole(a) for a in outs],
        ),
        out_shape=outs,
        compiler_params=params(32),
        cost_estimate=cost(4 * rows * shard * width, 4 * shard * width + 10 * rows * wide),
    )(info, *late, key_matrix, value_matrix, *rest)


def swap(x, mask, size):
    return lax.ppermute(x, "tp", [(i, i ^ mask) for i in range(size)])


def turn(x, shift, size):
    return lax.ppermute(x, "tp", [(i, (i + shift) % size) for i in range(size)])


def others(x, size):
    return [turn(x, shift, size) for shift in range(1, size)]


def shards(
    hidden_in,
    queries,
    cache_keys,
    cached_value_rows,
    cache_lengths,
    base_key_matrix,
    base_value_matrix,
    shrink_weights,
    pooled_up_weights,
    block_owner,
    block_slot,
):
    rows_here, shard_width = hidden_in.shape
    replicas = lax.axis_size("rep")
    parts = lax.axis_size("tp")
    place = lax.axis_index("tp")
    blocks_here = rows_here // BLK
    capacity = max(2, (2 * blocks_here + replicas - 1) // replicas)
    width = base_key_matrix.shape[1]

    def all_to_all(x):
        kept = x.shape
        x = x.reshape(replicas, kept[0] // replicas, kept[1])
        return lax.all_to_all(x, "rep", split_axis=0, concat_axis=0, tiled=True).reshape(kept)

    outgoing, pick = pack(block_owner, block_slot, hidden_in, replicas, capacity)
    arrived = all_to_all(outgoing)

    if parts == 4:
        two = swap(hidden_in, 2, parts)
        one = swap(hidden_in, 1, parts)
        inner = lax.ppermute(hidden_in, "tp", [(1, 2), (2, 1)])
        outer = lax.ppermute(two, "tp", [(1, 0), (2, 3)])
        early, late = [hidden_in, one, two], [inner, outer]
        index = jnp.stack([place, place ^ 1, place ^ 2]).astype(jnp.int32)
        is_outer = ((place == 0) | (place == parts - 1)).astype(jnp.int32)
        info = jnp.stack([place ^ 3, is_outer]).astype(jnp.int32)
    else:
        pieces = [hidden_in] + others(hidden_in, parts)
        early, late = pieces[:-1], pieces[-1:]
        index = ((place + parts - jnp.arange(parts - 1, dtype=jnp.int32)) % parts).astype(jnp.int32)
        info = jnp.stack([(place + 1) % parts, place * 0]).astype(jnp.int32)

    mean, lse = cached_attention(cache_lengths, queries, cache_keys, cached_value_rows)
    partial_rows = shrink(arrived, shrink_weights)
    if parts == 4:
        sums = [partial_rows] + [swap(partial_rows, mask, parts) for mask in (1, 2, 3)]
    else:
        sums = [partial_rows] + others(partial_rows, parts)
    back = all_to_all(expand(sums, arrived, pooled_up_weights))
    base = base_products(early, index, base_key_matrix, base_value_matrix)
    return finish(late, info, base_key_matrix, base_value_matrix, base, back, pick, queries, mean, lse)


def solution(mesh):
    return jax.shard_map(
        shards,
        mesh=mesh,
        in_specs=(
            P("rep", "tp"),
            P("rep", "tp"),
            P("rep", None, "tp"),
            P("rep", None, "tp"),
            P("rep"),
            P(None, "tp"),
            P(None, "tp"),
            P("rep", "tp", None),
            P("rep", None, None, "tp"),
            P("rep", None),
            P("rep"),
        ),
        out_specs=(P("rep", "tp"), P("rep", "tp"), P("rep", "tp")),
        check_vma=False,
    )
```

time: 125 us -> 104 us (0.83)
  blocking collectives: 35 us -> 0 us
  matrix products: 33.8 us -> 0 us
  Pallas kernels: 0 us -> 32.5 us
  waiting for transfers between devices: 0.69 us -> 24.7 us
  starting transfers between devices: 8.78 us -> 23.3 us
  between operations: 14.9 us -> 0.77 us
  local copies, waits for them, and re-layouts: 26.3 us -> 21.3 us
  other arithmetic: 4.25 us -> 0.15 us
    dot_general x9 -> x0, matrix products: 33.8 us -> none  [the longest x1 10.4 us: adapter_pass(): jnp.einsum('snd,sdr->snr', slot_rows, chosen_shrink, preferred_element_ty...]
    pallas_call x0 -> x6, Pallas kernels: none -> 32.5 us  [the longest x1 23.8 us: cached_attention(): pl.pallas_call(functools.partial(cached_kernel, heads), name='cached_atte...]
    ppermute x0 -> x7, waiting for transfers between devices: none -> 24.7 us  [the longest x5 24.7 us: swap(): return lax.ppermute(x, 'tp', [(i, i ^ mask) for i in range(size)])]
    psum x1 -> x0, blocking collectives: 20.4 us -> none  [sum_sent(): return lax.psum(partial_value, 'tp')]
    unnamed x20 -> x33, local copies, waits for them, and re-layouts: 3.45 us -> 20.5 us
    unnamed x1 -> x0, blocking collectives: 14.6 us -> none
    ppermute x0 -> x7, starting transfers between devices: none -> 14.4 us  [the longest x5 12.4 us: swap(): return lax.ppermute(x, 'tp', [(i, i ^ mask) for i in range(size)])]
    gather x2 -> x0, local copies, waits for them, and re-layouts: 12.2 us -> none  [the longest x1 9.59 us: adapter_pass(): chosen_shrink = jnp.take(shrink_weights, slot_index, axis=0)]
  transfers between devices with their start and end apart: 3 -> 9, of which waited for: 0 -> 3; matrix products, arithmetic and copies ran while one was open for 39% -> 0% of each run, Pallas kernels for 0% -> 28%
where the time goes in v1:
time: 104 us; the launch traced here: 103 us
  Pallas kernels  32.5 us (31%)
  waiting for transfers between devices  24.7 us (24%)
  starting transfers between devices  23.3 us (22%)
  local copies, waits for them, and re-layouts  21.3 us (20%)
    ppermute x5, waiting for transfers between devices, swap(): return lax.ppermute(x, 'tp', [(i, i ^ mask) for i in range(size)])  24.7 us
    pallas_call x1, Pallas kernels, cached_attention(): pl.pallas_call(functools.partial(cached_kernel, heads), name='cached_atte...  23.8 us
    unnamed x33, local copies, waits for them, and re-layouts  20.5 us
    ppermute x5, starting transfers between devices, swap(): return lax.ppermute(x, 'tp', [(i, i ^ mask) for i in range(size)])  12.4 us
    all_to_all x2, starting transfers between devices, all_to_all(): lax.all_to_all(x, 'rep', split_axis=0, concat_axis=0, tiled=True)  8.95 us
    pallas_call x1, Pallas kernels, base_products(): pl.pallas_call(functools.partial(base_kernel, len(pieces)), name='base_pr...  2.53 us
    pallas_call x1, Pallas kernels, finish(): pl.pallas_call(functools.partial(finish_kernel, len(late)), name='finish_...  2.38 us
  transfers between devices with their start and end apart: 9, of which 3 were waited for; matrix products, arithmetic and copies ran while one was open for 0% of the time, Pallas kernels for 28%

profile of v1, /device:TPU:0, one launch (start us, length us, event | category | flops | bytes accessed | tf_op | source)
XLA Modules:
  0.0 102.7 jit_solution(9091598636362036383)
XLA Ops:
  0.6 0.0 copy-start.7
  0.6 0.8 copy.14.owner_ref
  1.4 0.7 copy.15.slot_ref
  2.2 1.0 copy-done.8
  3.2 1.5 %pack_rows.1 = (bf16[192,2176]{1,0:T(8,128)(2,1)}, bf16[192,96]{1,0:T(8,128)(2,1)S(1)}) custom-call(s32[24,1]{1,0:T(8,128)S(1)} %copy.14.owner_ref, s32[24,1]{1,0:T(8,128)S(1)} %copy.15.slot_ref, bf16[96,2048]{1,0:T(8,128)(2,1)S(1)} %copy-done.8), custom_call_target="tpu_custom_call" | custom-call | flops 75497472 | bytes 1179648 | tf_op jit(solution)/shard_map/pack_rows/pallas_call | solution.py:59
  4.7 0.6 copy-done.11
  5.3 5.2 %all-to-all-start = ((bf16[8,24,2176]{2,1,0:T(8,128)(2,1)}), bf16[8,24,2176]{2,1,0:T(8,128)(2,1)S(1)}, u32[]{:S(2)}, u32[]{:S(2)}) async-start(bf16[8,24,2176]{2,1,0:T(8,128)(2,1)} %bitcast.6), calls=%async_computation | async-start | bytes 1671168 | tf_op jit(solution)/shard_map/all_to_all | solution.py:335
  10.5 2.6 %collective-permute-start.1 = (bf16[96,2048]{1,0:T(8,128)(2,1)}, bf16[96,2048]{1,0:T(8,128)(2,1)S(1)}, u32[]{:S(2)}, u32[]{:S(2)}) collective-permute-start(bf16[96,2048]{1,0:T(8,128)(2,1)} %hidden_ref.1), channel_id=1, source_target_pairs={{0,2},{1,3},{2,0},{3,1},{4,6},{5,7},{6,4},{7,5},{8,10},{9,11},{10,... | collective-permute-start | bytes 1179656 | tf_op jit(solution)/shard_map/ppermute | solution.py:300
  13.1 1.6 %collective-permute-start.3 = (bf16[96,2048]{1,0:T(8,128)(2,1)}, bf16[96,2048]{1,0:T(8,128)(2,1)S(1)}, u32[]{:S(2)}, u32[]{:S(2)}) collective-permute-start(bf16[96,2048]{1,0:T(8,128)(2,1)} %hidden_ref.1), channel_id=1, source_target_pairs={{0,1},{1,0},{2,3},{3,2},{4,5},{5,4},{6,7},{7,6},{8,9},{9,8},{10,11... | collective-permute-start | bytes 1179656 | tf_op jit(solution)/shard_map/ppermute | solution.py:300
  14.6 0.7 collective-permute-start
  15.3 16.6 %collective-permute-done.1.refs_2_ = bf16[96,2048]{1,0:T(8,128)(2,1)S(1)} collective-permute-done((bf16[96,2048]{1,0:T(8,128)(2,1)}, bf16[96,2048]{1,0:T(8,128)(2,1)S(1)}, u32[]{:S(2)}, u32[]{:S(2)}) %collective-permute-start.1) | collective-permute-done | bytes 393248 | tf_op jit(solution)/shard_map/ppermute | solution.py:300
  32.0 1.3 %collective-permute-start.2 = (bf16[96,2048]{1,0:T(8,128)(2,1)S(1)}, bf16[96,2048]{1,0:T(8,128)(2,1)S(1)}, u32[]{:S(2)}, u32[]{:S(2)}) collective-permute-start(bf16[96,2048]{1,0:T(8,128)(2,1)S(1)} %collective-permute-done.1.refs_2_), channel_id=1, source_target_pairs={{1,0},{2,3},{5,4},{6,7},{9,8},{10,11},{13,12},{14,15},{17,16},{18,... | collective-permute-start | bytes 1179656 | tf_op jit(solution)/shard_map/ppermute | solution.py:344
  33.2 0.0 all-to-all-done
  33.3 0.0 copy-start.6
  33.3 1.6 %copy-done.6 = bf16[4,2048,128]{2,1,0:T(8,128)(2,1)S(1)} copy-done((bf16[4,2048,128]{2,1,0:T(8,128)(2,1)S(1)}, bf16[4,2048,128]{2,1,0:T(8,128)(2,1)}, u32[]{:S(2)}) %copy-start.6) | copy-done | bytes 2097176
  34.9 1.0 shrink_rows.1.refs_0_
  35.8 2.7 %collective-permute-start.4 = (bf16[192,128]{1,0:T(8,128)(2,1)S(1)}, bf16[192,128]{1,0:T(8,128)(2,1)S(1)}, u32[]{:S(2)}, u32[]{:S(2)}) collective-permute-start(bf16[192,128]{1,0:T(8,128)(2,1)S(1)} %shrink_rows.1.refs_0_), channel_id=1, source_target_pairs={{0,1},{1,0},{2,3},{3,2},{4,5},{5,4},{6,7},{7,6},{8,9},{9,8},{10,11... | collective-permute-start | bytes 147464 | tf_op jit(solution)/shard_map/ppermute | solution.py:300
  38.6 1.7 %collective-permute-start.5 = (bf16[192,128]{1,0:T(8,128)(2,1)S(1)}, bf16[192,128]{1,0:T(8,128)(2,1)S(1)}, u32[]{:S(2)}, u32[]{:S(2)}) collective-permute-start(bf16[192,128]{1,0:T(8,128)(2,1)S(1)} %shrink_rows.1.refs_0_), channel_id=1, source_target_pairs={{0,2},{1,3},{2,0},{3,1},{4,6},{5,7},{6,4},{7,5},{8,10},{9,11},{10,... | collective-permute-start | bytes 147464 | tf_op jit(solution)/shard_map/ppermute | solution.py:300
  40.3 6.0 %collective-permute-done.4.refs_1_ = bf16[192,128]{1,0:T(8,128)(2,1)S(1)} collective-permute-done((bf16[192,128]{1,0:T(8,128)(2,1)S(1)}, bf16[192,128]{1,0:T(8,128)(2,1)S(1)}, u32[]{:S(2)}, u32[]{:S(2)}) %collective-permute-start.4) | collective-permute-done | bytes 49184 | tf_op jit(solution)/shard_map/ppermute | solution.py:300
  46.3 3.8 %collective-permute-start.6 = (bf16[192,128]{1,0:T(8,128)(2,1)S(1)}, bf16[192,128]{1,0:T(8,128)(2,1)S(1)}, u32[]{:S(2)}, u32[]{:S(2)}) collective-permute-start(bf16[192,128]{1,0:T(8,128)(2,1)S(1)} %shrink_rows.1.refs_0_), channel_id=1, source_target_pairs={{0,3},{1,2},{2,1},{3,0},{4,7},{5,6},{6,5},{7,4},{8,11},{9,10},{10,... | collective-permute-start | bytes 147464 | tf_op jit(solution)/shard_map/ppermute | solution.py:300
  50.1 0.1 pad_add_fusion.info_ref
  50.2 0.0 collective-permute-done.5.refs_2_
  50.2 2.0 %collective-permute-done.6.refs_3_ = bf16[192,128]{1,0:T(8,128)(2,1)S(1)} collective-permute-done((bf16[192,128]{1,0:T(8,128)(2,1)S(1)}, bf16[192,128]{1,0:T(8,128)(2,1)S(1)}, u32[]{:S(2)}, u32[]{:S(2)}) %collective-permute-start.6) | collective-permute-done | bytes 49184 | tf_op jit(solution)/shard_map/ppermute | solution.py:300
  52.2 0.0 copy-done.10
  52.2 1.3 %expand_rows.1 = bf16[192,512]{1,0:T(8,128)(2,1)} custom-call(bf16[192,128]{1,0:T(8,128)(2,1)S(1)} %shrink_rows.1.refs_0_, bf16[192,128]{1,0:T(8,128)(2,1)S(1)} %collective-permute-done.4.refs_1_, bf16[192,128]{1,0:T(8,128)(2,1)S(1)} %collective-permute-done.5.refs_2_, bf16[192,128]{1,0:T(8,128)(2,1)S(1)} %collective-permute-done.6.refs_3_, ...), custom_call_target="tpu_custom_call" | custom-call | flops 50331648 | bytes 458752 | tf_op jit(solution)/shard_map/expand_rows/pallas_call | solution.py:112
  53.5 3.8 %all-to-all-start.1 = ((bf16[8,24,512]{2,1,0:T(8,128)(2,1)}), bf16[8,24,512]{2,1,0:T(8,128)(2,1)S(1)}, u32[]{:S(2)}, u32[]{:S(2)}) async-start(bf16[8,24,512]{2,1,0:T(8,128)(2,1)} %bitcast.8), calls=%async_computation.1 | async-start | bytes 393216 | tf_op jit(solution)/shard_map/all_to_all | solution.py:335
  57.3 0.0 copy-done.7
  57.3 0.0 copy-done.15
  57.3 0.0 copy-start.4
  57.3 2.8 %copy-done.4 = bf16[96,128,256]{2,1,0:T(8,128)(2,1)S(1)} copy-done((bf16[96,128,256]{2,1,0:T(8,128)(2,1)S(1)}, bf16[96,128,256]{2,1,0:T(8,128)(2,1)}, u32[]{:S(2)}) %copy-start.4) | copy-done | bytes 6291480
  60.1 2.8 %copy-done.5 = bf16[96,128,256]{2,1,0:T(8,128)(2,1)S(1)} copy-done((bf16[96,128,256]{2,1,0:T(8,128)(2,1)S(1)}, bf16[96,128,256]{2,1,0:T(8,128)(2,1)}, u32[]{:S(2)}) %copy-start.5) | copy-done | bytes 6291480
  62.9 23.8 %cached_attention.1 = (f32[96,2048]{1,0:T(8,128)S(1)}, f32[96,128]{1,0:T(8,128)S(1)}) custom-call(s32[96]{0:T(128)S(1)} %copy-done.15, bf16[96,2048]{1,0:T(8,128)(2,1)S(1)} %copy-done.7, bf16[96,128,256]{2,1,0:T(8,128)(2,1)S(1)} %copy-done.4, bf16[96,128,256]{2,1,0:T(8,128)(2,1)S(1)} %copy-done.5), custom_call_target="tpu_custom_call" | custom-call | flops 201326592 | bytes 13762560 | tf_op jit(solution)/shard_map/cached_attention/pallas_call | solution.py:171
  86.7 0.0 copy-start.13
  86.7 0.6 copy-done.13
  87.3 0.1 pad_add_fusion.1.index_ref
  87.4 0.0 collective-permute-done.3.refs_1_
  87.4 2.2 %copy-done = bf16[8192,256]{1,0:T(8,128)(2,1)S(1)} copy-done((bf16[8192,256]{1,0:T(8,128)(2,1)S(1)}, bf16[8192,256]{1,0:T(8,128)(2,1)}, u32[]{:S(2)}) %copy-start) | copy-done | bytes 4194328
  89.6 2.2 %copy-done.2 = bf16[8192,256]{1,0:T(8,128)(2,1)S(1)} copy-done((bf16[8192,256]{1,0:T(8,128)(2,1)S(1)}, bf16[8192,256]{1,0:T(8,128)(2,1)}, u32[]{:S(2)}) %copy-start.2) | copy-done | bytes 4194328
  91.8 2.5 %base_products.1.refs_4_ = f32[96,512]{1,0:T(8,128)S(1)} custom-call(s32[3]{0:T(128)S(1)} %pad_add_fusion.1.index_ref, bf16[96,2048]{1,0:T(8,128)(2,1)S(1)} %copy-done.9, bf16[96,2048]{1,0:T(8,128)(2,1)S(1)} %collective-permute-done.3.refs_1_, bf16[96,2048]{1,0:T(8,128)(2,1)S(1)} %collective-permute-done.1.refs_2_, bf16[8192,256]{1,0:T(8,128)(2,1)S(1)} %copy-done, ...), custom_call_target="tpu_custom_call" | custom-call | flops 603979776 | bytes 7471104 | tf_op jit(solution)/shard_map/base_products/pallas_call | solution.py:218
  94.3 0.0 collective-permute-done.refs_0_
  94.3 0.0 collective-permute-done.2.refs_1_
  94.3 0.0 all-to-all-done.1
  94.4 0.0 copy-start.1
  94.4 2.2 %copy-done.1 = bf16[8192,256]{1,0:T(8,128)(2,1)S(1)} copy-done((bf16[8192,256]{1,0:T(8,128)(2,1)S(1)}, bf16[8192,256]{1,0:T(8,128)(2,1)}, u32[]{:S(2)}) %copy-start.1) | copy-done | bytes 4194328
  96.5 2.2 %copy-done.3 = bf16[8192,256]{1,0:T(8,128)(2,1)S(1)} copy-done((bf16[8192,256]{1,0:T(8,128)(2,1)S(1)}, bf16[8192,256]{1,0:T(8,128)(2,1)}, u32[]{:S(2)}) %copy-start.3) | copy-done | bytes 4194328
  98.7 0.8 copy-done.12
  99.5 0.8 copy-done.14
  100.3 2.4 %finish_rows.1 = (bf16[96,256]{1,0:T(8,128)(2,1)}, bf16[96,256]{1,0:T(8,128)(2,1)}, bf16[96,2048]{1,0:T(8,128)(2,1)}) custom-call(s32[2]{0:T(128)S(1)} %pad_add_fusion.info_ref, bf16[96,2048]{1,0:T(8,128)(2,1)S(1)} %collective-permute-done.refs_0_, bf16[96,2048]{1,0:T(8,128)(2,1)S(1)} %collective-permute-done.2.refs_1_, bf16[8192,256]{1,0:T(8,128)(2,1)S(1)} %copy-done.1, ...), custom_call_target="tpu_custom_call" | custom-call | flops 201326592 | bytes 4063232 | tf_op jit(solution)/shard_map/finish_rows/pallas_call | solution.py:284
  (12 shorter events, 0.0 us)
Async XLA Ops:
  0.6 56.6 %copy-start.7 = (bf16[96,2048]{1,0:T(8,128)(2,1)S(1)}, bf16[96,2048]{1,0:T(8,128)(2,1)}, u32[]{:S(2)}) copy-start(bf16[96,2048]{1,0:T(8,128)(2,1)} %refs_7_.1) | copy-start | bytes 1179652
  2.2 1.0 copy-start.8
  3.2 49.0 %copy-start.10 = (bf16[4,2,64,256]{3,2,1,0:T(8,128)(2,1)S(1)}, bf16[4,2,64,256]{3,2,1,0:T(8,128)(2,1)}, u32[]{:S(2)}) copy-start(bf16[4,2,64,256]{3,2,1,0:T(8,128)(2,1)} %refs_5_.1) | copy-start | bytes 786436
  3.2 54.1 %copy-start.15 = (s32[96]{0:T(128)S(1)}, s32[96]{0:T(128)}, u32[]{:S(2)}) copy-start(s32[96]{0:T(128)} %length_ref.1) | copy-start | bytes 1156
  4.7 0.6 copy-start.11
  5.3 28.0 %all-to-all-start = ((bf16[8,24,2176]{2,1,0:T(8,128)(2,1)}), bf16[8,24,2176]{2,1,0:T(8,128)(2,1)S(1)}, u32[]{:S(2)}, u32[]{:S(2)}) async-start(bf16[8,24,2176]{2,1,0:T(8,128)(2,1)} %bitcast.6), calls=%async_computation | async-start | bytes 1671168 | tf_op jit(solution)/shard_map/all_to_all | solution.py:335
  10.5 21.5 %collective-permute-start.1 = (bf16[96,2048]{1,0:T(8,128)(2,1)}, bf16[96,2048]{1,0:T(8,128)(2,1)S(1)}, u32[]{:S(2)}, u32[]{:S(2)}) collective-permute-start(bf16[96,2048]{1,0:T(8,128)(2,1)} %hidden_ref.1), channel_id=1, source_target_pairs={{0,2},{1,3},{2,0},{3,1},{4,6},{5,7},{6,4},{7,5},{8,10},{9,11},{10,... | collective-permute-start | bytes 1179656 | tf_op jit(solution)/shard_map/ppermute | solution.py:300
  13.1 74.3 %collective-permute-start.3 = (bf16[96,2048]{1,0:T(8,128)(2,1)}, bf16[96,2048]{1,0:T(8,128)(2,1)S(1)}, u32[]{:S(2)}, u32[]{:S(2)}) collective-permute-start(bf16[96,2048]{1,0:T(8,128)(2,1)} %hidden_ref.1), channel_id=1, source_target_pairs={{0,1},{1,0},{2,3},{3,2},{4,5},{5,4},{6,7},{7,6},{8,9},{9,8},{10,11... | collective-permute-start | bytes 1179656 | tf_op jit(solution)/shard_map/ppermute | solution.py:300
  14.6 79.7 %collective-permute-start = (bf16[96,2048]{1,0:T(8,128)(2,1)}, bf16[96,2048]{1,0:T(8,128)(2,1)S(1)}, u32[]{:S(2)}, u32[]{:S(2)}) collective-permute-start(bf16[96,2048]{1,0:T(8,128)(2,1)} %hidden_ref.1), channel_id=1, source_target_pairs={{1,2},{2,1},{5,6},{6,5},{9,10},{10,9},{13,14},{14,13},{17,18},{18,... | collective-permute-start | bytes 1179656 | tf_op jit(solution)/shard_map/ppermute | solution.py:343
  32.0 62.4 %collective-permute-start.2 = (bf16[96,2048]{1,0:T(8,128)(2,1)S(1)}, bf16[96,2048]{1,0:T(8,128)(2,1)S(1)}, u32[]{:S(2)}, u32[]{:S(2)}) collective-permute-start(bf16[96,2048]{1,0:T(8,128)(2,1)S(1)} %collective-permute-done.1.refs_2_), channel_id=1, source_target_pairs={{1,0},{2,3},{5,4},{6,7},{9,8},{10,11},{13,12},{14,15},{17,16},{18,... | collective-permute-start | bytes 1179656 | tf_op jit(solution)/shard_map/ppermute | solution.py:344
  33.3 1.6 %copy-start.6 = (bf16[4,2048,128]{2,1,0:T(8,128)(2,1)S(1)}, bf16[4,2048,128]{2,1,0:T(8,128)(2,1)}, u32[]{:S(2)}) copy-start(bf16[4,2048,128]{2,1,0:T(8,128)(2,1)} %shrink_ref.1) | copy-start | bytes 6291460
  35.8 10.5 %collective-permute-start.4 = (bf16[192,128]{1,0:T(8,128)(2,1)S(1)}, bf16[192,128]{1,0:T(8,128)(2,1)S(1)}, u32[]{:S(2)}, u32[]{:S(2)}) collective-permute-start(bf16[192,128]{1,0:T(8,128)(2,1)S(1)} %shrink_rows.1.refs_0_), channel_id=1, source_target_pairs={{0,1},{1,0},{2,3},{3,2},{4,5},{5,4},{6,7},{7,6},{8,9},{9,8},{10,11... | collective-permute-start | bytes 147464 | tf_op jit(solution)/shard_map/ppermute | solution.py:300
  38.6 11.6 %collective-permute-start.5 = (bf16[192,128]{1,0:T(8,128)(2,1)S(1)}, bf16[192,128]{1,0:T(8,128)(2,1)S(1)}, u32[]{:S(2)}, u32[]{:S(2)}) collective-permute-start(bf16[192,128]{1,0:T(8,128)(2,1)S(1)} %shrink_rows.1.refs_0_), channel_id=1, source_target_pairs={{0,2},{1,3},{2,0},{3,1},{4,6},{5,7},{6,4},{7,5},{8,10},{9,11},{10,... | collective-permute-start | bytes 147464 | tf_op jit(solution)/shard_map/ppermute | solution.py:300
  46.3 5.9 %collective-permute-start.6 = (bf16[192,128]{1,0:T(8,128)(2,1)S(1)}, bf16[192,128]{1,0:T(8,128)(2,1)S(1)}, u32[]{:S(2)}, u32[]{:S(2)}) collective-permute-start(bf16[192,128]{1,0:T(8,128)(2,1)S(1)} %shrink_rows.1.refs_0_), channel_id=1, source_target_pairs={{0,3},{1,2},{2,1},{3,0},{4,7},{5,6},{6,5},{7,4},{8,11},{9,10},{10,... | collective-permute-start | bytes 147464 | tf_op jit(solution)/shard_map/ppermute | solution.py:300
  53.5 40.9 %all-to-all-start.1 = ((bf16[8,24,512]{2,1,0:T(8,128)(2,1)}), bf16[8,24,512]{2,1,0:T(8,128)(2,1)S(1)}, u32[]{:S(2)}, u32[]{:S(2)}) async-start(bf16[8,24,512]{2,1,0:T(8,128)(2,1)} %bitcast.8), calls=%async_computation.1 | async-start | bytes 393216 | tf_op jit(solution)/shard_map/all_to_all | solution.py:335
  57.3 2.8 %copy-start.4 = (bf16[96,128,256]{2,1,0:T(8,128)(2,1)S(1)}, bf16[96,128,256]{2,1,0:T(8,128)(2,1)}, u32[]{:S(2)}) copy-start(bf16[96,128,256]{2,1,0:T(8,128)(2,1)} %key_ref.1) | copy-start | bytes 18874372
  60.1 2.8 %copy-start.5 = (bf16[96,128,256]{2,1,0:T(8,128)(2,1)S(1)}, bf16[96,128,256]{2,1,0:T(8,128)(2,1)}, u32[]{:S(2)}) copy-start(bf16[96,128,256]{2,1,0:T(8,128)(2,1)} %value_ref.1) | copy-start | bytes 18874372
  62.9 24.5 %copy-start.9 = (bf16[96,2048]{1,0:T(8,128)(2,1)S(1)}, bf16[96,2048]{1,0:T(8,128)(2,1)}, u32[]{:S(2)}) copy-start(bf16[96,2048]{1,0:T(8,128)(2,1)} %hidden_ref.1) | copy-start | bytes 1179652
  86.7 0.6 copy-start.13
  87.4 2.2 %copy-start = (bf16[8192,256]{1,0:T(8,128)(2,1)S(1)}, bf16[8192,256]{1,0:T(8,128)(2,1)}, u32[]{:S(2)}) copy-start(bf16[8192,256]{1,0:T(8,128)(2,1)} %refs_2_.1) | copy-start | bytes 12582916
  89.6 2.2 %copy-start.2 = (bf16[8192,256]{1,0:T(8,128)(2,1)S(1)}, bf16[8192,256]{1,0:T(8,128)(2,1)}, u32[]{:S(2)}) copy-start(bf16[8192,256]{1,0:T(8,128)(2,1)} %refs_3_.3) | copy-start | bytes 12582916
  94.4 2.2 %copy-start.1 = (bf16[8192,256]{1,0:T(8,128)(2,1)S(1)}, bf16[8192,256]{1,0:T(8,128)(2,1)}, u32[]{:S(2)}) copy-start(bf16[8192,256]{1,0:T(8,128)(2,1)} %refs_2_.1) | copy-start | bytes 12582916
  96.5 2.2 %copy-start.3 = (bf16[8192,256]{1,0:T(8,128)(2,1)S(1)}, bf16[8192,256]{1,0:T(8,128)(2,1)}, u32[]{:S(2)}) copy-start(bf16[8192,256]{1,0:T(8,128)(2,1)} %refs_3_.3) | copy-start | bytes 12582916
  98.7 0.8 copy-start.12
  99.5 0.8 copy-start.14

commit v2 on v1

v2 whole, which is shorter than its diff:
```python
import functools

import jax
import jax.numpy as jnp
from jax import lax
from jax.experimental import pallas as pl
from jax.experimental.pallas import tpu as pltpu
from jax.sharding import PartitionSpec as P

HEAD_SIZE = 128
BLK = 4
LANES = 128
MIB = 1 << 20

adapter_scale = 0.5
masked_score = -1e30


def params(mib):
    return pltpu.CompilerParams(vmem_limit_bytes=mib * MIB)


def cost(flops, moved, exps=0):
    return pl.CostEstimate(flops=flops, bytes_accessed=moved, transcendentals=exps)


def pinned(x):
    return pltpu.with_memory_space_constraint(x, pltpu.HBM)


def iota(shape, dim):
    return lax.broadcasted_iota(jnp.int32, shape, dim)


def pack_kernel(capacity, owner_ref, slot_ref, hidden_ref, out_ref, pick_ref):
    blocks = owner_ref.shape[0]
    rows, width = hidden_ref.shape
    places = out_ref.shape[0]
    square = (blocks, blocks)
    down, across = iota(square, 0), iota(square, 1)
    owner_across = jnp.zeros((1, blocks), jnp.int32)
    owner_down = jnp.zeros((blocks, 1), jnp.int32)
    row_slot = jnp.zeros((rows, 1), jnp.int32)
    for b in range(blocks):
        owner_across = jnp.where(iota((1, blocks), 1) == b, owner_ref[b], owner_across)
        owner_down = jnp.where(iota((blocks, 1), 0) == b, owner_ref[b], owner_down)
        row_slot = jnp.where(iota((rows, 1), 0) // BLK == b, slot_ref[b], row_slot)
    same = (owner_down == owner_across) & (across < down)
    rank = jnp.sum(jnp.where(same, 1.0, 0.0), axis=1, keepdims=True)
    target = owner_down.astype(jnp.float32) * capacity + rank
    spread = iota((blocks, rows), 0) == iota((blocks, rows), 1) // BLK
    row_target = jnp.sum(jnp.where(spread, jnp.broadcast_to(target, (blocks, rows)), 0.0), axis=0, keepdims=True)
    row_target = row_target.astype(jnp.int32) * BLK + iota((1, rows), 1) % BLK
    pick = jnp.where(iota((places, rows), 0) == row_target, 1.0, 0.0).astype(jnp.bfloat16)
    pick_ref[...] = pick
    flags = jnp.where(iota((rows, LANES), 1) == row_slot, 1.0, 0.0).astype(jnp.bfloat16)
    out_ref[:, :width] = jnp.dot(pick, hidden_ref[...], preferred_element_type=jnp.float32).astype(jnp.bfloat16)
    out_ref[:, width:] = jnp.dot(pick, flags, preferred_element_type=jnp.float32).astype(jnp.bfloat16)


def pack(block_owner, block_slot, hidden, replicas, capacity):
    rows, width = hidden.shape
    places = replicas * capacity * BLK
    scalars = pl.BlockSpec(memory_space=pltpu.SMEM)
    return pl.pallas_call(
        functools.partial(pack_kernel, capacity),
        name="pack_rows",
        in_specs=[scalars, scalars, pl.BlockSpec(memory_space=pltpu.VMEM)],
        out_shape=(
            jax.ShapeDtypeStruct((places, width + LANES), jnp.bfloat16),
            jax.ShapeDtypeStruct((places, rows), jnp.bfloat16),
        ),
        compiler_params=params(61),
        cost_estimate=cost(2 * places * rows * width, 2 * (places + rows) * width),
    )(block_owner[:, 0], block_slot, hidden)


def shrink_kernel(rows_ref, shrink_ref, up_hbm, out_ref, flag_ref, up_ref, sem):
    pool, width, rank = shrink_ref.shape
    copy = pltpu.make_async_copy(up_hbm, up_ref, sem)
    copy.start()
    rows = rows_ref[:, :width]
    flag_ref[...] = rows_ref[:, width:]
    total = jnp.zeros(out_ref.shape, jnp.float32)
    for a in range(pool):
        part = jnp.dot(rows, shrink_ref[a], preferred_element_type=jnp.float32)
        total += part * rows_ref[:, width + a : width + a + 1].astype(jnp.float32)
    out_ref[...] = total
    copy.wait()


def shrink(arrived, weights, up):
    places = arrived.shape[0]
    pool, width, rank = weights.shape
    inside, outside = pl.BlockSpec(memory_space=pltpu.VMEM), pl.BlockSpec(memory_space=pltpu.HBM)
    return pl.pallas_call(
        shrink_kernel,
        name="shrink_rows",
        in_specs=[inside, inside, outside],
        out_specs=[inside] * 3,
        out_shape=(
            jax.ShapeDtypeStruct((places, rank), jnp.float32),
            jax.ShapeDtypeStruct((places, LANES), jnp.bfloat16),
            jax.ShapeDtypeStruct(up.shape, up.dtype),
        ),
        scratch_shapes=[pltpu.SemaphoreType.DMA],
        compiler_params=params(8),
        cost_estimate=cost(2 * places * width * rank * pool, 2 * (places * width + weights.size)),
    )(arrived, weights, pinned(up))


def expand_kernel(count, *refs):
    parts, flag_ref, up_ref, out_ref = refs[:count], refs[count], refs[count + 1], refs[count + 2]
    pool, halves, rank, width = up_ref.shape
    total = parts[0][...].astype(jnp.float32)
    for part in parts[1:]:
        total += part[...].astype(jnp.float32)
    shrunk = total.astype(jnp.bfloat16)
    mine = [shrunk * flag_ref[:, a : a + 1] for a in range(pool)]
    table = up_ref[...].reshape(pool * halves * rank, width)
    side = iota(shrunk.shape, 1) // rank
    for half in range(halves):
        wide = jnp.concatenate([jnp.where(side == half, x, jnp.zeros_like(x)) for x in mine], axis=1)
        product = jnp.dot(wide, table, preferred_element_type=jnp.float32)
        out_ref[:, half * width : (half + 1) * width] = (adapter_scale * product).astype(jnp.bfloat16)


def expand(parts, flags, up):
    places = parts[0].shape[0]
    pool, halves, rank, width = up.shape
    return pl.pallas_call(
        functools.partial(expand_kernel, len(parts)),
        name="expand_rows",
        out_shape=jax.ShapeDtypeStruct((places, halves * width), jnp.bfloat16),
        compiler_params=params(8),
        cost_estimate=cost(2 * places * up.size, 2 * up.size + 2 * places * halves * width),
    )(*parts, flags, up)


def cached_kernel(heads, group, length_hbm, query_hbm, key_hbm, value_hbm, shrink_hbm, *refs):
    mean_hbm, lse_ref, shrink_ref, length_ref, query_ref, keys, values, mean_ref, wide_q, wide_o, sems, more = refs
    rows, window, width = keys.shape
    groups = width // HEAD_SIZE
    each = heads // groups
    packed = LANES // heads
    inverse_root = HEAD_SIZE ** (-0.5)

    def copies(i):
        here = pl.ds(i * group, group)
        return (
            pltpu.make_async_copy(key_hbm.at[here], keys.at[here], sems.at[0, i]),
            pltpu.make_async_copy(value_hbm.at[here], values.at[here], sems.at[1, i]),
        )

    ahead = 2
    for i in range(ahead):
        for copy in copies(i):
            copy.start()
    small = [(length_hbm, length_ref), (query_hbm, query_ref), (shrink_hbm, shrink_ref)]
    small = [pltpu.make_async_copy(a, b, more.at[n]) for n, (a, b) in enumerate(small)]
    for copy in small:
        copy.start()
    wide_q[...] = jnp.zeros_like(wide_q)
    lane = iota((window, LANES), 1) // heads
    position = iota((window, LANES), 0)
    sublane = iota((packed, LANES), 0)

    small[0].wait()
    small[1].wait()

    def finished(i):
        here = pl.ds(pl.multiple_of(i * group, group), group)
        return pltpu.make_async_copy(mean_ref.at[here], mean_hbm.at[here], sems.at[2, i])

    def step(i, carry):
        start = pl.multiple_of(i * group, group)
        for h in range(heads):
            part = query_ref[pl.ds(start, group), h * HEAD_SIZE : (h + 1) * HEAD_SIZE]
            wide_q[h // each, pl.ds(h, group, stride=heads), :] = part.astype(jnp.float32)
        key_copy, value_copy = copies(i)
        key_copy.wait()

        @pl.when(i + ahead < rows // group)
        def _():
            for copy in copies(i + ahead):
                copy.start()

        all_weights = []
        for first in range(0, group, packed):
            here = pl.ds(first * heads, LANES)
            query = jnp.concatenate([wide_q[k, here, :] for k in range(groups)], axis=1).astype(jnp.bfloat16)
            block = keys[pl.ds(start + first, packed)].reshape(packed * window, width)
            product = lax.dot_general(block, query, (((1,), (1,)), ((), ())), preferred_element_type=jnp.float32)
            scores = jnp.zeros((window, LANES), jnp.float32)
            limit = jnp.zeros((1, LANES), jnp.int32)
            for r in range(packed):
                scores = jnp.where(lane == r, product[r * window : (r + 1) * window], scores)
                limit = jnp.where(lane[:1] == r, length_ref[start + first + r], limit)
            scores = jnp.where(position < limit, scores * inverse_root, masked_score)
            highest = jnp.max(scores, axis=0, keepdims=True)
            terms = jnp.exp(scores - highest)
            total = jnp.sum(terms, axis=0, keepdims=True)
            all_weights.append(jnp.transpose(terms * (1.0 / total)).astype(jnp.bfloat16))
            logs = jnp.broadcast_to(highest + jnp.log(total), (packed, LANES))
            spread = logs
            for r in range(1, packed):
                spread = jnp.where(sublane == r, pltpu.roll(logs, LANES - r * heads, 1), spread)
            lse_ref[pl.ds(start + first, packed), :] = spread
        value_copy.wait()
        for r in range(0, group, 2):
            weights = all_weights[r // packed][(r % packed) * heads : (r % packed + 2) * heads]
            upper = iota(weights.shape, 0) < heads
            zero = jnp.zeros_like(weights)
            weights = jnp.concatenate([jnp.where(upper, weights, zero), jnp.where(upper, zero, weights)], axis=1)
            block = values[pl.ds(start + r, 2)].reshape(2 * window, width)
            mixed = jnp.dot(weights, block, preferred_element_type=jnp.float32)
            for j in range(2):
                for k in range(groups):
                    mine = pl.ds((r + j) * heads + k * each, each)
                    top = j * heads + k * each
                    wide_o[mine, :] = mixed[top : top + each, k * HEAD_SIZE : (k + 1) * HEAD_SIZE]
        for h in range(heads):
            mean_ref[pl.ds(start, group), h * HEAD_SIZE : (h + 1) * HEAD_SIZE] = wide_o[pl.ds(h, group, stride=heads), :]
        finished(i).start()
        return carry

    lax.fori_loop(0, rows // group, step, 0)
    for i in range(rows // group):
        finished(i).wait()
    small[2].wait()


def cached_attention(lengths, queries, keys, values, weights):
    rows, window, width = keys.shape
    wide = queries.shape[1]
    heads = wide // HEAD_SIZE
    group = max(16, LANES // heads)
    inside, outside = pl.BlockSpec(memory_space=pltpu.VMEM), pl.BlockSpec(memory_space=pltpu.HBM)
    return pl.pallas_call(
        functools.partial(cached_kernel, heads, group),
        name="cached_attention",
        in_specs=[outside] * 5,
        out_specs=[outside, inside, inside],
        scratch_shapes=[
            pltpu.SMEM(lengths.shape, lengths.dtype),
            pltpu.VMEM(queries.shape, queries.dtype),
            pltpu.VMEM(keys.shape, keys.dtype),
            pltpu.VMEM(values.shape, values.dtype),
            pltpu.VMEM((rows, wide), jnp.float32),
            pltpu.VMEM((width // HEAD_SIZE, group * heads, HEAD_SIZE), jnp.float32),
            pltpu.VMEM((group * heads, HEAD_SIZE), jnp.float32),
            pltpu.SemaphoreType.DMA((3, rows // group)),
            pltpu.SemaphoreType.DMA((3,)),
        ],
        out_shape=[
            jax.ShapeDtypeStruct((rows, wide), jnp.float32),
            jax.ShapeDtypeStruct((rows, LANES), jnp.float32),
            jax.ShapeDtypeStruct(weights.shape, weights.dtype),
        ],
        compiler_params=params(20),
        cost_estimate=cost(4 * rows * heads * window * width, 4 * keys.size + 6 * rows * wide, rows * heads * window),
    )(*(pinned(x) for x in (lengths, queries, keys, values, weights)))


def owner_of(place, p, parts):
    return place ^ p if parts == 4 else lax.rem(place + parts - p, parts)


def base_kernel(total, *refs):
    count = total - 1
    pieces, key_hbm, value_hbm, out_ref, last_keys, last_values, keys, values, sems = refs[:count], *refs[count:]
    shard, width = last_keys.shape
    place = lax.axis_index("tp")

    def copies(p):
        rows = pl.ds(pl.multiple_of(owner_of(place, p, total) * shard, shard), shard)
        key_to, value_to = (last_keys, last_values) if p == count else (keys.at[p], values.at[p])
        return (
            pltpu.make_async_copy(key_hbm.at[rows], key_to, sems.at[0, p]),
            pltpu.make_async_copy(value_hbm.at[rows], value_to, sems.at[1, p]),
        )

    for p in range(total):
        for copy in copies(p):
            copy.start()
    for p in range(count):
        for half, (copy, weights) in enumerate(zip(copies(p), (keys, values))):
            here = slice(half * width, (half + 1) * width)
            copy.wait()
            product = jnp.dot(pieces[p][...], weights[p], preferred_element_type=jnp.float32)
            out_ref[:, here] = product if p == 0 else out_ref[:, here] + product
    for copy in copies(count):
        copy.wait()


def base_products(pieces, key_matrix, value_matrix):
    rows, shard = pieces[0].shape
    width = key_matrix.shape[1]
    count = len(pieces)
    inside, outside = pl.BlockSpec(memory_space=pltpu.VMEM), pl.BlockSpec(memory_space=pltpu.HBM)
    last = jax.ShapeDtypeStruct((shard, width), key_matrix.dtype)
    return pl.pallas_call(
        functools.partial(base_kernel, count + 1),
        name="base_products",
        in_specs=[inside] * count + [outside, outside],
        out_specs=[inside] * 3,
        scratch_shapes=[
            pltpu.VMEM((count, shard, width), key_matrix.dtype),
            pltpu.VMEM((count, shard, width), key_matrix.dtype),
            pltpu.SemaphoreType.DMA((2, count + 1)),
        ],
        out_shape=[jax.ShapeDtypeStruct((rows, 2 * width), jnp.float32), last, last],
        compiler_params=params(16),
        cost_estimate=cost(4 * count * rows * shard * width, count * (4 * shard * width + 2 * rows * shard)),
    )(*pieces, pinned(key_matrix), pinned(value_matrix))


def finish_kernel(count, total, *refs):
    late, refs = refs[:count], refs[count:]
    last_keys, last_values, base_ref, back_ref, pick_ref, query_ref, mean_ref, lse_ref = refs[:8]
    new_key_ref, new_value_ref, context_ref = refs[8:]
    rows, wide = query_ref.shape
    width = new_key_ref.shape[1]
    heads = wide // HEAD_SIZE
    each = heads // (width // HEAD_SIZE)
    inverse_root = HEAD_SIZE ** (-0.5)
    delta = lax.dot_general(pick_ref[...], back_ref[...], (((0,), (0,)), ((), ())), preferred_element_type=jnp.float32)
    place = lax.axis_index("tp")
    piece = late[0][...]
    for other in late[1:]:
        piece = jnp.where((place == 0) | (place == total - 1), other[...], piece)
    last = [jnp.dot(piece, w[...], preferred_element_type=jnp.float32) for w in (last_keys, last_values)]
    base = (base_ref[...] + jnp.concatenate(last, axis=1) + delta).astype(jnp.bfloat16)
    new_key_ref[...] = base[:, :width]
    new_value_ref[...] = base[:, width:]
    keys, values = base[:, :width].astype(jnp.float32), base[:, width:].astype(jnp.float32)
    column = iota((rows, LANES), 1)
    own = jnp.zeros((rows, LANES), jnp.float32)
    for h in range(heads):
        k = h // each
        query = query_ref[:, h * HEAD_SIZE : (h + 1) * HEAD_SIZE].astype(jnp.float32)
        score = jnp.sum(query * keys[:, k * HEAD_SIZE : (k + 1) * HEAD_SIZE], axis=1, keepdims=True)
        own = jnp.where(column == h, score * inverse_root, own)
    share = 1.0 / (1.0 + jnp.exp(lse_ref[...] - own))
    for h in range(heads):
        k = h // each
        mean = mean_ref[:, h * HEAD_SIZE : (h + 1) * HEAD_SIZE]
        mixed = mean + share[:, h : h + 1] * (values[:, k * HEAD_SIZE : (k + 1) * HEAD_SIZE] - mean)
        context_ref[:, h * HEAD_SIZE : (h + 1) * HEAD_SIZE] = mixed.astype(jnp.bfloat16)


def finish(late, total, last_keys, last_values, base, back, pick, queries, mean, lse):
    rows, wide = queries.shape
    width = base.shape[1] // 2
    return pl.pallas_call(
        functools.partial(finish_kernel, len(late), total),
        name="finish_rows",
        out_shape=(
            jax.ShapeDtypeStruct((rows, width), jnp.bfloat16),
            jax.ShapeDtypeStruct((rows, width), jnp.bfloat16),
            jax.ShapeDtypeStruct((rows, wide), jnp.bfloat16),
        ),
        compiler_params=params(8),
        cost_estimate=cost(4 * rows * wide, 10 * rows * wide),
    )(*late, last_keys, last_values, base, back, pick, queries, mean, lse)


def swap(x, mask, size):
    return lax.ppermute(x, "tp", [(i, i ^ mask) for i in range(size)])


def turn(x, shift, size):
    return lax.ppermute(x, "tp", [(i, (i + shift) % size) for i in range(size)])


def others(x, size):
    return [turn(x, shift, size) for shift in range(1, size)]


def shards(
    hidden_in,
    queries,
    cache_keys,
    cached_value_rows,
    cache_lengths,
    base_key_matrix,
    base_value_matrix,
    shrink_weights,
    pooled_up_weights,
    block_owner,
    block_slot,
):
    rows_here, shard_width = hidden_in.shape
    replicas = lax.axis_size("rep")
    parts = lax.axis_size("tp")
    blocks_here = rows_here // BLK
    capacity = max(2, (2 * blocks_here + replicas - 1) // replicas)

    def all_to_all(x):
        kept = x.shape
        x = x.reshape(replicas, kept[0] // replicas, kept[1])
        return lax.all_to_all(x, "rep", split_axis=0, concat_axis=0, tiled=True).reshape(kept)

    outgoing, pick = pack(block_owner, block_slot, hidden_in, replicas, capacity)
    arrived = all_to_all(outgoing)

    if parts == 4:
        two = swap(hidden_in, 2, parts)
        one = swap(hidden_in, 1, parts)
    mean, lse, shrink_here = cached_attention(cache_lengths, queries, cache_keys, cached_value_rows, shrink_weights)
    arrived, mean, lse = lax.optimization_barrier((arrived, mean, lse))
    partial_rows, flags, up_here = shrink(arrived, shrink_here, pooled_up_weights)
    if parts == 4:
        paired = partial_rows + swap(partial_rows, 1, parts)
        one, paired = lax.optimization_barrier((one, paired))
        sums = [paired, swap(paired, 2, parts)]
        two, again, *sums = lax.optimization_barrier((two, hidden_in, *sums))
        outer = lax.ppermute(two, "tp", [(1, 0), (2, 3)])
        inner = lax.ppermute(again, "tp", [(1, 2), (2, 1)])
        early, late = [hidden_in, one, two], [inner, outer]
    else:
        sums = [partial_rows] + others(partial_rows, parts)
        pieces = [hidden_in] + others(hidden_in, parts)
        early, late = pieces[:-1], pieces[-1:]
    deltas = expand(sums, flags, up_here)
    back = all_to_all(deltas)
    deltas, *early = lax.optimization_barrier((deltas, *early))
    base, *last = base_products(early, base_key_matrix, base_value_matrix)
    return finish(late, parts, *last, base, back, pick, queries, mean, lse)


def solution(mesh):
    return jax.shard_map(
        shards,
        mesh=mesh,
        in_specs=(
            P("rep", "tp"),
            P("rep", "tp"),
            P("rep", None, "tp"),
            P("rep", None, "tp"),
            P("rep"),
            P(None, "tp"),
            P(None, "tp"),
            P("rep", "tp", None),
            P("rep", None, None, "tp"),
            P("rep", None),
            P("rep"),
        ),
        out_specs=(P("rep", "tp"), P("rep", "tp"), P("rep", "tp")),
        check_vma=False,
    )
```

time: 104 us -> 59.4 us (0.57)
  the two profiles are of different devices: /device:TPU:0 before, /device:TPU:8 now
where the time goes in v2:
time: 59.4 us; the launch traced here: 59 us
  starting transfers between devices  22.8 us (38%)
  Pallas kernels  20.8 us (35%)
  waiting for transfers between devices  12.6 us (21%)
  local copies, waits for them, and re-layouts  2.05 us (3%)
  between operations  0.72 us (1%)
    ppermute x4, waiting for transfers between devices, swap(): return lax.ppermute(x, 'tp', [(i, i ^ mask) for i in range(size)])  10.7 us
    pallas_call x1, Pallas kernels, cached_attention(): pl.pallas_call(functools.partial(cached_kernel, heads, group), name='cach...  8.83 us
    all_to_all x2, starting transfers between devices, all_to_all(): lax.all_to_all(x, 'rep', split_axis=0, concat_axis=0, tiled=True)  7.25 us
    ppermute x4, starting transfers between devices, swap(): return lax.ppermute(x, 'tp', [(i, i ^ mask) for i in range(size)])  7.09 us
    pallas_call x1, Pallas kernels, base_products(): pl.pallas_call(functools.partial(base_kernel, count + 1), name='base_prod...  4.64 us
    ppermute x1, starting transfers between devices, shards(): inner = lax.ppermute(again, 'tp', [(1, 2), (2, 1)])  4.53 us
    ppermute x1, starting transfers between devices, shards(): outer = lax.ppermute(two, 'tp', [(1, 0), (2, 3)])  3.96 us
    pallas_call x1, Pallas kernels, finish(): pl.pallas_call(functools.partial(finish_kernel, len(late), total), name='...  2.96 us
  transfers between devices with their start and end apart: 8, of which 4 were waited for; matrix products, arithmetic and copies ran while one was open for 0% of the time, Pallas kernels for 26%

profile of v2, /device:TPU:8, one launch (start us, length us, event | category | flops | bytes accessed | tf_op | source)
XLA Modules:
  0.0 59.0 jit_solution(8482400110546719879)
XLA Ops:
  0.6 2.4 %pack_rows.1 = (bf16[192,2176]{1,0:T(8,128)(2,1)}, bf16[192,96]{1,0:T(8,128)(2,1)}) custom-call(s32[24]{0:T(128)} %bitcast.8, s32[24]{0:T(128)} %slot_ref.1, bf16[96,2048]{1,0:T(8,128)(2,1)} %refs_0_), custom_call_target="tpu_custom_call" | custom-call | flops 75497472 | bytes 1179648 | tf_op jit(solution)/shard_map/pack_rows/pallas_call | solution.py:65
  3.0 3.7 %all-to-all-start = ((bf16[8,24,2176]{2,1,0:T(8,128)(2,1)}), bf16[8,24,2176]{2,1,0:T(8,128)(2,1)S(1)}, u32[]{:S(2)}, u32[]{:S(2)}) async-start(bf16[8,24,2176]{2,1,0:T(8,128)(2,1)} %bitcast.7), calls=%async_computation | async-start | bytes 1671168 | tf_op jit(solution)/shard_map/all_to_all | solution.py:402
  6.7 0.0 copy-start
  6.7 0.5 collective-permute-start.1
  7.2 2.6 %collective-permute-start = (bf16[96,2048]{1,0:T(8,128)(2,1)}, bf16[96,2048]{1,0:T(8,128)(2,1)}, u32[]{:S(2)}, u32[]{:S(2)}) collective-permute-start(bf16[96,2048]{1,0:T(8,128)(2,1)} %refs_0_), channel_id=1, source_target_pairs={{0,2},{1,3},{2,0},{3,1},{4,6},{5,7},{6,4},{7,5},{8,10},{9,11},{10,... | collective-permute-start | bytes 1179656 | tf_op jit(solution)/shard_map/ppermute | solution.py:369
  9.8 8.8 %cached_attention.1 = (f32[96,2048]{1,0:T(8,128)S(1)}, f32[96,128]{1,0:T(8,128)S(1)}, bf16[4,2048,128]{2,1,0:T(8,128)(2,1)S(1)}) custom-call(s32[96]{0:T(128)} %length_hbm.1, bf16[96,2048]{1,0:T(8,128)(2,1)} %refs_7_.1, bf16[96,128,256]{2,1,0:T(8,128)(2,1)} %key_hbm.1, bf16[96,128,256]{2,1,0:T(8,128)(2,1)} %value_hbm.1, bf16[4,2048,128]{2,1,0:T(8,128)(2,1)} %shrink_hbm.1), custom_call_target="tpu_custom_call" | custom-call | flops 201326592 | bytes 13762560 | tf_op jit(solution)/shard_map/cached_attention/pallas_call | solution.py:239
  18.7 0.0 copy-start.2
  18.7 0.9 %copy-done.2 = f32[96,2048]{1,0:T(8,128)} copy-done((f32[96,2048]{1,0:T(8,128)}, f32[96,2048]{1,0:T(8,128)S(1)}, u32[]{:S(2)}) %copy-start.2) | copy-done | bytes 786456
  19.6 0.3 all-to-all-done
  19.9 1.0 %shrink_rows.1 = (f32[192,128]{1,0:T(8,128)S(1)}, bf16[192,128]{1,0:T(8,128)(2,1)S(1)}, bf16[4,2,64,256]{3,2,1,0:T(8,128)(2,1)S(1)}) custom-call(bf16[192,2176]{1,0:T(8,128)(2,1)S(1)} %bitcast.5, bf16[4,2048,128]{2,1,0:T(8,128)(2,1)S(1)} %get-tuple-element.30.shrink_ref, bf16[4,2,64,256]{3,2,1,0:T(8,128)(2,1)} %up_hbm.1), custom_call_target="tpu_custom_call" | custom-call | flops 402653184 | bytes 2883584 | tf_op jit(solution)/shard_map/shrink_rows/pallas_call | solution.py:96
  20.8 1.4 %collective-permute-start.2 = (f32[192,128]{1,0:T(8,128)S(1)}, f32[192,128]{1,0:T(8,128)S(1)}, u32[]{:S(2)}, u32[]{:S(2)}) collective-permute-start(f32[192,128]{1,0:T(8,128)S(1)} %get-tuple-element.31), channel_id=1, source_target_pairs={{0,1},{1,0},{2,3},{3,2},{4,5},{5,4},{6,7},{7,6},{8,9},{9,8},{10,11... | collective-permute-start | bytes 294920 | tf_op jit(solution)/shard_map/ppermute | solution.py:369
  22.2 6.8 %collective-permute-done.2 = f32[192,128]{1,0:T(8,128)S(1)} collective-permute-done((f32[192,128]{1,0:T(8,128)S(1)}, f32[192,128]{1,0:T(8,128)S(1)}, u32[]{:S(2)}, u32[]{:S(2)}) %collective-permute-start.2) | collective-permute-done | bytes 98336 | tf_op jit(solution)/shard_map/ppermute | solution.py:369
  29.1 0.0 collective-permute-done.1.refs_1_
  29.1 2.6 %collective-permute-start.3 = (f32[192,128]{1,0:T(8,128)S(1)}, f32[192,128]{1,0:T(8,128)S(1)}, u32[]{:S(2)}, u32[]{:S(2)}) collective-permute-start(f32[192,128]{1,0:T(8,128)S(1)} %add.3.refs_0_), channel_id=1, source_target_pairs={{0,2},{1,3},{2,0},{3,1},{4,6},{5,7},{6,4},{7,5},{8,10},{9,11},{10,... | collective-permute-start | bytes 294920 | tf_op jit(solution)/shard_map/ppermute | solution.py:369
  31.7 0.0 collective-permute-done.refs_2_
  31.7 3.9 %collective-permute-done.3.refs_1_ = f32[192,128]{1,0:T(8,128)S(1)} collective-permute-done((f32[192,128]{1,0:T(8,128)S(1)}, f32[192,128]{1,0:T(8,128)S(1)}, u32[]{:S(2)}, u32[]{:S(2)}) %collective-permute-start.3) | collective-permute-done | bytes 98336 | tf_op jit(solution)/shard_map/ppermute | solution.py:369
  35.6 4.0 %collective-permute-start.5 = (bf16[96,2048]{1,0:T(8,128)(2,1)}, bf16[96,2048]{1,0:T(8,128)(2,1)}, u32[]{:S(2)}, u32[]{:S(2)}) collective-permute-start(bf16[96,2048]{1,0:T(8,128)(2,1)} %collective-permute-done.refs_2_), channel_id=1, source_target_pairs={{1,0},{2,3},{5,4},{6,7},{9,8},{10,11},{13,12},{14,15},{17,16},{18,... | collective-permute-start | bytes 1179656 | tf_op jit(solution)/shard_map/ppermute | solution.py:418
  39.5 0.0 copy-done
  39.5 4.5 %collective-permute-start.4 = (bf16[96,2048]{1,0:T(8,128)(2,1)S(1)}, bf16[96,2048]{1,0:T(8,128)(2,1)}, u32[]{:S(2)}, u32[]{:S(2)}) collective-permute-start(bf16[96,2048]{1,0:T(8,128)(2,1)S(1)} %copy-done), channel_id=1, source_target_pairs={{1,2},{2,1},{5,6},{6,5},{9,10},{10,9},{13,14},{14,13},{17,18},{18,... | collective-permute-start | bytes 1179656 | tf_op jit(solution)/shard_map/ppermute | solution.py:419
  44.1 1.0 %expand_rows.1 = bf16[192,512]{1,0:T(8,128)(2,1)} custom-call(f32[192,128]{1,0:T(8,128)S(1)} %add.3.refs_0_, f32[192,128]{1,0:T(8,128)S(1)} %collective-permute-done.3.refs_1_, bf16[192,128]{1,0:T(8,128)(2,1)S(1)} %get-tuple-element.37.refs_2_, bf16[4,2,64,256]{3,2,1,0:T(8,128)(2,1)S(1)} %get-tuple-element.38.refs_3_), custom_call_target="tpu_custom_call" | custom-call | flops 50331648 | bytes 458752 | tf_op jit(solution)/shard_map/expand_rows/pallas_call | solution.py:131
  45.1 3.5 %all-to-all-start.1 = ((bf16[8,24,512]{2,1,0:T(8,128)(2,1)}), bf16[8,24,512]{2,1,0:T(8,128)(2,1)S(1)}, u32[]{:S(2)}, u32[]{:S(2)}) async-start(bf16[8,24,512]{2,1,0:T(8,128)(2,1)} %bitcast.3), calls=%async_computation.1 | async-start | bytes 393216 | tf_op jit(solution)/shard_map/all_to_all | solution.py:402
  48.6 0.0 copy-start.1
  48.6 0.0 copy-start.4
  48.6 4.6 %base_products.1 = (f32[96,512]{1,0:T(8,128)S(1)}, bf16[2048,256]{1,0:T(8,128)(2,1)S(1)}, bf16[2048,256]{1,0:T(8,128)(2,1)S(1)}) custom-call(bf16[96,2048]{1,0:T(8,128)(2,1)S(1)} %copy-done, bf16[96,2048]{1,0:T(8,128)(2,1)} %collective-permute-done.1.refs_1_, bf16[96,2048]{1,0:T(8,128)(2,1)} %collective-permute-done.refs_2_, bf16[8192,256]{1,0:T(8,128)(2,1)} %refs_3_.1, ...), custom_call_target="tpu_custom_call" | custom-call | flops 603979776 | bytes 7471104 | tf_op jit(solution)/shard_map/base_products/pallas_call | solution.py:302
  53.3 1.6 %all-to-all-done.1 = bf16[8,24,512]{2,1,0:T(8,128)(2,1)S(1)} async-done(((bf16[8,24,512]{2,1,0:T(8,128)(2,1)}), bf16[8,24,512]{2,1,0:T(8,128)(2,1)S(1)}, u32[]{:S(2)}, u32[]{:S(2)}) %all-to-all-start.1) | async-done | bytes 196640 | tf_op jit(solution)/shard_map/all_to_all | solution.py:402
  54.9 0.0 collective-permute-done.5.refs_1_
  54.9 0.0 collective-permute-done.4.refs_0_
  54.9 0.0 copy-done.1
  54.9 0.0 copy-done.4
  54.9 0.0 copy-start.3
  54.9 1.1 %copy-done.3 = f32[96,2048]{1,0:T(8,128)S(1)} copy-done((f32[96,2048]{1,0:T(8,128)S(1)}, f32[96,2048]{1,0:T(8,128)}, u32[]{:S(2)}) %copy-start.3) | copy-done | bytes 786456
  56.0 3.0 %finish_rows.1 = (bf16[96,256]{1,0:T(8,128)(2,1)}, bf16[96,256]{1,0:T(8,128)(2,1)}, bf16[96,2048]{1,0:T(8,128)(2,1)}) custom-call(bf16[96,2048]{1,0:T(8,128)(2,1)} %collective-permute-done.4.refs_0_, bf16[96,2048]{1,0:T(8,128)(2,1)} %collective-permute-done.5.refs_1_, bf16[2048,256]{1,0:T(8,128)(2,1)S(1)} %get-tuple-element.43.refs_2_, ...), custom_call_target="tpu_custom_call" | custom-call | flops 786432 | bytes 1966080 | tf_op jit(solution)/shard_map/finish_rows/pallas_call | solution.py:355
  (1 shorter events, 0.0 us)
Async XLA Ops:
  3.0 16.9 %all-to-all-start = ((bf16[8,24,2176]{2,1,0:T(8,128)(2,1)}), bf16[8,24,2176]{2,1,0:T(8,128)(2,1)S(1)}, u32[]{:S(2)}, u32[]{:S(2)}) async-start(bf16[8,24,2176]{2,1,0:T(8,128)(2,1)} %bitcast.7), calls=%async_computation | async-start | bytes 1671168 | tf_op jit(solution)/shard_map/all_to_all | solution.py:402
  6.7 32.8 %copy-start = (bf16[96,2048]{1,0:T(8,128)(2,1)S(1)}, bf16[96,2048]{1,0:T(8,128)(2,1)}, u32[]{:S(2)}) copy-start(bf16[96,2048]{1,0:T(8,128)(2,1)} %refs_0_) | copy-start | bytes 1179652
  6.7 22.3 %collective-permute-start.1 = (bf16[96,2048]{1,0:T(8,128)(2,1)}, bf16[96,2048]{1,0:T(8,128)(2,1)}, u32[]{:S(2)}, u32[]{:S(2)}) collective-permute-start(bf16[96,2048]{1,0:T(8,128)(2,1)} %refs_0_), channel_id=1, source_target_pairs={{0,1},{1,0},{2,3},{3,2},{4,5},{5,4},{6,7},{7,6},{8,9},{9,8},{10,11... | collective-permute-start | bytes 1179656 | tf_op jit(solution)/shard_map/ppermute | solution.py:369
  7.2 24.4 %collective-permute-start = (bf16[96,2048]{1,0:T(8,128)(2,1)}, bf16[96,2048]{1,0:T(8,128)(2,1)}, u32[]{:S(2)}, u32[]{:S(2)}) collective-permute-start(bf16[96,2048]{1,0:T(8,128)(2,1)} %refs_0_), channel_id=1, source_target_pairs={{0,2},{1,3},{2,0},{3,1},{4,6},{5,7},{6,4},{7,5},{8,10},{9,11},{10,... | collective-permute-start | bytes 1179656 | tf_op jit(solution)/shard_map/ppermute | solution.py:369
  18.7 0.9 %copy-start.2 = (f32[96,2048]{1,0:T(8,128)}, f32[96,2048]{1,0:T(8,128)S(1)}, u32[]{:S(2)}) copy-start(f32[96,2048]{1,0:T(8,128)S(1)} %get-tuple-element.47.refs_8_) | copy-start | bytes 2359300
  20.8 8.2 %collective-permute-start.2 = (f32[192,128]{1,0:T(8,128)S(1)}, f32[192,128]{1,0:T(8,128)S(1)}, u32[]{:S(2)}, u32[]{:S(2)}) collective-permute-start(f32[192,128]{1,0:T(8,128)S(1)} %get-tuple-element.31), channel_id=1, source_target_pairs={{0,1},{1,0},{2,3},{3,2},{4,5},{5,4},{6,7},{7,6},{8,9},{9,8},{10,11... | collective-permute-start | bytes 294920 | tf_op jit(solution)/shard_map/ppermute | solution.py:369
  29.1 6.5 %collective-permute-start.3 = (f32[192,128]{1,0:T(8,128)S(1)}, f32[192,128]{1,0:T(8,128)S(1)}, u32[]{:S(2)}, u32[]{:S(2)}) collective-permute-start(f32[192,128]{1,0:T(8,128)S(1)} %add.3.refs_0_), channel_id=1, source_target_pairs={{0,2},{1,3},{2,0},{3,1},{4,6},{5,7},{6,4},{7,5},{8,10},{9,11},{10,... | collective-permute-start | bytes 294920 | tf_op jit(solution)/shard_map/ppermute | solution.py:369
  35.6 19.3 %collective-permute-start.5 = (bf16[96,2048]{1,0:T(8,128)(2,1)}, bf16[96,2048]{1,0:T(8,128)(2,1)}, u32[]{:S(2)}, u32[]{:S(2)}) collective-permute-start(bf16[96,2048]{1,0:T(8,128)(2,1)} %collective-permute-done.refs_2_), channel_id=1, source_target_pairs={{1,0},{2,3},{5,4},{6,7},{9,8},{10,11},{13,12},{14,15},{17,16},{18,... | collective-permute-start | bytes 1179656 | tf_op jit(solution)/shard_map/ppermute | solution.py:418
  39.5 15.3 %collective-permute-start.4 = (bf16[96,2048]{1,0:T(8,128)(2,1)S(1)}, bf16[96,2048]{1,0:T(8,128)(2,1)}, u32[]{:S(2)}, u32[]{:S(2)}) collective-permute-start(bf16[96,2048]{1,0:T(8,128)(2,1)S(1)} %copy-done), channel_id=1, source_target_pairs={{1,2},{2,1},{5,6},{6,5},{9,10},{10,9},{13,14},{14,13},{17,18},{18,... | collective-permute-start | bytes 1179656 | tf_op jit(solution)/shard_map/ppermute | solution.py:419
  45.1 9.8 %all-to-all-start.1 = ((bf16[8,24,512]{2,1,0:T(8,128)(2,1)}), bf16[8,24,512]{2,1,0:T(8,128)(2,1)S(1)}, u32[]{:S(2)}, u32[]{:S(2)}) async-start(bf16[8,24,512]{2,1,0:T(8,128)(2,1)} %bitcast.3), calls=%async_computation.1 | async-start | bytes 393216 | tf_op jit(solution)/shard_map/all_to_all | solution.py:402
  48.6 6.2 %copy-start.1 = (bf16[96,2048]{1,0:T(8,128)(2,1)S(1)}, bf16[96,2048]{1,0:T(8,128)(2,1)}, u32[]{:S(2)}) copy-start(bf16[96,2048]{1,0:T(8,128)(2,1)} %refs_7_.1) | copy-start | bytes 1179652
  48.6 6.2 %copy-start.4 = (bf16[192,96]{1,0:T(8,128)(2,1)S(1)}, bf16[192,96]{1,0:T(8,128)(2,1)}, u32[]{:S(2)}) copy-start(bf16[192,96]{1,0:T(8,128)(2,1)} %get-tuple-element.46.refs_6_) | copy-start | bytes 110596
  54.9 1.1 %copy-start.3 = (f32[96,2048]{1,0:T(8,128)S(1)}, f32[96,2048]{1,0:T(8,128)}, u32[]{:S(2)}) copy-start(f32[96,2048]{1,0:T(8,128)} %copy-done.2) | copy-start | bytes 2359300

commit v3 on v2

--- a/solution.py
+++ b/solution.py
@@ -52,7 +52,11 @@
     row_target = jnp.sum(jnp.where(spread, jnp.broadcast_to(target, (blocks, rows)), 0.0), axis=0, keepdims=True)
     row_target = row_target.astype(jnp.int32) * BLK + iota((1, rows), 1) % BLK
     pick = jnp.where(iota((places, rows), 0) == row_target, 1.0, 0.0).astype(jnp.bfloat16)
-    pick_ref[...] = pick
+    gather = iota((rows, blocks), 1) == iota((rows, blocks), 0) // BLK
+    target = jnp.sum(jnp.where(iota(square, 0) == iota(square, 1), target, 0.0), axis=0, keepdims=True)
+    target = jnp.sum(jnp.where(gather, target, 0.0), axis=1, keepdims=True)
+    target = target.astype(jnp.int32) * BLK + iota((rows, 1), 0) % BLK
+    pick_ref[...] = jnp.where(iota((rows, places), 1) == target, 1.0, 0.0).astype(jnp.bfloat16)
     flags = jnp.where(iota((rows, LANES), 1) == row_slot, 1.0, 0.0).astype(jnp.bfloat16)
     out_ref[:, :width] = jnp.dot(pick, hidden_ref[...], preferred_element_type=jnp.float32).astype(jnp.bfloat16)
     out_ref[:, width:] = jnp.dot(pick, flags, preferred_element_type=jnp.float32).astype(jnp.bfloat16)
@@ -68,14 +72,14 @@
         in_specs=[scalars, scalars, pl.BlockSpec(memory_space=pltpu.VMEM)],
         out_shape=(
             jax.ShapeDtypeStruct((places, width + LANES), jnp.bfloat16),
-            jax.ShapeDtypeStruct((places, rows), jnp.bfloat16),
+            jax.ShapeDtypeStruct((rows, places), jnp.bfloat16),
         ),
         compiler_params=params(61),
         cost_estimate=cost(2 * places * rows * width, 2 * (places + rows) * width),
     )(block_owner[:, 0], block_slot, hidden)
 
 
-def shrink_kernel(rows_ref, shrink_ref, up_hbm, out_ref, flag_ref, up_ref, sem):
+def shrink_kernel(rows_ref, shrink_ref, up_hbm, out_ref, sent_ref, flag_ref, up_ref, sem):
     pool, width, rank = shrink_ref.shape
     copy = pltpu.make_async_copy(up_hbm, up_ref, sem)
     copy.start()
@@ -86,6 +90,7 @@
         part = jnp.dot(rows, shrink_ref[a], preferred_element_type=jnp.float32)
         total += part * rows_ref[:, width + a : width + a + 1].astype(jnp.float32)
     out_ref[...] = total
+    sent_ref[...] = total.astype(jnp.bfloat16)
     copy.wait()
 
 
@@ -97,9 +102,10 @@
         shrink_kernel,
         name="shrink_rows",
         in_specs=[inside, inside, outside],
-        out_specs=[inside] * 3,
+        out_specs=[inside] * 4,
         out_shape=(
             jax.ShapeDtypeStruct((places, rank), jnp.float32),
+            jax.ShapeDtypeStruct((places, rank), jnp.bfloat16),
             jax.ShapeDtypeStruct((places, LANES), jnp.bfloat16),
             jax.ShapeDtypeStruct(up.shape, up.dtype),
         ),
@@ -138,9 +144,9 @@
 
 
 def cached_kernel(heads, group, length_hbm, query_hbm, key_hbm, value_hbm, shrink_hbm, *refs):
+    groups = key_hbm.shape[2] // HEAD_SIZE
     mean_hbm, lse_ref, shrink_ref, length_ref, query_ref, keys, values, mean_ref, wide_q, wide_o, sems, more = refs
     rows, window, width = keys.shape
-    groups = width // HEAD_SIZE
     each = heads // groups
     packed = LANES // heads
     inverse_root = HEAD_SIZE ** (-0.5)
@@ -235,6 +241,7 @@
     wide = queries.shape[1]
     heads = wide // HEAD_SIZE
     group = max(16, LANES // heads)
+    groups = width // HEAD_SIZE
     inside, outside = pl.BlockSpec(memory_space=pltpu.VMEM), pl.BlockSpec(memory_space=pltpu.HBM)
     return pl.pallas_call(
         functools.partial(cached_kernel, heads, group),
@@ -247,13 +254,13 @@
             pltpu.VMEM(keys.shape, keys.dtype),
             pltpu.VMEM(values.shape, values.dtype),
             pltpu.VMEM((rows, wide), jnp.float32),
-            pltpu.VMEM((width // HEAD_SIZE, group * heads, HEAD_SIZE), jnp.float32),
+            pltpu.VMEM((groups, group * heads, HEAD_SIZE), jnp.float32),
             pltpu.VMEM((group * heads, HEAD_SIZE), jnp.float32),
             pltpu.SemaphoreType.DMA((3, rows // group)),
             pltpu.SemaphoreType.DMA((3,)),
         ],
         out_shape=[
-            jax.ShapeDtypeStruct((rows, wide), jnp.float32),
+            pltpu.HBM((rows, wide), jnp.float32),
             jax.ShapeDtypeStruct((rows, LANES), jnp.float32),
             jax.ShapeDtypeStruct(weights.shape, weights.dtype),
         ],
@@ -315,22 +322,50 @@
     )(*pieces, pinned(key_matrix), pinned(value_matrix))
 
 
-def finish_kernel(count, total, *refs):
-    late, refs = refs[:count], refs[count:]
-    last_keys, last_values, base_ref, back_ref, pick_ref, query_ref, mean_ref, lse_ref = refs[:8]
-    new_key_ref, new_value_ref, context_ref = refs[8:]
+def last_kernel(count, total, *refs):
+    sources, (keys, values, base_ref, out_ref, piece_ref, sem) = refs[:count], refs[count:]
+    width = keys.shape[1]
+    place = lax.axis_index("tp")
+    outer = (place == 0) | (place == total - 1)
+    for n, source in enumerate(sources):
+
+        @pl.when(True if count == 1 else outer == (n == count - 1))
+        def _():
+            copy = pltpu.make_async_copy(source, piece_ref, sem)
+            copy.start()
+            copy.wait()
+
+    for half, weights in enumerate((keys, values)):
+        here = slice(half * width, (half + 1) * width)
+        out_ref[:, here] = base_ref[:, here] + jnp.dot(piece_ref[...], weights[...], preferred_element_type=jnp.float32)
+
+
+def last_product(late, total, keys, values, base):
+    inside, outside = pl.BlockSpec(memory_space=pltpu.VMEM), pl.BlockSpec(memory_space=pltpu.HBM)
+    return pl.pallas_call(
+        functools.partial(last_kernel, len(late), total),
+        name="last_product",
+        in_specs=[outside] * len(late) + [inside] * 3,
+        out_specs=inside,
+        out_shape=jax.ShapeDtypeStruct(base.shape, base.dtype),
+        scratch_shapes=[pltpu.VMEM(late[0].shape, late[0].dtype), pltpu.SemaphoreType.DMA],
+        compiler_params=params(8),
+        cost_estimate=cost(2 * late[0].size * base.shape[1], 4 * keys.size),
+    )(*late, keys, values, base)
+
+
+def finish_kernel(base_ref, back_ref, pick_ref, query_ref, lse_ref, mean_hbm, *refs):
+    new_key_ref, new_value_ref, context_hbm, mean_ref, context_ref, sems = refs
     rows, wide = query_ref.shape
     width = new_key_ref.shape[1]
     heads = wide // HEAD_SIZE
-    each = heads // (width // HEAD_SIZE)
+    groups = width // HEAD_SIZE
+    each = heads // groups
     inverse_root = HEAD_SIZE ** (-0.5)
-    delta = lax.dot_general(pick_ref[...], back_ref[...], (((0,), (0,)), ((), ())), preferred_element_type=jnp.float32)
-    place = lax.axis_index("tp")
-    piece = late[0][...]
-    for other in late[1:]:
-        piece = jnp.where((place == 0) | (place == total - 1), other[...], piece)
-    last = [jnp.dot(piece, w[...], preferred_element_type=jnp.float32) for w in (last_keys, last_values)]
-    base = (base_ref[...] + jnp.concatenate(last, axis=1) + delta).astype(jnp.bfloat16)
+    mean_copy = pltpu.make_async_copy(mean_hbm, mean_ref, sems.at[groups])
+    mean_copy.start()
+    delta = jnp.dot(pick_ref[...], back_ref[...], preferred_element_type=jnp.float32)
+    base = (base_ref[...] + delta).astype(jnp.bfloat16)
     new_key_ref[...] = base[:, :width]
     new_value_ref[...] = base[:, width:]
     keys, values = base[:, :width].astype(jnp.float32), base[:, width:].astype(jnp.float32)
@@ -342,27 +377,41 @@
         score = jnp.sum(query * keys[:, k * HEAD_SIZE : (k + 1) * HEAD_SIZE], axis=1, keepdims=True)
         own = jnp.where(column == h, score * inverse_root, own)
     share = 1.0 / (1.0 + jnp.exp(lse_ref[...] - own))
-    for h in range(heads):
-        k = h // each
-        mean = mean_ref[:, h * HEAD_SIZE : (h + 1) * HEAD_SIZE]
-        mixed = mean + share[:, h : h + 1] * (values[:, k * HEAD_SIZE : (k + 1) * HEAD_SIZE] - mean)
-        context_ref[:, h * HEAD_SIZE : (h + 1) * HEAD_SIZE] = mixed.astype(jnp.bfloat16)
-
-
-def finish(late, total, last_keys, last_values, base, back, pick, queries, mean, lse):
+    mean_copy.wait()
+    for k in range(groups):
+        for h in range(k * each, (k + 1) * each):
+            mean = mean_ref[:, h * HEAD_SIZE : (h + 1) * HEAD_SIZE]
+            mixed = mean + share[:, h : h + 1] * (values[:, k * HEAD_SIZE : (k + 1) * HEAD_SIZE] - mean)
+            context_ref[:, h * HEAD_SIZE : (h + 1) * HEAD_SIZE] = mixed.astype(jnp.bfloat16)
+        part = pl.ds(k * each * HEAD_SIZE, each * HEAD_SIZE)
+        pltpu.make_async_copy(context_ref.at[:, part], context_hbm.at[:, part], sems.at[k]).start()
+    for k in range(groups):
+        part = pl.ds(k * each * HEAD_SIZE, each * HEAD_SIZE)
+        pltpu.make_async_copy(context_ref.at[:, part], context_hbm.at[:, part], sems.at[k]).wait()
+
+
+def finish(base, back, pick, queries, lse, mean):
     rows, wide = queries.shape
     width = base.shape[1] // 2
-    return pl.pallas_call(
-        functools.partial(finish_kernel, len(late), total),
+    inside, outside = pl.BlockSpec(memory_space=pltpu.VMEM), pl.BlockSpec(memory_space=pltpu.HBM)
+    return pl.pallas_call(
+        finish_kernel,
         name="finish_rows",
+        in_specs=[inside] * 5 + [outside],
+        out_specs=[inside, inside, outside],
         out_shape=(
             jax.ShapeDtypeStruct((rows, width), jnp.bfloat16),
             jax.ShapeDtypeStruct((rows, width), jnp.bfloat16),
             jax.ShapeDtypeStruct((rows, wide), jnp.bfloat16),
         ),
+        scratch_shapes=[
+            pltpu.VMEM(mean.shape, mean.dtype),
+            pltpu.VMEM((rows, wide), jnp.bfloat16),
+            pltpu.SemaphoreType.DMA((width // HEAD_SIZE + 1,)),
+        ],
         compiler_params=params(8),
         cost_estimate=cost(4 * rows * wide, 10 * rows * wide),
-    )(*late, last_keys, last_values, base, back, pick, queries, mean, lse)
+    )(base, back, pick, queries, lse, pinned(mean))
 
 
 def swap(x, mask, size):
@@ -405,28 +454,29 @@
     arrived = all_to_all(outgoing)
 
     if parts == 4:
+        one = swap(hidden_in, 1, parts)
         two = swap(hidden_in, 2, parts)
-        one = swap(hidden_in, 1, parts)
     mean, lse, shrink_here = cached_attention(cache_lengths, queries, cache_keys, cached_value_rows, shrink_weights)
-    arrived, mean, lse = lax.optimization_barrier((arrived, mean, lse))
-    partial_rows, flags, up_here = shrink(arrived, shrink_here, pooled_up_weights)
+    arrived, lse = lax.optimization_barrier((arrived, lse))
+    partial_rows, sent, flags, up_here = shrink(arrived, shrink_here, pooled_up_weights)
     if parts == 4:
-        paired = partial_rows + swap(partial_rows, 1, parts)
+        paired = partial_rows + swap(sent, 1, parts).astype(jnp.float32)
         one, paired = lax.optimization_barrier((one, paired))
-        sums = [paired, swap(paired, 2, parts)]
+        sums = [paired, swap(paired.astype(jnp.bfloat16), 2, parts)]
         two, again, *sums = lax.optimization_barrier((two, hidden_in, *sums))
         outer = lax.ppermute(two, "tp", [(1, 0), (2, 3)])
         inner = lax.ppermute(again, "tp", [(1, 2), (2, 1)])
         early, late = [hidden_in, one, two], [inner, outer]
     else:
-        sums = [partial_rows] + others(partial_rows, parts)
+        sums = [partial_rows] + others(sent, parts)
         pieces = [hidden_in] + others(hidden_in, parts)
         early, late = pieces[:-1], pieces[-1:]
     deltas = expand(sums, flags, up_here)
     back = all_to_all(deltas)
     deltas, *early = lax.optimization_barrier((deltas, *early))
     base, *last = base_products(early, base_key_matrix, base_value_matrix)
-    return finish(late, parts, *last, base, back, pick, queries, mean, lse)
+    base = last_product(late, parts, *last, base)
+    return finish(base, back, pick, queries, lse, mean)
 
 
 def solution(mesh):

time: 59.4 us -> 53.6 us (0.902)
  the two profiles are of different devices: /device:TPU:8 before, /device:TPU:11 now
where the time goes in v3:
time: 53.6 us; the launch traced here: 53.2 us
  Pallas kernels  21 us (39%)
  starting transfers between devices  21 us (39%)
  waiting for transfers between devices  10.4 us (19%)
  between operations  0.75 us (1%)
    all_to_all x2, starting transfers between devices, all_to_all(): lax.all_to_all(x, 'rep', split_axis=0, concat_axis=0, tiled=True)  11.7 us
    ppermute x4, waiting for transfers between devices, swap(): return lax.ppermute(x, 'tp', [(i, i ^ mask) for i in range(size)])  9.7 us
    pallas_call x1, Pallas kernels, cached_attention(): pl.pallas_call(functools.partial(cached_kernel, heads, group), name='cach...  8.46 us
    pallas_call x1, Pallas kernels, base_products(): pl.pallas_call(functools.partial(base_kernel, count + 1), name='base_prod...  4.64 us
    ppermute x4, starting transfers between devices, swap(): return lax.ppermute(x, 'tp', [(i, i ^ mask) for i in range(size)])  4.25 us
    ppermute x1, starting transfers between devices, shards(): inner = lax.ppermute(again, 'tp', [(1, 2), (2, 1)])  3.09 us
    pallas_call x1, Pallas kernels, finish(): pl.pallas_call(finish_kernel, name='finish_rows', in_specs=[inside] * 5 +...  2.79 us
    pallas_call x1, Pallas kernels, pack(): pl.pallas_call(functools.partial(pack_kernel, capacity), name='pack_rows'...  2.37 us
  transfers between devices with their start and end apart: 8, of which 3 were waited for; matrix products, arithmetic and copies ran while one was open for 0% of the time, Pallas kernels for 30%

profile of v3, /device:TPU:11, one launch (start us, length us, event | category | flops | bytes accessed | tf_op | source)
XLA Modules:
  0.0 53.2 jit_solution(1357580931011725314)
XLA Ops:
  0.6 2.4 %pack_rows.1 = (bf16[192,2176]{1,0:T(8,128)(2,1)}, bf16[96,192]{1,0:T(8,128)(2,1)}) custom-call(s32[24]{0:T(128)} %bitcast.8, s32[24]{0:T(128)} %slot_ref.1, bf16[96,2048]{1,0:T(8,128)(2,1)} %refs_0_), custom_call_target="tpu_custom_call" | custom-call | flops 75497472 | bytes 1179648 | tf_op jit(solution)/shard_map/pack_rows/pallas_call | solution.py:69
  3.0 4.6 %all-to-all-start = ((bf16[8,24,2176]{2,1,0:T(8,128)(2,1)}), bf16[8,24,2176]{2,1,0:T(8,128)(2,1)S(1)}, u32[]{:S(2)}, u32[]{:S(2)}) async-start(bf16[8,24,2176]{2,1,0:T(8,128)(2,1)} %bitcast.7), calls=%async_computation | async-start | bytes 1671168 | tf_op jit(solution)/shard_map/all_to_all | solution.py:451
  7.6 0.0 copy-start
  7.6 0.2 collective-permute-start.1
  7.7 2.3 %collective-permute-start = (bf16[96,2048]{1,0:T(8,128)(2,1)}, bf16[96,2048]{1,0:T(8,128)(2,1)}, u32[]{:S(2)}, u32[]{:S(2)}) collective-permute-start(bf16[96,2048]{1,0:T(8,128)(2,1)} %refs_0_), channel_id=1, source_target_pairs={{0,2},{1,3},{2,0},{3,1},{4,6},{5,7},{6,4},{7,5},{8,10},{9,11},{10,... | collective-permute-start | bytes 1179656 | tf_op jit(solution)/shard_map/ppermute | solution.py:418
  10.1 8.5 %cached_attention.1 = (f32[96,2048]{1,0:T(8,128)}, f32[96,128]{1,0:T(8,128)S(1)}, bf16[4,2048,128]{2,1,0:T(8,128)(2,1)S(1)}) custom-call(s32[96]{0:T(128)} %length_hbm.1, bf16[96,2048]{1,0:T(8,128)(2,1)} %query_ref.1, bf16[96,128,256]{2,1,0:T(8,128)(2,1)} %key_hbm.1, bf16[96,128,256]{2,1,0:T(8,128)(2,1)} %value_hbm.1, bf16[4,2048,128]{2,1,0:T(8,128)(2,1)} %shrink_hbm.1), custom_call_target="tpu_custom_call" | custom-call | flops 201326592 | bytes 13762560 | tf_op jit(solution)/shard_map/cached_attention/pallas_call | solution.py:246
  18.5 0.7 %all-to-all-done = bf16[8,24,2176]{2,1,0:T(8,128)(2,1)S(1)} async-done(((bf16[8,24,2176]{2,1,0:T(8,128)(2,1)}), bf16[8,24,2176]{2,1,0:T(8,128)(2,1)S(1)}, u32[]{:S(2)}, u32[]{:S(2)}) %all-to-all-start) | async-done | bytes 835616 | tf_op jit(solution)/shard_map/all_to_all | solution.py:451
  19.2 1.0 %shrink_rows.1 = (f32[192,128]{1,0:T(8,128)S(1)}, bf16[192,128]{1,0:T(8,128)(2,1)S(1)}, bf16[192,128]{1,0:T(8,128)(2,1)S(1)}, bf16[4,2,64,256]{3,2,1,0:T(8,128)(2,1)S(1)}) custom-call(bf16[192,2176]{1,0:T(8,128)(2,1)S(1)} %bitcast.5, bf16[4,2048,128]{2,1,0:T(8,128)(2,1)S(1)} %get-tuple-element.29.shrink_ref, bf16[4,2,64,256]{3,2,1,0:T(8,128)(2,1)} %up_hbm.1), custom_call_target="tpu_custom_call" | custom-call | flops 402653184 | bytes 2883584 | tf_op jit(solution)/shard_map/shrink_rows/pallas_call | solution.py:101
  20.2 0.7 %collective-permute-start.2 = (bf16[192,128]{1,0:T(8,128)(2,1)S(1)}, bf16[192,128]{1,0:T(8,128)(2,1)S(1)}, u32[]{:S(2)}, u32[]{:S(2)}) collective-permute-start(bf16[192,128]{1,0:T(8,128)(2,1)S(1)} %get-tuple-element.31), channel_id=1, source_target_pairs={{0,1},{1,0},{2,3},{3,2},{4,5},{5,4},{6,7},{7,6},{8,9},{9,8},{10,11... | collective-permute-start | bytes 147464 | tf_op jit(solution)/shard_map/ppermute | solution.py:418
  20.9 6.9 %collective-permute-done.2 = bf16[192,128]{1,0:T(8,128)(2,1)S(1)} collective-permute-done((bf16[192,128]{1,0:T(8,128)(2,1)S(1)}, bf16[192,128]{1,0:T(8,128)(2,1)S(1)}, u32[]{:S(2)}, u32[]{:S(2)}) %collective-permute-start.2) | collective-permute-done | bytes 49184 | tf_op jit(solution)/shard_map/ppermute | solution.py:418
  27.8 0.0 collective-permute-done.1.refs_1_
  27.8 1.1 %collective-permute-start.3 = (bf16[192,128]{1,0:T(8,128)(2,1)S(1)}, bf16[192,128]{1,0:T(8,128)(2,1)S(1)}, u32[]{:S(2)}, u32[]{:S(2)}) collective-permute-start(bf16[192,128]{1,0:T(8,128)(2,1)S(1)} %convert_element_type.7), channel_id=1, source_target_pairs={{0,2},{1,3},{2,0},{3,1},{4,6},{5,7},{6,4},{7,5},{8,10},{9,11},{10,... | collective-permute-start | bytes 147464 | tf_op jit(solution)/shard_map/ppermute | solution.py:418
  28.9 0.0 collective-permute-done.refs_2_
  28.9 2.8 %collective-permute-done.3.refs_1_ = bf16[192,128]{1,0:T(8,128)(2,1)S(1)} collective-permute-done((bf16[192,128]{1,0:T(8,128)(2,1)S(1)}, bf16[192,128]{1,0:T(8,128)(2,1)S(1)}, u32[]{:S(2)}, u32[]{:S(2)}) %collective-permute-start.3) | collective-permute-done | bytes 49184 | tf_op jit(solution)/shard_map/ppermute | solution.py:418
  31.7 2.0 %collective-permute-start.5 = (bf16[96,2048]{1,0:T(8,128)(2,1)}, bf16[96,2048]{1,0:T(8,128)(2,1)S(1)}, u32[]{:S(2)}, u32[]{:S(2)}) collective-permute-start(bf16[96,2048]{1,0:T(8,128)(2,1)} %collective-permute-done.refs_2_), channel_id=1, source_target_pairs={{1,0},{2,3},{5,4},{6,7},{9,8},{10,11},{13,12},{14,15},{17,16},{18,... | collective-permute-start | bytes 1179656 | tf_op jit(solution)/shard_map/ppermute | solution.py:467
  33.7 0.0 copy-done
  33.8 3.1 %collective-permute-start.4 = (bf16[96,2048]{1,0:T(8,128)(2,1)S(1)}, bf16[96,2048]{1,0:T(8,128)(2,1)S(1)}, u32[]{:S(2)}, u32[]{:S(2)}) collective-permute-start(bf16[96,2048]{1,0:T(8,128)(2,1)S(1)} %copy-done), channel_id=1, source_target_pairs={{1,2},{2,1},{5,6},{6,5},{9,10},{10,9},{13,14},{14,13},{17,18},{18,... | collective-permute-start | bytes 1179656 | tf_op jit(solution)/shard_map/ppermute | solution.py:468
  36.9 1.0 %expand_rows.1 = bf16[192,512]{1,0:T(8,128)(2,1)} custom-call(f32[192,128]{1,0:T(8,128)S(1)} %convert_add_fusion.refs_0_, bf16[192,128]{1,0:T(8,128)(2,1)S(1)} %collective-permute-done.3.refs_1_, bf16[192,128]{1,0:T(8,128)(2,1)S(1)} %get-tuple-element.37.refs_2_, bf16[4,2,64,256]{3,2,1,0:T(8,128)(2,1)S(1)} %get-tuple-element.38.refs_3_), custom_call_target="tpu_custom_call" | custom-call | flops 50331648 | bytes 458752 | tf_op jit(solution)/shard_map/expand_rows/pallas_call | solution.py:137
  37.9 7.1 %all-to-all-start.1 = ((bf16[8,24,512]{2,1,0:T(8,128)(2,1)}), bf16[8,24,512]{2,1,0:T(8,128)(2,1)S(1)}, u32[]{:S(2)}, u32[]{:S(2)}) async-start(bf16[8,24,512]{2,1,0:T(8,128)(2,1)} %bitcast.3), calls=%async_computation.1 | async-start | bytes 393216 | tf_op jit(solution)/shard_map/all_to_all | solution.py:451
  45.0 0.0 copy-start.1
  45.0 0.0 copy-start.2
  45.0 4.6 %base_products.1 = (f32[96,512]{1,0:T(8,128)S(1)}, bf16[2048,256]{1,0:T(8,128)(2,1)S(1)}, bf16[2048,256]{1,0:T(8,128)(2,1)S(1)}) custom-call(bf16[96,2048]{1,0:T(8,128)(2,1)S(1)} %copy-done, bf16[96,2048]{1,0:T(8,128)(2,1)} %collective-permute-done.1.refs_1_, bf16[96,2048]{1,0:T(8,128)(2,1)} %collective-permute-done.refs_2_, bf16[8192,256]{1,0:T(8,128)(2,1)} %refs_3_.1, ...), custom_call_target="tpu_custom_call" | custom-call | flops 603979776 | bytes 7471104 | tf_op jit(solution)/shard_map/base_products/pallas_call | solution.py:309
  49.6 0.0 collective-permute-done.5.refs_1_
  49.7 0.0 collective-permute-done.4.refs_0_
  49.7 0.7 %last_product.1.base_ref = f32[96,512]{1,0:T(8,128)S(1)} custom-call(bf16[96,2048]{1,0:T(8,128)(2,1)S(1)} %collective-permute-done.4.refs_0_, bf16[96,2048]{1,0:T(8,128)(2,1)S(1)} %collective-permute-done.5.refs_1_, bf16[2048,256]{1,0:T(8,128)(2,1)S(1)} %get-tuple-element.43.refs_2_, bf16[2048,256]{1,0:T(8,128)(2,1)S(1)} %get-tuple-element.44.refs_3_, ...), custom_call_target="tpu_custom_call" | custom-call | flops 201326592 | bytes 2097152 | tf_op jit(solution)/shard_map/last_product/pallas_call | solution.py:345
  50.4 0.0 all-to-all-done.1
  50.4 0.0 copy-done.1
  50.4 0.0 copy-done.2
  50.4 2.8 %finish_rows.1 = (bf16[96,256]{1,0:T(8,128)(2,1)}, bf16[96,256]{1,0:T(8,128)(2,1)}, bf16[96,2048]{1,0:T(8,128)(2,1)}) custom-call(f32[96,512]{1,0:T(8,128)S(1)} %last_product.1.base_ref, bf16[192,512]{1,0:T(8,128)(2,1)S(1)} %bitcast.6, bf16[96,192]{1,0:T(8,128)(2,1)S(1)} %copy-done.2, bf16[96,2048]{1,0:T(8,128)(2,1)S(1)} %copy-done.1, ...), custom_call_target="tpu_custom_call" | custom-call | flops 786432 | bytes 1966080 | tf_op jit(solution)/shard_map/finish_rows/pallas_call | solution.py:397
  (2 shorter events, 0.0 us)
Async XLA Ops:
  3.0 16.2 %all-to-all-start = ((bf16[8,24,2176]{2,1,0:T(8,128)(2,1)}), bf16[8,24,2176]{2,1,0:T(8,128)(2,1)S(1)}, u32[]{:S(2)}, u32[]{:S(2)}) async-start(bf16[8,24,2176]{2,1,0:T(8,128)(2,1)} %bitcast.7), calls=%async_computation | async-start | bytes 1671168 | tf_op jit(solution)/shard_map/all_to_all | solution.py:451
  7.6 26.2 %copy-start = (bf16[96,2048]{1,0:T(8,128)(2,1)S(1)}, bf16[96,2048]{1,0:T(8,128)(2,1)}, u32[]{:S(2)}) copy-start(bf16[96,2048]{1,0:T(8,128)(2,1)} %refs_0_) | copy-start | bytes 1179652
  7.6 20.2 %collective-permute-start.1 = (bf16[96,2048]{1,0:T(8,128)(2,1)}, bf16[96,2048]{1,0:T(8,128)(2,1)}, u32[]{:S(2)}, u32[]{:S(2)}) collective-permute-start(bf16[96,2048]{1,0:T(8,128)(2,1)} %refs_0_), channel_id=1, source_target_pairs={{0,1},{1,0},{2,3},{3,2},{4,5},{5,4},{6,7},{7,6},{8,9},{9,8},{10,11... | collective-permute-start | bytes 1179656 | tf_op jit(solution)/shard_map/ppermute | solution.py:418
  7.7 21.1 %collective-permute-start = (bf16[96,2048]{1,0:T(8,128)(2,1)}, bf16[96,2048]{1,0:T(8,128)(2,1)}, u32[]{:S(2)}, u32[]{:S(2)}) collective-permute-start(bf16[96,2048]{1,0:T(8,128)(2,1)} %refs_0_), channel_id=1, source_target_pairs={{0,2},{1,3},{2,0},{3,1},{4,6},{5,7},{6,4},{7,5},{8,10},{9,11},{10,... | collective-permute-start | bytes 1179656 | tf_op jit(solution)/shard_map/ppermute | solution.py:418
  20.2 7.5 %collective-permute-start.2 = (bf16[192,128]{1,0:T(8,128)(2,1)S(1)}, bf16[192,128]{1,0:T(8,128)(2,1)S(1)}, u32[]{:S(2)}, u32[]{:S(2)}) collective-permute-start(bf16[192,128]{1,0:T(8,128)(2,1)S(1)} %get-tuple-element.31), channel_id=1, source_target_pairs={{0,1},{1,0},{2,3},{3,2},{4,5},{5,4},{6,7},{7,6},{8,9},{9,8},{10,11... | collective-permute-start | bytes 147464 | tf_op jit(solution)/shard_map/ppermute | solution.py:418
  27.8 3.9 %collective-permute-start.3 = (bf16[192,128]{1,0:T(8,128)(2,1)S(1)}, bf16[192,128]{1,0:T(8,128)(2,1)S(1)}, u32[]{:S(2)}, u32[]{:S(2)}) collective-permute-start(bf16[192,128]{1,0:T(8,128)(2,1)S(1)} %convert_element_type.7), channel_id=1, source_target_pairs={{0,2},{1,3},{2,0},{3,1},{4,6},{5,7},{6,4},{7,5},{8,10},{9,11},{10,... | collective-permute-start | bytes 147464 | tf_op jit(solution)/shard_map/ppermute | solution.py:418
  31.7 17.9 %collective-permute-start.5 = (bf16[96,2048]{1,0:T(8,128)(2,1)}, bf16[96,2048]{1,0:T(8,128)(2,1)S(1)}, u32[]{:S(2)}, u32[]{:S(2)}) collective-permute-start(bf16[96,2048]{1,0:T(8,128)(2,1)} %collective-permute-done.refs_2_), channel_id=1, source_target_pairs={{1,0},{2,3},{5,4},{6,7},{9,8},{10,11},{13,12},{14,15},{17,16},{18,... | collective-permute-start | bytes 1179656 | tf_op jit(solution)/shard_map/ppermute | solution.py:467
  33.8 15.9 %collective-permute-start.4 = (bf16[96,2048]{1,0:T(8,128)(2,1)S(1)}, bf16[96,2048]{1,0:T(8,128)(2,1)S(1)}, u32[]{:S(2)}, u32[]{:S(2)}) collective-permute-start(bf16[96,2048]{1,0:T(8,128)(2,1)S(1)} %copy-done), channel_id=1, source_target_pairs={{1,2},{2,1},{5,6},{6,5},{9,10},{10,9},{13,14},{14,13},{17,18},{18,... | collective-permute-start | bytes 1179656 | tf_op jit(solution)/shard_map/ppermute | solution.py:468
  37.9 12.5 %all-to-all-start.1 = ((bf16[8,24,512]{2,1,0:T(8,128)(2,1)}), bf16[8,24,512]{2,1,0:T(8,128)(2,1)S(1)}, u32[]{:S(2)}, u32[]{:S(2)}) async-start(bf16[8,24,512]{2,1,0:T(8,128)(2,1)} %bitcast.3), calls=%async_computation.1 | async-start | bytes 393216 | tf_op jit(solution)/shard_map/all_to_all | solution.py:451
  45.0 5.4 %copy-start.1 = (bf16[96,2048]{1,0:T(8,128)(2,1)S(1)}, bf16[96,2048]{1,0:T(8,128)(2,1)}, u32[]{:S(2)}) copy-start(bf16[96,2048]{1,0:T(8,128)(2,1)} %query_ref.1) | copy-start | bytes 1179652
  45.0 5.4 %copy-start.2 = (bf16[96,192]{1,0:T(8,128)(2,1)S(1)}, bf16[96,192]{1,0:T(8,128)(2,1)}, u32[]{:S(2)}) copy-start(bf16[96,192]{1,0:T(8,128)(2,1)} %get-tuple-element.46.pick_ref) | copy-start | bytes 110596

commit v4 on v3

--- a/solution.py
+++ b/solution.py
@@ -79,10 +79,8 @@
     )(block_owner[:, 0], block_slot, hidden)
 
 
-def shrink_kernel(rows_ref, shrink_ref, up_hbm, out_ref, sent_ref, flag_ref, up_ref, sem):
+def shrink_kernel(rows_ref, shrink_ref, out_ref, sent_ref, flag_ref):
     pool, width, rank = shrink_ref.shape
-    copy = pltpu.make_async_copy(up_hbm, up_ref, sem)
-    copy.start()
     rows = rows_ref[:, :width]
     flag_ref[...] = rows_ref[:, width:]
     total = jnp.zeros(out_ref.shape, jnp.float32)
@@ -91,43 +89,39 @@
         total += part * rows_ref[:, width + a : width + a + 1].astype(jnp.float32)
     out_ref[...] = total
     sent_ref[...] = total.astype(jnp.bfloat16)
-    copy.wait()
-
-
-def shrink(arrived, weights, up):
+
+
+def shrink(arrived, weights):
     places = arrived.shape[0]
     pool, width, rank = weights.shape
-    inside, outside = pl.BlockSpec(memory_space=pltpu.VMEM), pl.BlockSpec(memory_space=pltpu.HBM)
     return pl.pallas_call(
         shrink_kernel,
         name="shrink_rows",
-        in_specs=[inside, inside, outside],
-        out_specs=[inside] * 4,
         out_shape=(
             jax.ShapeDtypeStruct((places, rank), jnp.float32),
             jax.ShapeDtypeStruct((places, rank), jnp.bfloat16),
             jax.ShapeDtypeStruct((places, LANES), jnp.bfloat16),
-            jax.ShapeDtypeStruct(up.shape, up.dtype),
         ),
-        scratch_shapes=[pltpu.SemaphoreType.DMA],
         compiler_params=params(8),
         cost_estimate=cost(2 * places * width * rank * pool, 2 * (places * width + weights.size)),
-    )(arrived, weights, pinned(up))
+    )(arrived, weights)
 
 
 def expand_kernel(count, *refs):
-    parts, flag_ref, up_ref, out_ref = refs[:count], refs[count], refs[count + 1], refs[count + 2]
+    parts, flag_ref, up_ref, out_ref = refs[:count], *refs[count:]
     pool, halves, rank, width = up_ref.shape
     total = parts[0][...].astype(jnp.float32)
     for part in parts[1:]:
         total += part[...].astype(jnp.float32)
     shrunk = total.astype(jnp.bfloat16)
     mine = [shrunk * flag_ref[:, a : a + 1] for a in range(pool)]
+    side = iota(shrunk.shape, 1) // rank
+    wide = [
+        jnp.concatenate([jnp.where(side == half, x, jnp.zeros_like(x)) for x in mine], axis=1) for half in range(halves)
+    ]
     table = up_ref[...].reshape(pool * halves * rank, width)
-    side = iota(shrunk.shape, 1) // rank
     for half in range(halves):
-        wide = jnp.concatenate([jnp.where(side == half, x, jnp.zeros_like(x)) for x in mine], axis=1)
-        product = jnp.dot(wide, table, preferred_element_type=jnp.float32)
+        product = jnp.dot(wide[half], table, preferred_element_type=jnp.float32)
         out_ref[:, half * width : (half + 1) * width] = (adapter_scale * product).astype(jnp.bfloat16)
 
 
@@ -273,53 +267,93 @@
     return place ^ p if parts == 4 else lax.rem(place + parts - p, parts)
 
 
+def own_kernel(total, piece_ref, key_hbm, value_hbm, up_hbm, out_ref, up_ref, keys, values, sems):
+    shard, width = keys.shape
+    rows = pl.ds(pl.multiple_of(owner_of(lax.axis_index("tp"), 0, total) * shard, shard), shard)
+    copies = [
+        pltpu.make_async_copy(key_hbm.at[rows], keys, sems.at[0]),
+        pltpu.make_async_copy(value_hbm.at[rows], values, sems.at[1]),
+        pltpu.make_async_copy(up_hbm, up_ref, sems.at[2]),
+    ]
+    for copy in copies:
+        copy.start()
+    for half, weights in enumerate((keys, values)):
+        copies[half].wait()
+        product = jnp.dot(piece_ref[...], weights[...], preferred_element_type=jnp.float32)
+        out_ref[:, half * width : (half + 1) * width] = product
+    copies[2].wait()
+
+
+def own_product(piece, total, key_matrix, value_matrix, up):
+    rows, shard = piece.shape
+    width = key_matrix.shape[1]
+    inside, outside = pl.BlockSpec(memory_space=pltpu.VMEM), pl.BlockSpec(memory_space=pltpu.HBM)
+    return pl.pallas_call(
+        functools.partial(own_kernel, total),
+        name="own_product",
+        in_specs=[inside, outside, outside, outside],
+        out_specs=[inside, inside],
+        out_shape=[jax.ShapeDtypeStruct((rows, 2 * width), jnp.float32), jax.ShapeDtypeStruct(up.shape, up.dtype)],
+        scratch_shapes=[pltpu.VMEM((shard, width), key_matrix.dtype)] * 2 + [pltpu.SemaphoreType.DMA((3,))],
+        compiler_params=params(8),
+        cost_estimate=cost(4 * rows * shard * width, 4 * shard * width),
+    )(piece, pinned(key_matrix), pinned(value_matrix), pinned(up))
+
+
 def base_kernel(total, *refs):
-    count = total - 1
-    pieces, key_hbm, value_hbm, out_ref, last_keys, last_values, keys, values, sems = refs[:count], *refs[count:]
+    count = total - 2
+    pieces, refs = refs[:count], refs[count:]
+    so_far, key_hbm, value_hbm, mean_hbm, out_ref, last_keys, last_values, mean_ref, keys, values, sems = refs
     shard, width = last_keys.shape
     place = lax.axis_index("tp")
 
     def copies(p):
-        rows = pl.ds(pl.multiple_of(owner_of(place, p, total) * shard, shard), shard)
+        rows = pl.ds(pl.multiple_of(owner_of(place, p + 1, total) * shard, shard), shard)
         key_to, value_to = (last_keys, last_values) if p == count else (keys.at[p], values.at[p])
-        return (
-            pltpu.make_async_copy(key_hbm.at[rows], key_to, sems.at[0, p]),
-            pltpu.make_async_copy(value_hbm.at[rows], value_to, sems.at[1, p]),
-        )
-
-    for p in range(total):
-        for copy in copies(p):
-            copy.start()
+        key_copy = pltpu.make_async_copy(key_hbm.at[rows], key_to, sems.at[0, p]) if p > 0 else None
+        return key_copy, pltpu.make_async_copy(value_hbm.at[rows], value_to, sems.at[1, p])
+
+    everything = [copy for p in range(count + 1) for copy in copies(p) if copy is not None]
+    everything.append(pltpu.make_async_copy(mean_hbm, mean_ref, sems.at[0, 0]))
+    for copy in everything:
+        copy.start()
+    out_ref[...] = so_far[...]
     for p in range(count):
         for half, (copy, weights) in enumerate(zip(copies(p), (keys, values))):
+            if copy is None:
+                continue
             here = slice(half * width, (half + 1) * width)
             copy.wait()
-            product = jnp.dot(pieces[p][...], weights[p], preferred_element_type=jnp.float32)
-            out_ref[:, here] = product if p == 0 else out_ref[:, here] + product
-    for copy in copies(count):
+            out_ref[:, here] += jnp.dot(pieces[p][...], weights[p], preferred_element_type=jnp.float32)
+    for copy in everything[-3:]:
         copy.wait()
 
 
-def base_products(pieces, key_matrix, value_matrix):
+def base_products(pieces, so_far, key_matrix, value_matrix, mean):
     rows, shard = pieces[0].shape
     width = key_matrix.shape[1]
     count = len(pieces)
     inside, outside = pl.BlockSpec(memory_space=pltpu.VMEM), pl.BlockSpec(memory_space=pltpu.HBM)
     last = jax.ShapeDtypeStruct((shard, width), key_matrix.dtype)
     return pl.pallas_call(
-        functools.partial(base_kernel, count + 1),
+        functools.partial(base_kernel, count + 2),
         name="base_products",
-        in_specs=[inside] * count + [outside, outside],
-        out_specs=[inside] * 3,
+        in_specs=[inside] * (count + 1) + [outside] * 3,
+        out_specs=[inside] * 4,
         scratch_shapes=[
             pltpu.VMEM((count, shard, width), key_matrix.dtype),
             pltpu.VMEM((count, shard, width), key_matrix.dtype),
             pltpu.SemaphoreType.DMA((2, count + 1)),
         ],
-        out_shape=[jax.ShapeDtypeStruct((rows, 2 * width), jnp.float32), last, last],
+        out_shape=[
+            jax.ShapeDtypeStruct((rows, 2 * width), jnp.float32),
+            last,
+            last,
+            jax.ShapeDtypeStruct(mean.shape, mean.dtype),
+        ],
         compiler_params=params(16),
         cost_estimate=cost(4 * count * rows * shard * width, count * (4 * shard * width + 2 * rows * shard)),
-    )(*pieces, pinned(key_matrix), pinned(value_matrix))
+    )(*pieces, so_far, pinned(key_matrix), pinned(value_matrix), pinned(mean))
 
 
 def last_kernel(count, total, *refs):
@@ -337,7 +371,8 @@
 
     for half, weights in enumerate((keys, values)):
         here = slice(half * width, (half + 1) * width)
-        out_ref[:, here] = base_ref[:, here] + jnp.dot(piece_ref[...], weights[...], preferred_element_type=jnp.float32)
+        product = jnp.dot(piece_ref[...], weights[...], preferred_element_type=jnp.float32)
+        out_ref[:, here] = base_ref[:, here] + product
 
 
 def last_product(late, total, keys, values, base):
@@ -354,16 +389,14 @@
     )(*late, keys, values, base)
 
 
-def finish_kernel(base_ref, back_ref, pick_ref, query_ref, lse_ref, mean_hbm, *refs):
-    new_key_ref, new_value_ref, context_hbm, mean_ref, context_ref, sems = refs
+def finish_kernel(base_ref, back_ref, pick_ref, query_ref, lse_ref, mean_ref, *refs):
+    new_key_ref, new_value_ref, context_hbm, context_ref, sems = refs
     rows, wide = query_ref.shape
     width = new_key_ref.shape[1]
     heads = wide // HEAD_SIZE
     groups = width // HEAD_SIZE
     each = heads // groups
     inverse_root = HEAD_SIZE ** (-0.5)
-    mean_copy = pltpu.make_async_copy(mean_hbm, mean_ref, sems.at[groups])
-    mean_copy.start()
     delta = jnp.dot(pick_ref[...], back_ref[...], preferred_element_type=jnp.float32)
     base = (base_ref[...] + delta).astype(jnp.bfloat16)
     new_key_ref[...] = base[:, :width]
@@ -377,7 +410,6 @@
         score = jnp.sum(query * keys[:, k * HEAD_SIZE : (k + 1) * HEAD_SIZE], axis=1, keepdims=True)
         own = jnp.where(column == h, score * inverse_root, own)
     share = 1.0 / (1.0 + jnp.exp(lse_ref[...] - own))
-    mean_copy.wait()
     for k in range(groups):
         for h in range(k * each, (k + 1) * each):
             mean = mean_ref[:, h * HEAD_SIZE : (h + 1) * HEAD_SIZE]
@@ -397,7 +429,7 @@
     return pl.pallas_call(
         finish_kernel,
         name="finish_rows",
-        in_specs=[inside] * 5 + [outside],
+        in_specs=[inside] * 6,
         out_specs=[inside, inside, outside],
         out_shape=(
             jax.ShapeDtypeStruct((rows, width), jnp.bfloat16),
@@ -405,13 +437,12 @@
             jax.ShapeDtypeStruct((rows, wide), jnp.bfloat16),
         ),
         scratch_shapes=[
-            pltpu.VMEM(mean.shape, mean.dtype),
             pltpu.VMEM((rows, wide), jnp.bfloat16),
-            pltpu.SemaphoreType.DMA((width // HEAD_SIZE + 1,)),
+            pltpu.SemaphoreType.DMA((width // HEAD_SIZE,)),
         ],
         compiler_params=params(8),
         cost_estimate=cost(4 * rows * wide, 10 * rows * wide),
-    )(base, back, pick, queries, lse, pinned(mean))
+    )(base, back, pick, queries, lse, mean)
 
 
 def swap(x, mask, size):
@@ -458,23 +489,31 @@
         two = swap(hidden_in, 2, parts)
     mean, lse, shrink_here = cached_attention(cache_lengths, queries, cache_keys, cached_value_rows, shrink_weights)
     arrived, lse = lax.optimization_barrier((arrived, lse))
-    partial_rows, sent, flags, up_here = shrink(arrived, shrink_here, pooled_up_weights)
+    partial_rows, sent, flags = shrink(arrived, shrink_here)
+    matrices = (base_key_matrix, base_value_matrix)
+    partial_rows, own_piece = lax.optimization_barrier((partial_rows, hidden_in))
+    base, up_here = own_product(own_piece, parts, *matrices, pooled_up_weights)
     if parts == 4:
-        paired = partial_rows + swap(sent, 1, parts).astype(jnp.float32)
-        one, paired = lax.optimization_barrier((one, paired))
+        received = swap(sent, 1, parts)
+        received, base = lax.optimization_barrier((received, base))
+        paired = partial_rows + received.astype(jnp.float32)
         sums = [paired, swap(paired.astype(jnp.bfloat16), 2, parts)]
-        two, again, *sums = lax.optimization_barrier((two, hidden_in, *sums))
+        one, two, again, _ = lax.optimization_barrier((one, two, hidden_in, paired))
         outer = lax.ppermute(two, "tp", [(1, 0), (2, 3)])
         inner = lax.ppermute(again, "tp", [(1, 2), (2, 1)])
-        early, late = [hidden_in, one, two], [inner, outer]
+        between, late = [one, two], [inner, outer]
     else:
         sums = [partial_rows] + others(sent, parts)
-        pieces = [hidden_in] + others(hidden_in, parts)
-        early, late = pieces[:-1], pieces[-1:]
+        pieces = others(hidden_in, parts)
+        between, late = pieces[:-1], pieces[-1:]
     deltas = expand(sums, flags, up_here)
     back = all_to_all(deltas)
-    deltas, *early = lax.optimization_barrier((deltas, *early))
-    base, *last = base_products(early, base_key_matrix, base_value_matrix)
+    deltas, *between = lax.optimization_barrier((deltas, *between))
+    base, *last, mean = base_products(between, base, *matrices, mean)
+    owner = owner_of(lax.axis_index("tp"), 1, parts)
+    key_rows = lax.dynamic_slice_in_dim(base_key_matrix, owner * shard_width, shard_width, 0)
+    more = jnp.dot(between[0], key_rows, preferred_element_type=jnp.float32)
+    base = base + jnp.concatenate([more, jnp.zeros_like(more)], axis=1)
     base = last_product(late, parts, *last, base)
     return finish(base, back, pick, queries, lse, mean)
 

time: 53.6 us -> 50.1 us (0.935)
  waiting for transfers between devices: 10.4 us -> 5.54 us
  matrix products: 0 us -> 1.7 us
  starting transfers between devices: 21 us -> 20 us
  Pallas kernels: 21 us -> 21.6 us
    ppermute x4, waiting for transfers between devices: 9.7 us -> 4.82 us  [swap(): return lax.ppermute(x, 'tp', [(i, i ^ mask) for i in range(size)])]
    dot_general x0 -> x1, matrix products: none -> 1.7 us  [shards(): more = jnp.dot(between[0], key_rows, preferred_element_type=jnp.float32)]
    ppermute x1, starting transfers between devices: 2.02 us -> 3.37 us  [shards(): outer = lax.ppermute(two, 'tp', [(1, 0), (2, 3)])]
    all_to_all x2, starting transfers between devices: 11.7 us -> 10.3 us  [all_to_all(): lax.all_to_all(x, 'rep', split_axis=0, concat_axis=0, tiled=True)]
    ppermute x1, starting transfers between devices: 3.09 us -> 2.08 us  [shards(): inner = lax.ppermute(again, 'tp', [(1, 2), (2, 1)])]
    pallas_call x3 -> x4, Pallas kernels: 8.41 us -> 9.07 us  [the longest x1 3.93 us: base_products(): pl.pallas_call(functools.partial(base_kernel, count + 2), name='base_prod...]
  transfers between devices with their start and end apart: 8 -> 8, of which waited for: 3 -> 2; matrix products, arithmetic and copies ran while one was open for 0% -> 4% of each run, Pallas kernels for 30% -> 34%
where the time goes in v4:
time: 50.1 us; the launch traced here: 49.7 us
  Pallas kernels  21.6 us (43%)
  starting transfers between devices  20 us (40%)
  waiting for transfers between devices  5.54 us (11%)
  matrix products  1.7 us (3%)
  between operations  0.77 us (2%)
    all_to_all x2, starting transfers between devices, all_to_all(): lax.all_to_all(x, 'rep', split_axis=0, concat_axis=0, tiled=True)  10.3 us
    pallas_call x1, Pallas kernels, cached_attention(): pl.pallas_call(functools.partial(cached_kernel, heads, group), name='cach...  8.45 us
    ppermute x4, waiting for transfers between devices, swap(): return lax.ppermute(x, 'tp', [(i, i ^ mask) for i in range(size)])  4.82 us
    ppermute x4, starting transfers between devices, swap(): return lax.ppermute(x, 'tp', [(i, i ^ mask) for i in range(size)])  4.23 us
    pallas_call x1, Pallas kernels, base_products(): pl.pallas_call(functools.partial(base_kernel, count + 2), name='base_prod...  3.93 us
    ppermute x1, starting transfers between devices, shards(): outer = lax.ppermute(two, 'tp', [(1, 0), (2, 3)])  3.37 us
    pallas_call x1, Pallas kernels, pack(): pl.pallas_call(functools.partial(pack_kernel, capacity), name='pack_rows'...  2.37 us
    pallas_call x1, Pallas kernels, finish(): pl.pallas_call(finish_kernel, name='finish_rows', in_specs=[inside] * 6,...  2.1 us
  transfers between devices with their start and end apart: 8, of which 2 were waited for; matrix products, arithmetic and copies ran while one was open for 4% of the time, Pallas kernels for 34%

profile of v4, /device:TPU:11, one launch (start us, length us, event | category | flops | bytes accessed | tf_op | source)
XLA Modules:
  0.0 49.7 jit_solution(15727554004025887973)
XLA Ops:
  0.6 2.4 %pack_rows.1 = (bf16[192,2176]{1,0:T(8,128)(2,1)}, bf16[96,192]{1,0:T(8,128)(2,1)}) custom-call(s32[24]{0:T(128)} %bitcast.9, s32[24]{0:T(128)} %slot_ref.1, bf16[96,2048]{1,0:T(8,128)(2,1)} %piece_ref), custom_call_target="tpu_custom_call" | custom-call | flops 75497472 | bytes 1179648 | tf_op jit(solution)/shard_map/pack_rows/pallas_call | solution.py:69
  3.0 4.6 %all-to-all-start = ((bf16[8,24,2176]{2,1,0:T(8,128)(2,1)}), bf16[8,24,2176]{2,1,0:T(8,128)(2,1)S(1)}, u32[]{:S(2)}, u32[]{:S(2)}) async-start(bf16[8,24,2176]{2,1,0:T(8,128)(2,1)} %bitcast.8), calls=%async_computation | async-start | bytes 1671168 | tf_op jit(solution)/shard_map/all_to_all | solution.py:482
  7.6 0.0 copy-start
  7.6 0.2 collective-permute-start
  7.7 2.3 %collective-permute-start.1 = (bf16[96,2048]{1,0:T(8,128)(2,1)}, bf16[96,2048]{1,0:T(8,128)(2,1)}, u32[]{:S(2)}, u32[]{:S(2)}) collective-permute-start(bf16[96,2048]{1,0:T(8,128)(2,1)} %piece_ref), channel_id=1, source_target_pairs={{0,2},{1,3},{2,0},{3,1},{4,6},{5,7},{6,4},{7,5},{8,10},{9,11},{10,... | collective-permute-start | bytes 1179656 | tf_op jit(solution)/shard_map/ppermute | solution.py:449
  10.0 8.4 %cached_attention.1 = (f32[96,2048]{1,0:T(8,128)}, f32[96,128]{1,0:T(8,128)S(1)}, bf16[4,2048,128]{2,1,0:T(8,128)(2,1)S(1)}) custom-call(s32[96]{0:T(128)} %length_hbm.1, bf16[96,2048]{1,0:T(8,128)(2,1)} %query_ref.1, bf16[96,128,256]{2,1,0:T(8,128)(2,1)} %key_hbm.2, bf16[96,128,256]{2,1,0:T(8,128)(2,1)} %value_hbm.2, bf16[4,2048,128]{2,1,0:T(8,128)(2,1)} %shrink_hbm.1), custom_call_target="tpu_custom_call" | custom-call | flops 201326592 | bytes 13762560 | tf_op jit(solution)/shard_map/cached_attention/pallas_call | solution.py:240
  18.5 0.7 %all-to-all-done = bf16[8,24,2176]{2,1,0:T(8,128)(2,1)S(1)} async-done(((bf16[8,24,2176]{2,1,0:T(8,128)(2,1)}), bf16[8,24,2176]{2,1,0:T(8,128)(2,1)S(1)}, u32[]{:S(2)}, u32[]{:S(2)}) %all-to-all-start) | async-done | bytes 835616 | tf_op jit(solution)/shard_map/all_to_all | solution.py:482
  19.2 1.0 %shrink_rows.1 = (f32[192,128]{1,0:T(8,128)S(1)}, bf16[192,128]{1,0:T(8,128)(2,1)S(1)}, bf16[192,128]{1,0:T(8,128)(2,1)S(1)}) custom-call(bf16[192,2176]{1,0:T(8,128)(2,1)S(1)} %bitcast.6, bf16[4,2048,128]{2,1,0:T(8,128)(2,1)S(1)} %get-tuple-element.31.shrink_ref), custom_call_target="tpu_custom_call" | custom-call | flops 402653184 | bytes 2883584 | tf_op jit(solution)/shard_map/shrink_rows/pallas_call | solution.py:97
  20.2 0.7 %collective-permute-start.2 = (bf16[192,128]{1,0:T(8,128)(2,1)S(1)}, bf16[192,128]{1,0:T(8,128)(2,1)S(1)}, u32[]{:S(2)}, u32[]{:S(2)}) collective-permute-start(bf16[192,128]{1,0:T(8,128)(2,1)S(1)} %get-tuple-element.34), channel_id=1, source_target_pairs={{0,1},{1,0},{2,3},{3,2},{4,5},{5,4},{6,7},{7,6},{8,9},{9,8},{10,11... | collective-permute-start | bytes 147464 | tf_op jit(solution)/shard_map/ppermute | solution.py:449
  20.8 0.0 copy-done
  20.9 2.1 %own_product.1 = (f32[96,512]{1,0:T(8,128)S(1)}, bf16[4,2,64,256]{3,2,1,0:T(8,128)(2,1)S(1)}) custom-call(bf16[96,2048]{1,0:T(8,128)(2,1)S(1)} %copy-done, bf16[8192,256]{1,0:T(8,128)(2,1)} %refs_3_.1, bf16[8192,256]{1,0:T(8,128)(2,1)} %refs_4_.1, bf16[4,2,64,256]{3,2,1,0:T(8,128)(2,1)} %up_hbm.1), custom_call_target="tpu_custom_call" | custom-call | flops 201326592 | bytes 2097152 | tf_op jit(solution)/shard_map/own_product/pallas_call | solution.py:291
  22.9 4.8 %collective-permute-done.2 = bf16[192,128]{1,0:T(8,128)(2,1)S(1)} collective-permute-done((bf16[192,128]{1,0:T(8,128)(2,1)S(1)}, bf16[192,128]{1,0:T(8,128)(2,1)S(1)}, u32[]{:S(2)}, u32[]{:S(2)}) %collective-permute-start.2) | collective-permute-done | bytes 49184 | tf_op jit(solution)/shard_map/ppermute | solution.py:449
  27.8 1.1 %collective-permute-start.5 = (bf16[192,128]{1,0:T(8,128)(2,1)S(1)}, bf16[192,128]{1,0:T(8,128)(2,1)S(1)}, u32[]{:S(2)}, u32[]{:S(2)}) collective-permute-start(bf16[192,128]{1,0:T(8,128)(2,1)S(1)} %get-tuple-element.53), channel_id=1, source_target_pairs={{0,2},{1,3},{2,0},{3,1},{4,6},{5,7},{6,4},{7,5},{8,10},{9,11},{10,... | collective-permute-start | bytes 147464 | tf_op jit(solution)/shard_map/ppermute | solution.py:449
  28.9 0.0 collective-permute-done.refs_0_
  28.9 0.0 collective-permute-done.1.refs_1_
  28.9 3.4 %collective-permute-start.4 = (bf16[96,2048]{1,0:T(8,128)(2,1)}, bf16[96,2048]{1,0:T(8,128)(2,1)S(1)}, u32[]{:S(2)}, u32[]{:S(2)}) collective-permute-start(bf16[96,2048]{1,0:T(8,128)(2,1)} %collective-permute-done.1.refs_1_), channel_id=1, source_target_pairs={{1,0},{2,3},{5,4},{6,7},{9,8},{10,11},{13,12},{14,15},{17,16},{18,... | collective-permute-start | bytes 1179656 | tf_op jit(solution)/shard_map/ppermute | solution.py:502
  32.3 2.1 %collective-permute-start.3 = (bf16[96,2048]{1,0:T(8,128)(2,1)S(1)}, bf16[96,2048]{1,0:T(8,128)(2,1)S(1)}, u32[]{:S(2)}, u32[]{:S(2)}) collective-permute-start(bf16[96,2048]{1,0:T(8,128)(2,1)S(1)} %copy-done), channel_id=1, source_target_pairs={{1,2},{2,1},{5,6},{6,5},{9,10},{10,9},{13,14},{14,13},{17,18},{18,... | collective-permute-start | bytes 1179656 | tf_op jit(solution)/shard_map/ppermute | solution.py:503
  34.3 0.0 collective-permute-done.5.refs_1_
  34.3 1.0 %expand_rows.1 = bf16[192,512]{1,0:T(8,128)(2,1)} custom-call(f32[192,128]{1,0:T(8,128)S(1)} %get-tuple-element.54.refs_0_, bf16[192,128]{1,0:T(8,128)(2,1)S(1)} %collective-permute-done.5.refs_1_, bf16[192,128]{1,0:T(8,128)(2,1)S(1)} %get-tuple-element.40.refs_2_, bf16[4,2,64,256]{3,2,1,0:T(8,128)(2,1)S(1)} %get-tuple-element.41.refs_3_), custom_call_target="tpu_custom_call" | custom-call | flops 50331648 | bytes 458752 | tf_op jit(solution)/shard_map/expand_rows/pallas_call | solution.py:131
  35.4 5.8 %all-to-all-start.1 = ((bf16[8,24,512]{2,1,0:T(8,128)(2,1)}), bf16[8,24,512]{2,1,0:T(8,128)(2,1)S(1)}, u32[]{:S(2)}, u32[]{:S(2)}) async-start(bf16[8,24,512]{2,1,0:T(8,128)(2,1)} %bitcast.3), calls=%async_computation.1 | async-start | bytes 393216 | tf_op jit(solution)/shard_map/all_to_all | solution.py:482
  41.1 3.9 %base_products.1 = (f32[96,512]{1,0:T(8,128)S(1)}, bf16[2048,256]{1,0:T(8,128)(2,1)S(1)}, bf16[2048,256]{1,0:T(8,128)(2,1)S(1)}, f32[96,2048]{1,0:T(8,128)S(1)}) custom-call(bf16[96,2048]{1,0:T(8,128)(2,1)} %collective-permute-done.refs_0_, bf16[96,2048]{1,0:T(8,128)(2,1)} %collective-permute-done.1.refs_1_, f32[96,512]{1,0:T(8,128)S(1)} %get-tuple-element.45.refs_2_, ...), custom_call_target="tpu_custom_call" | custom-call | flops 402653184 | bytes 4980736 | tf_op jit(solution)/shard_map/base_products/pallas_call | solution.py:338
  45.1 0.0 copy-start.1
  45.1 0.0 copy-start.2
  45.1 1.7 %fusion = f32[96,256]{1,0:T(8,128)S(1)} fusion(bf16[96,2048]{1,0:T(8,128)(2,1)} %collective-permute-done.refs_0_, bf16[8192,256]{1,0:T(8,128)(2,1)} %refs_3_.1, s32[]{:T(128)S(6)} %select_n.3), kind=kOutput, calls=%fused_computation | convolution fusion | flops 100663296 | bytes 1540100 | tf_op jit(solution)/shard_map/dot_general | solution.py:515
  46.8 0.0 collective-permute-done.4.refs_1_
  46.8 0.0 collective-permute-done.3.refs_0_
  46.9 0.7 %last_product.1.base_ref = f32[96,512]{1,0:T(8,128)S(1)} custom-call(bf16[96,2048]{1,0:T(8,128)(2,1)S(1)} %collective-permute-done.3.refs_0_, bf16[96,2048]{1,0:T(8,128)(2,1)S(1)} %collective-permute-done.4.refs_1_, bf16[2048,256]{1,0:T(8,128)(2,1)S(1)} %get-tuple-element.47.refs_2_, bf16[2048,256]{1,0:T(8,128)(2,1)S(1)} %get-tuple-element.48.refs_3_, ...), custom_call_target="tpu_custom_call" | custom-call | flops 201326592 | bytes 2097152 | tf_op jit(solution)/shard_map/last_product/pallas_call | solution.py:380
  47.5 0.0 all-to-all-done.1
  47.6 0.0 copy-done.1
  47.6 0.0 copy-done.2
  47.6 2.1 %finish_rows.1 = (bf16[96,256]{1,0:T(8,128)(2,1)}, bf16[96,256]{1,0:T(8,128)(2,1)}, bf16[96,2048]{1,0:T(8,128)(2,1)}) custom-call(f32[96,512]{1,0:T(8,128)S(1)} %last_product.1.base_ref, bf16[192,512]{1,0:T(8,128)(2,1)S(1)} %bitcast.7, bf16[96,192]{1,0:T(8,128)(2,1)S(1)} %copy-done.2, bf16[96,2048]{1,0:T(8,128)(2,1)S(1)} %copy-done.1, ...), custom_call_target="tpu_custom_call" | custom-call | flops 786432 | bytes 1966080 | tf_op jit(solution)/shard_map/finish_rows/pallas_call | solution.py:429
  (2 shorter events, 0.0 us)
Async XLA Ops:
  3.0 16.2 %all-to-all-start = ((bf16[8,24,2176]{2,1,0:T(8,128)(2,1)}), bf16[8,24,2176]{2,1,0:T(8,128)(2,1)S(1)}, u32[]{:S(2)}, u32[]{:S(2)}) async-start(bf16[8,24,2176]{2,1,0:T(8,128)(2,1)} %bitcast.8), calls=%async_computation | async-start | bytes 1671168 | tf_op jit(solution)/shard_map/all_to_all | solution.py:482
  7.6 13.3 %copy-start = (bf16[96,2048]{1,0:T(8,128)(2,1)S(1)}, bf16[96,2048]{1,0:T(8,128)(2,1)}, u32[]{:S(2)}) copy-start(bf16[96,2048]{1,0:T(8,128)(2,1)} %piece_ref) | copy-start | bytes 1179652
  7.6 21.3 %collective-permute-start = (bf16[96,2048]{1,0:T(8,128)(2,1)}, bf16[96,2048]{1,0:T(8,128)(2,1)}, u32[]{:S(2)}, u32[]{:S(2)}) collective-permute-start(bf16[96,2048]{1,0:T(8,128)(2,1)} %piece_ref), channel_id=1, source_target_pairs={{0,1},{1,0},{2,3},{3,2},{4,5},{5,4},{6,7},{7,6},{8,9},{9,8},{10,11... | collective-permute-start | bytes 1179656 | tf_op jit(solution)/shard_map/ppermute | solution.py:449
  7.7 21.1 %collective-permute-start.1 = (bf16[96,2048]{1,0:T(8,128)(2,1)}, bf16[96,2048]{1,0:T(8,128)(2,1)}, u32[]{:S(2)}, u32[]{:S(2)}) collective-permute-start(bf16[96,2048]{1,0:T(8,128)(2,1)} %piece_ref), channel_id=1, source_target_pairs={{0,2},{1,3},{2,0},{3,1},{4,6},{5,7},{6,4},{7,5},{8,10},{9,11},{10,... | collective-permute-start | bytes 1179656 | tf_op jit(solution)/shard_map/ppermute | solution.py:449
  20.2 7.6 %collective-permute-start.2 = (bf16[192,128]{1,0:T(8,128)(2,1)S(1)}, bf16[192,128]{1,0:T(8,128)(2,1)S(1)}, u32[]{:S(2)}, u32[]{:S(2)}) collective-permute-start(bf16[192,128]{1,0:T(8,128)(2,1)S(1)} %get-tuple-element.34), channel_id=1, source_target_pairs={{0,1},{1,0},{2,3},{3,2},{4,5},{5,4},{6,7},{7,6},{8,9},{9,8},{10,11... | collective-permute-start | bytes 147464 | tf_op jit(solution)/shard_map/ppermute | solution.py:449
  27.8 6.6 %collective-permute-start.5 = (bf16[192,128]{1,0:T(8,128)(2,1)S(1)}, bf16[192,128]{1,0:T(8,128)(2,1)S(1)}, u32[]{:S(2)}, u32[]{:S(2)}) collective-permute-start(bf16[192,128]{1,0:T(8,128)(2,1)S(1)} %get-tuple-element.53), channel_id=1, source_target_pairs={{0,2},{1,3},{2,0},{3,1},{4,6},{5,7},{6,4},{7,5},{8,10},{9,11},{10,... | collective-permute-start | bytes 147464 | tf_op jit(solution)/shard_map/ppermute | solution.py:449
  28.9 18.0 %collective-permute-start.4 = (bf16[96,2048]{1,0:T(8,128)(2,1)}, bf16[96,2048]{1,0:T(8,128)(2,1)S(1)}, u32[]{:S(2)}, u32[]{:S(2)}) collective-permute-start(bf16[96,2048]{1,0:T(8,128)(2,1)} %collective-permute-done.1.refs_1_), channel_id=1, source_target_pairs={{1,0},{2,3},{5,4},{6,7},{9,8},{10,11},{13,12},{14,15},{17,16},{18,... | collective-permute-start | bytes 1179656 | tf_op jit(solution)/shard_map/ppermute | solution.py:502
  32.3 14.6 %collective-permute-start.3 = (bf16[96,2048]{1,0:T(8,128)(2,1)S(1)}, bf16[96,2048]{1,0:T(8,128)(2,1)S(1)}, u32[]{:S(2)}, u32[]{:S(2)}) collective-permute-start(bf16[96,2048]{1,0:T(8,128)(2,1)S(1)} %copy-done), channel_id=1, source_target_pairs={{1,2},{2,1},{5,6},{6,5},{9,10},{10,9},{13,14},{14,13},{17,18},{18,... | collective-permute-start | bytes 1179656 | tf_op jit(solution)/shard_map/ppermute | solution.py:503
  35.4 12.2 %all-to-all-start.1 = ((bf16[8,24,512]{2,1,0:T(8,128)(2,1)}), bf16[8,24,512]{2,1,0:T(8,128)(2,1)S(1)}, u32[]{:S(2)}, u32[]{:S(2)}) async-start(bf16[8,24,512]{2,1,0:T(8,128)(2,1)} %bitcast.3), calls=%async_computation.1 | async-start | bytes 393216 | tf_op jit(solution)/shard_map/all_to_all | solution.py:482
  45.1 2.5 %copy-start.1 = (bf16[96,2048]{1,0:T(8,128)(2,1)S(1)}, bf16[96,2048]{1,0:T(8,128)(2,1)}, u32[]{:S(2)}) copy-start(bf16[96,2048]{1,0:T(8,128)(2,1)} %query_ref.1) | copy-start | bytes 1179652
  45.1 2.5 %copy-start.2 = (bf16[96,192]{1,0:T(8,128)(2,1)S(1)}, bf16[96,192]{1,0:T(8,128)(2,1)}, u32[]{:S(2)}) copy-start(bf16[96,192]{1,0:T(8,128)(2,1)} %get-tuple-element.50.pick_ref) | copy-start | bytes 110596

commit v5 on v4

--- a/solution.py
+++ b/solution.py
@@ -32,7 +32,7 @@
     return lax.broadcasted_iota(jnp.int32, shape, dim)
 
 
-def pack_kernel(capacity, owner_ref, slot_ref, hidden_ref, out_ref, pick_ref):
+def pack_kernel(capacity, owner_ref, slot_ref, hidden_ref, out_hbm, pick_hbm, out_ref, pick_ref, sems):
     blocks = owner_ref.shape[0]
     rows, width = hidden_ref.shape
     places = out_ref.shape[0]
@@ -52,28 +52,46 @@
     row_target = jnp.sum(jnp.where(spread, jnp.broadcast_to(target, (blocks, rows)), 0.0), axis=0, keepdims=True)
     row_target = row_target.astype(jnp.int32) * BLK + iota((1, rows), 1) % BLK
     pick = jnp.where(iota((places, rows), 0) == row_target, 1.0, 0.0).astype(jnp.bfloat16)
+    flags = jnp.where(iota((rows, LANES), 1) == row_slot, 1.0, 0.0).astype(jnp.bfloat16)
+    sent = []
+    part = places // 2
+    for n in range(2):
+        here = slice(n * part, (n + 1) * part)
+        out_ref[here, :width] = jnp.dot(pick[here], hidden_ref[...], preferred_element_type=jnp.float32).astype(jnp.bfloat16)
+        out_ref[here, width:] = jnp.dot(pick[here], flags, preferred_element_type=jnp.float32).astype(jnp.bfloat16)
+        rows_there = pl.ds(n * part, part)
+        sent.append(pltpu.make_async_copy(out_ref.at[rows_there], out_hbm.at[rows_there], sems.at[n]))
+        sent[n].start()
     gather = iota((rows, blocks), 1) == iota((rows, blocks), 0) // BLK
     target = jnp.sum(jnp.where(iota(square, 0) == iota(square, 1), target, 0.0), axis=0, keepdims=True)
     target = jnp.sum(jnp.where(gather, target, 0.0), axis=1, keepdims=True)
     target = target.astype(jnp.int32) * BLK + iota((rows, 1), 0) % BLK
     pick_ref[...] = jnp.where(iota((rows, places), 1) == target, 1.0, 0.0).astype(jnp.bfloat16)
-    flags = jnp.where(iota((rows, LANES), 1) == row_slot, 1.0, 0.0).astype(jnp.bfloat16)
-    out_ref[:, :width] = jnp.dot(pick, hidden_ref[...], preferred_element_type=jnp.float32).astype(jnp.bfloat16)
-    out_ref[:, width:] = jnp.dot(pick, flags, preferred_element_type=jnp.float32).astype(jnp.bfloat16)
+    sent.append(pltpu.make_async_copy(pick_ref, pick_hbm, sems.at[2]))
+    sent[-1].start()
+    for copy in sent:
+        copy.wait()
 
 
 def pack(block_owner, block_slot, hidden, replicas, capacity):
     rows, width = hidden.shape
     places = replicas * capacity * BLK
     scalars = pl.BlockSpec(memory_space=pltpu.SMEM)
+    outside = pl.BlockSpec(memory_space=pltpu.HBM)
     return pl.pallas_call(
         functools.partial(pack_kernel, capacity),
         name="pack_rows",
         in_specs=[scalars, scalars, pl.BlockSpec(memory_space=pltpu.VMEM)],
+        out_specs=[outside, outside],
         out_shape=(
-            jax.ShapeDtypeStruct((places, width + LANES), jnp.bfloat16),
-            jax.ShapeDtypeStruct((rows, places), jnp.bfloat16),
+            pltpu.HBM((places, width + LANES), jnp.bfloat16),
+            pltpu.HBM((rows, places), jnp.bfloat16),
         ),
+        scratch_shapes=[
+            pltpu.VMEM((places, width + LANES), jnp.bfloat16),
+            pltpu.VMEM((rows, places), jnp.bfloat16),
+            pltpu.SemaphoreType.DMA((3,)),
+        ],
         compiler_params=params(61),
         cost_estimate=cost(2 * places * rows * width, 2 * (places + rows) * width),
     )(block_owner[:, 0], block_slot, hidden)
@@ -267,48 +285,54 @@
     return place ^ p if parts == 4 else lax.rem(place + parts - p, parts)
 
 
-def own_kernel(total, piece_ref, key_hbm, value_hbm, up_hbm, out_ref, up_ref, keys, values, sems):
-    shard, width = keys.shape
-    rows = pl.ds(pl.multiple_of(owner_of(lax.axis_index("tp"), 0, total) * shard, shard), shard)
-    copies = [
-        pltpu.make_async_copy(key_hbm.at[rows], keys, sems.at[0]),
-        pltpu.make_async_copy(value_hbm.at[rows], values, sems.at[1]),
-        pltpu.make_async_copy(up_hbm, up_ref, sems.at[2]),
-    ]
+def early_kernel(count, total, *refs):
+    pieces, (key_hbm, value_hbm, up_hbm, out_ref, up_ref, keys, values, sems) = refs[:count], refs[count:]
+    shard, width = keys.shape[1:]
+    place = lax.axis_index("tp")
+    copies = []
+    for p in range(count):
+        rows = pl.ds(pl.multiple_of(owner_of(place, p, total) * shard, shard), shard)
+        copies.append(pltpu.make_async_copy(key_hbm.at[rows], keys.at[p], sems.at[0, p]))
+        copies.append(pltpu.make_async_copy(value_hbm.at[rows], values.at[p], sems.at[1, p]))
+    copies.append(pltpu.make_async_copy(up_hbm, up_ref, sems.at[0, count]))
     for copy in copies:
         copy.start()
-    for half, weights in enumerate((keys, values)):
-        copies[half].wait()
-        product = jnp.dot(piece_ref[...], weights[...], preferred_element_type=jnp.float32)
-        out_ref[:, half * width : (half + 1) * width] = product
-    copies[2].wait()
-
-
-def own_product(piece, total, key_matrix, value_matrix, up):
-    rows, shard = piece.shape
+    for p in range(count):
+        for half, weights in enumerate((keys, values)):
+            here = slice(half * width, (half + 1) * width)
+            copies[2 * p + half].wait()
+            product = jnp.dot(pieces[p][...], weights[p], preferred_element_type=jnp.float32)
+            out_ref[:, here] = out_ref[:, here] + product if p else product
+    copies[-1].wait()
+
+
+def early_products(pieces, total, key_matrix, value_matrix, up):
+    rows, shard = pieces[0].shape
     width = key_matrix.shape[1]
+    count = len(pieces)
     inside, outside = pl.BlockSpec(memory_space=pltpu.VMEM), pl.BlockSpec(memory_space=pltpu.HBM)
     return pl.pallas_call(
-        functools.partial(own_kernel, total),
-        name="own_product",
-        in_specs=[inside, outside, outside, outside],
+        functools.partial(early_kernel, count, total),
+        name="early_products",
+        in_specs=[inside] * count + [outside, outside, outside],
         out_specs=[inside, inside],
         out_shape=[jax.ShapeDtypeStruct((rows, 2 * width), jnp.float32), jax.ShapeDtypeStruct(up.shape, up.dtype)],
-        scratch_shapes=[pltpu.VMEM((shard, width), key_matrix.dtype)] * 2 + [pltpu.SemaphoreType.DMA((3,))],
-        compiler_params=params(8),
-        cost_estimate=cost(4 * rows * shard * width, 4 * shard * width),
-    )(piece, pinned(key_matrix), pinned(value_matrix), pinned(up))
-
-
-def base_kernel(total, *refs):
-    count = total - 2
+        scratch_shapes=[pltpu.VMEM((count, shard, width), key_matrix.dtype)] * 2
+        + [pltpu.SemaphoreType.DMA((2, count + 1))],
+        compiler_params=params(12),
+        cost_estimate=cost(4 * count * rows * shard * width, 4 * count * shard * width),
+    )(*pieces, pinned(key_matrix), pinned(value_matrix), pinned(up))
+
+
+def base_kernel(first, total, *refs):
+    count = total - 1 - first
     pieces, refs = refs[:count], refs[count:]
     so_far, key_hbm, value_hbm, mean_hbm, out_ref, last_keys, last_values, mean_ref, keys, values, sems = refs
     shard, width = last_keys.shape
     place = lax.axis_index("tp")
 
     def copies(p):
-        rows = pl.ds(pl.multiple_of(owner_of(place, p + 1, total) * shard, shard), shard)
+        rows = pl.ds(pl.multiple_of(owner_of(place, p + first, total) * shard, shard), shard)
         key_to, value_to = (last_keys, last_values) if p == count else (keys.at[p], values.at[p])
         key_copy = pltpu.make_async_copy(key_hbm.at[rows], key_to, sems.at[0, p]) if p > 0 else None
         return key_copy, pltpu.make_async_copy(value_hbm.at[rows], value_to, sems.at[1, p])
@@ -329,14 +353,14 @@
         copy.wait()
 
 
-def base_products(pieces, so_far, key_matrix, value_matrix, mean):
+def base_products(pieces, total, so_far, key_matrix, value_matrix, mean):
     rows, shard = pieces[0].shape
     width = key_matrix.shape[1]
     count = len(pieces)
     inside, outside = pl.BlockSpec(memory_space=pltpu.VMEM), pl.BlockSpec(memory_space=pltpu.HBM)
     last = jax.ShapeDtypeStruct((shard, width), key_matrix.dtype)
     return pl.pallas_call(
-        functools.partial(base_kernel, count + 2),
+        functools.partial(base_kernel, total - 1 - count, total),
         name="base_products",
         in_specs=[inside] * (count + 1) + [outside] * 3,
         out_specs=[inside] * 4,
@@ -356,51 +380,39 @@
     )(*pieces, so_far, pinned(key_matrix), pinned(value_matrix), pinned(mean))
 
 
-def last_kernel(count, total, *refs):
-    sources, (keys, values, base_ref, out_ref, piece_ref, sem) = refs[:count], refs[count:]
+def last_kernel(piece_ref, keys, values, base_ref, out_ref):
     width = keys.shape[1]
-    place = lax.axis_index("tp")
-    outer = (place == 0) | (place == total - 1)
-    for n, source in enumerate(sources):
-
-        @pl.when(True if count == 1 else outer == (n == count - 1))
-        def _():
-            copy = pltpu.make_async_copy(source, piece_ref, sem)
-            copy.start()
-            copy.wait()
-
     for half, weights in enumerate((keys, values)):
         here = slice(half * width, (half + 1) * width)
         product = jnp.dot(piece_ref[...], weights[...], preferred_element_type=jnp.float32)
         out_ref[:, here] = base_ref[:, here] + product
 
 
-def last_product(late, total, keys, values, base):
-    inside, outside = pl.BlockSpec(memory_space=pltpu.VMEM), pl.BlockSpec(memory_space=pltpu.HBM)
-    return pl.pallas_call(
-        functools.partial(last_kernel, len(late), total),
+def last_product(late, keys, values, base):
+    return pl.pallas_call(
+        last_kernel,
         name="last_product",
-        in_specs=[outside] * len(late) + [inside] * 3,
-        out_specs=inside,
         out_shape=jax.ShapeDtypeStruct(base.shape, base.dtype),
-        scratch_shapes=[pltpu.VMEM(late[0].shape, late[0].dtype), pltpu.SemaphoreType.DMA],
         compiler_params=params(8),
-        cost_estimate=cost(2 * late[0].size * base.shape[1], 4 * keys.size),
-    )(*late, keys, values, base)
+        cost_estimate=cost(2 * late.size * base.shape[1], 4 * keys.size),
+    )(late, keys, values, base)
 
 
 def finish_kernel(base_ref, back_ref, pick_ref, query_ref, lse_ref, mean_ref, *refs):
-    new_key_ref, new_value_ref, context_hbm, context_ref, sems = refs
+    new_key_hbm, new_value_hbm, context_hbm, new_ref, context_ref, sems = refs
     rows, wide = query_ref.shape
-    width = new_key_ref.shape[1]
+    width = new_ref.shape[2]
     heads = wide // HEAD_SIZE
     groups = width // HEAD_SIZE
     each = heads // groups
     inverse_root = HEAD_SIZE ** (-0.5)
     delta = jnp.dot(pick_ref[...], back_ref[...], preferred_element_type=jnp.float32)
     base = (base_ref[...] + delta).astype(jnp.bfloat16)
-    new_key_ref[...] = base[:, :width]
-    new_value_ref[...] = base[:, width:]
+    sent = []
+    for half, target in enumerate((new_key_hbm, new_value_hbm)):
+        new_ref[half] = base[:, half * width : (half + 1) * width]
+        sent.append(pltpu.make_async_copy(new_ref.at[half], target, sems.at[groups + half]))
+        sent[half].start()
     keys, values = base[:, :width].astype(jnp.float32), base[:, width:].astype(jnp.float32)
     column = iota((rows, LANES), 1)
     own = jnp.zeros((rows, LANES), jnp.float32)
@@ -416,10 +428,10 @@
             mixed = mean + share[:, h : h + 1] * (values[:, k * HEAD_SIZE : (k + 1) * HEAD_SIZE] - mean)
             context_ref[:, h * HEAD_SIZE : (h + 1) * HEAD_SIZE] = mixed.astype(jnp.bfloat16)
         part = pl.ds(k * each * HEAD_SIZE, each * HEAD_SIZE)
-        pltpu.make_async_copy(context_ref.at[:, part], context_hbm.at[:, part], sems.at[k]).start()
-    for k in range(groups):
-        part = pl.ds(k * each * HEAD_SIZE, each * HEAD_SIZE)
-        pltpu.make_async_copy(context_ref.at[:, part], context_hbm.at[:, part], sems.at[k]).wait()
+        sent.append(pltpu.make_async_copy(context_ref.at[:, part], context_hbm.at[:, part], sems.at[k]))
+        sent[-1].start()
+    for copy in sent:
+        copy.wait()
 
 
 def finish(base, back, pick, queries, lse, mean):
@@ -430,15 +442,16 @@
         finish_kernel,
         name="finish_rows",
         in_specs=[inside] * 6,
-        out_specs=[inside, inside, outside],
+        out_specs=[outside] * 3,
         out_shape=(
             jax.ShapeDtypeStruct((rows, width), jnp.bfloat16),
             jax.ShapeDtypeStruct((rows, width), jnp.bfloat16),
             jax.ShapeDtypeStruct((rows, wide), jnp.bfloat16),
         ),
         scratch_shapes=[
+            pltpu.VMEM((2, rows, width), jnp.bfloat16),
             pltpu.VMEM((rows, wide), jnp.bfloat16),
-            pltpu.SemaphoreType.DMA((width // HEAD_SIZE,)),
+            pltpu.SemaphoreType.DMA((width // HEAD_SIZE + 2,)),
         ],
         compiler_params=params(8),
         cost_estimate=cost(4 * rows * wide, 10 * rows * wide),
@@ -491,30 +504,31 @@
     arrived, lse = lax.optimization_barrier((arrived, lse))
     partial_rows, sent, flags = shrink(arrived, shrink_here)
     matrices = (base_key_matrix, base_value_matrix)
-    partial_rows, own_piece = lax.optimization_barrier((partial_rows, hidden_in))
-    base, up_here = own_product(own_piece, parts, *matrices, pooled_up_weights)
     if parts == 4:
+        pieces = [hidden_in, one]
         received = swap(sent, 1, parts)
+    else:
+        pieces = [hidden_in] + others(hidden_in, parts)
+    early = 1
+    sent, *first = lax.optimization_barrier((sent, *pieces[:early]))
+    base, up_here = early_products(first, parts, *matrices, pooled_up_weights)
+    if parts == 4:
         received, base = lax.optimization_barrier((received, base))
         paired = partial_rows + received.astype(jnp.float32)
         sums = [paired, swap(paired.astype(jnp.bfloat16), 2, parts)]
-        one, two, again, _ = lax.optimization_barrier((one, two, hidden_in, paired))
-        outer = lax.ppermute(two, "tp", [(1, 0), (2, 3)])
-        inner = lax.ppermute(again, "tp", [(1, 2), (2, 1)])
-        between, late = [one, two], [inner, outer]
+        one, two, _ = lax.optimization_barrier((one, two, paired))
+        pieces = [hidden_in, one, two, swap(two, 1, parts)]
     else:
         sums = [partial_rows] + others(sent, parts)
-        pieces = others(hidden_in, parts)
-        between, late = pieces[:-1], pieces[-1:]
     deltas = expand(sums, flags, up_here)
     back = all_to_all(deltas)
-    deltas, *between = lax.optimization_barrier((deltas, *between))
-    base, *last, mean = base_products(between, base, *matrices, mean)
-    owner = owner_of(lax.axis_index("tp"), 1, parts)
+    deltas, *between = lax.optimization_barrier((deltas, *pieces[early:-1]))
+    base, *last, mean = base_products(between, parts, base, *matrices, mean)
+    owner = owner_of(lax.axis_index("tp"), early, parts)
     key_rows = lax.dynamic_slice_in_dim(base_key_matrix, owner * shard_width, shard_width, 0)
     more = jnp.dot(between[0], key_rows, preferred_element_type=jnp.float32)
     base = base + jnp.concatenate([more, jnp.zeros_like(more)], axis=1)
-    base = last_product(late, parts, *last, base)
+    base = last_product(pieces[-1], *last, base)
     return finish(base, back, pick, queries, lse, mean)
 
 

time: 50.1 us -> 47.5 us (0.948)
  the two profiles are of different devices: /device:TPU:11 before, /device:TPU:0 now
where the time goes in v5:
time: 47.5 us; the launch traced here: 47.1 us
  Pallas kernels  20.7 us (44%)
  starting transfers between devices  18 us (38%)
  waiting for transfers between devices  5.96 us (13%)
  matrix products  1.7 us (4%)
  between operations  0.72 us (2%)
    ppermute x5, starting transfers between devices, swap(): return lax.ppermute(x, 'tp', [(i, i ^ mask) for i in range(size)])  9.35 us
    all_to_all x2, starting transfers between devices, all_to_all(): lax.all_to_all(x, 'rep', split_axis=0, concat_axis=0, tiled=True)  8.64 us
    pallas_call x1, Pallas kernels, cached_attention(): pl.pallas_call(functools.partial(cached_kernel, heads, group), name='cach...  8.45 us
    ppermute x5, waiting for transfers between devices, swap(): return lax.ppermute(x, 'tp', [(i, i ^ mask) for i in range(size)])  5.42 us
    pallas_call x1, Pallas kernels, base_products(): pl.pallas_call(functools.partial(base_kernel, total - 1 - count, total),...  3.88 us
    pallas_call x1, Pallas kernels, pack(): pl.pallas_call(functools.partial(pack_kernel, capacity), name='pack_rows'...  2.31 us
    pallas_call x1, Pallas kernels, early_products(): pl.pallas_call(functools.partial(early_kernel, count, total), name='early...  2.08 us
    dot_general x1, matrix products, shards(): more = jnp.dot(between[0], key_rows, preferred_element_type=jnp.float32)  1.7 us
  transfers between devices with their start and end apart: 7, of which 4 were waited for; matrix products, arithmetic and copies ran while one was open for 4% of the time, Pallas kernels for 36%

profile of v5, /device:TPU:0, one launch (start us, length us, event | category | flops | bytes accessed | tf_op | source)
XLA Modules:
  0.0 47.1 jit_solution(13557791340348122606)
XLA Ops:
  0.6 2.3 %pack_rows.1 = (bf16[192,2176]{1,0:T(8,128)(2,1)}, bf16[96,192]{1,0:T(8,128)(2,1)}) custom-call(s32[24]{0:T(128)} %bitcast.9, s32[24]{0:T(128)} %slot_ref.1, bf16[96,2048]{1,0:T(8,128)(2,1)} %refs_0_), custom_call_target="tpu_custom_call" | custom-call | flops 75497472 | bytes 1179648 | tf_op jit(solution)/shard_map/pack_rows/pallas_call | solution.py:81
  2.9 5.2 %all-to-all-start = ((bf16[8,24,2176]{2,1,0:T(8,128)(2,1)}), bf16[8,24,2176]{2,1,0:T(8,128)(2,1)S(1)}, u32[]{:S(2)}, u32[]{:S(2)}) async-start(bf16[8,24,2176]{2,1,0:T(8,128)(2,1)} %bitcast.8), calls=%async_computation | async-start | bytes 1671168 | tf_op jit(solution)/shard_map/all_to_all | solution.py:495
  8.1 0.0 copy-start
  8.1 1.6 %collective-permute-start = (bf16[96,2048]{1,0:T(8,128)(2,1)}, bf16[96,2048]{1,0:T(8,128)(2,1)}, u32[]{:S(2)}, u32[]{:S(2)}) collective-permute-start(bf16[96,2048]{1,0:T(8,128)(2,1)} %refs_0_), channel_id=1, source_target_pairs={{0,1},{1,0},{2,3},{3,2},{4,5},{5,4},{6,7},{7,6},{8,9},{9,8},{10,11... | collective-permute-start | bytes 1179656 | tf_op jit(solution)/shard_map/ppermute | solution.py:462
  9.8 2.6 %collective-permute-start.1 = (bf16[96,2048]{1,0:T(8,128)(2,1)}, bf16[96,2048]{1,0:T(8,128)(2,1)}, u32[]{:S(2)}, u32[]{:S(2)}) collective-permute-start(bf16[96,2048]{1,0:T(8,128)(2,1)} %refs_0_), channel_id=1, source_target_pairs={{0,2},{1,3},{2,0},{3,1},{4,6},{5,7},{6,4},{7,5},{8,10},{9,11},{10,... | collective-permute-start | bytes 1179656 | tf_op jit(solution)/shard_map/ppermute | solution.py:462
  12.4 8.4 %cached_attention.1 = (f32[96,2048]{1,0:T(8,128)}, f32[96,128]{1,0:T(8,128)S(1)}, bf16[4,2048,128]{2,1,0:T(8,128)(2,1)S(1)}) custom-call(s32[96]{0:T(128)} %length_hbm.1, bf16[96,2048]{1,0:T(8,128)(2,1)} %query_ref.1, bf16[96,128,256]{2,1,0:T(8,128)(2,1)} %key_hbm.1, bf16[96,128,256]{2,1,0:T(8,128)(2,1)} %value_hbm.1, bf16[4,2048,128]{2,1,0:T(8,128)(2,1)} %shrink_hbm.1), custom_call_target="tpu_custom_call" | custom-call | flops 201326592 | bytes 13762560 | tf_op jit(solution)/shard_map/cached_attention/pallas_call | solution.py:258
  20.8 0.4 all-to-all-done
  21.3 1.0 %shrink_rows.1 = (f32[192,128]{1,0:T(8,128)S(1)}, bf16[192,128]{1,0:T(8,128)(2,1)S(1)}, bf16[192,128]{1,0:T(8,128)(2,1)S(1)}) custom-call(bf16[192,2176]{1,0:T(8,128)(2,1)S(1)} %bitcast.6, bf16[4,2048,128]{2,1,0:T(8,128)(2,1)S(1)} %get-tuple-element.29.shrink_ref), custom_call_target="tpu_custom_call" | custom-call | flops 402653184 | bytes 2883584 | tf_op jit(solution)/shard_map/shrink_rows/pallas_call | solution.py:115
  22.2 1.6 %collective-permute-start.2 = (bf16[192,128]{1,0:T(8,128)(2,1)S(1)}, bf16[192,128]{1,0:T(8,128)(2,1)S(1)}, u32[]{:S(2)}, u32[]{:S(2)}) collective-permute-start(bf16[192,128]{1,0:T(8,128)(2,1)S(1)} %get-tuple-element.31), channel_id=1, source_target_pairs={{0,1},{1,0},{2,3},{3,2},{4,5},{5,4},{6,7},{7,6},{8,9},{9,8},{10,11... | collective-permute-start | bytes 147464 | tf_op jit(solution)/shard_map/ppermute | solution.py:462
  23.9 0.0 copy-done
  23.9 2.1 %early_products.1 = (f32[96,512]{1,0:T(8,128)S(1)}, bf16[4,2,64,256]{3,2,1,0:T(8,128)(2,1)S(1)}) custom-call(bf16[96,2048]{1,0:T(8,128)(2,1)S(1)} %copy-done, bf16[8192,256]{1,0:T(8,128)(2,1)} %refs_3_.3, bf16[8192,256]{1,0:T(8,128)(2,1)} %refs_4_.1, bf16[4,2,64,256]{3,2,1,0:T(8,128)(2,1)} %refs_3_.2), custom_call_target="tpu_custom_call" | custom-call | flops 201326592 | bytes 2097152 | tf_op jit(solution)/shard_map/early_products/pallas_call | solution.py:314
  26.0 3.2 %collective-permute-done.2 = bf16[192,128]{1,0:T(8,128)(2,1)S(1)} collective-permute-done((bf16[192,128]{1,0:T(8,128)(2,1)S(1)}, bf16[192,128]{1,0:T(8,128)(2,1)S(1)}, u32[]{:S(2)}, u32[]{:S(2)}) %collective-permute-start.2) | collective-permute-done | bytes 49184 | tf_op jit(solution)/shard_map/ppermute | solution.py:462
  29.2 2.8 %collective-permute-start.4 = (bf16[192,128]{1,0:T(8,128)(2,1)S(1)}, bf16[192,128]{1,0:T(8,128)(2,1)S(1)}, u32[]{:S(2)}, u32[]{:S(2)}) collective-permute-start(bf16[192,128]{1,0:T(8,128)(2,1)S(1)} %get-tuple-element.49), channel_id=1, source_target_pairs={{0,2},{1,3},{2,0},{3,1},{4,6},{5,7},{6,4},{7,5},{8,10},{9,11},{10,... | collective-permute-start | bytes 147464 | tf_op jit(solution)/shard_map/ppermute | solution.py:462
  32.1 0.0 collective-permute-done.refs_0_
  32.1 0.0 collective-permute-done.1.refs_1_
  32.1 0.6 %collective-permute-start.3 = (bf16[96,2048]{1,0:T(8,128)(2,1)}, bf16[96,2048]{1,0:T(8,128)(2,1)S(1)}, u32[]{:S(2)}, u32[]{:S(2)}) collective-permute-start(bf16[96,2048]{1,0:T(8,128)(2,1)} %collective-permute-done.1.refs_1_), channel_id=1, source_target_pairs={{0,1},{1,0},{2,3},{3,2},{4,5},{5,4},{6,7},{7,6},{8,9},{9,8},{10,11... | collective-permute-start | bytes 1179656 | tf_op jit(solution)/shard_map/ppermute | solution.py:462
  32.7 2.2 %collective-permute-done.4.refs_1_ = bf16[192,128]{1,0:T(8,128)(2,1)S(1)} collective-permute-done((bf16[192,128]{1,0:T(8,128)(2,1)S(1)}, bf16[192,128]{1,0:T(8,128)(2,1)S(1)}, u32[]{:S(2)}, u32[]{:S(2)}) %collective-permute-start.4) | collective-permute-done | bytes 49184 | tf_op jit(solution)/shard_map/ppermute | solution.py:462
  34.9 1.0 %expand_rows.1 = bf16[192,512]{1,0:T(8,128)(2,1)} custom-call(f32[192,128]{1,0:T(8,128)S(1)} %get-tuple-element.50.refs_0_, bf16[192,128]{1,0:T(8,128)(2,1)S(1)} %collective-permute-done.4.refs_1_, bf16[192,128]{1,0:T(8,128)(2,1)S(1)} %get-tuple-element.36.refs_2_, bf16[4,2,64,256]{3,2,1,0:T(8,128)(2,1)S(1)} %get-tuple-element.37.refs_3_), custom_call_target="tpu_custom_call" | custom-call | flops 50331648 | bytes 458752 | tf_op jit(solution)/shard_map/expand_rows/pallas_call | solution.py:149
  35.9 3.5 %all-to-all-start.1 = ((bf16[8,24,512]{2,1,0:T(8,128)(2,1)}), bf16[8,24,512]{2,1,0:T(8,128)(2,1)S(1)}, u32[]{:S(2)}, u32[]{:S(2)}) async-start(bf16[8,24,512]{2,1,0:T(8,128)(2,1)} %bitcast.3), calls=%async_computation.1 | async-start | bytes 393216 | tf_op jit(solution)/shard_map/all_to_all | solution.py:495
  39.4 3.9 %base_products.1 = (f32[96,512]{1,0:T(8,128)S(1)}, bf16[2048,256]{1,0:T(8,128)(2,1)S(1)}, bf16[2048,256]{1,0:T(8,128)(2,1)S(1)}, f32[96,2048]{1,0:T(8,128)S(1)}) custom-call(bf16[96,2048]{1,0:T(8,128)(2,1)} %collective-permute-done.refs_0_, bf16[96,2048]{1,0:T(8,128)(2,1)} %collective-permute-done.1.refs_1_, f32[96,512]{1,0:T(8,128)S(1)} %get-tuple-element.41.refs_2_, ...), custom_call_target="tpu_custom_call" | custom-call | flops 402653184 | bytes 4980736 | tf_op jit(solution)/shard_map/base_products/pallas_call | solution.py:362
  43.3 0.0 copy-start.1
  43.3 0.0 copy-start.2
  43.3 1.7 %fusion = f32[96,256]{1,0:T(8,128)S(1)} fusion(bf16[96,2048]{1,0:T(8,128)(2,1)} %collective-permute-done.refs_0_, bf16[8192,256]{1,0:T(8,128)(2,1)} %refs_3_.3, s32[]{:T(128)S(6)} %select_n.3), kind=kOutput, calls=%fused_computation | convolution fusion | flops 100663296 | bytes 1540100 | tf_op jit(solution)/shard_map/dot_general | solution.py:529
  45.0 0.0 collective-permute-done.3.piece_ref
  45.0 0.5 %last_product.1.base_ref = f32[96,512]{1,0:T(8,128)S(1)} custom-call(bf16[96,2048]{1,0:T(8,128)(2,1)S(1)} %collective-permute-done.3.piece_ref, bf16[2048,256]{1,0:T(8,128)(2,1)S(1)} %get-tuple-element.43.keys, bf16[2048,256]{1,0:T(8,128)(2,1)S(1)} %get-tuple-element.44.values, f32[96,512]{1,0:T(8,128)S(1)} %pad_add_fusion.base_ref), custom_call_target="tpu_custom_call" | custom-call | flops 201326592 | bytes 2097152 | tf_op jit(solution)/shard_map/last_product/pallas_call | solution.py:392
  45.5 0.1 all-to-all-done.1
  45.6 0.0 copy-done.1
  45.6 0.0 copy-done.2
  45.6 1.5 %finish_rows.1 = (bf16[96,256]{1,0:T(8,128)(2,1)}, bf16[96,256]{1,0:T(8,128)(2,1)}, bf16[96,2048]{1,0:T(8,128)(2,1)}) custom-call(f32[96,512]{1,0:T(8,128)S(1)} %last_product.1.base_ref, bf16[192,512]{1,0:T(8,128)(2,1)S(1)} %bitcast.7, bf16[96,192]{1,0:T(8,128)(2,1)S(1)} %copy-done.2, bf16[96,2048]{1,0:T(8,128)(2,1)S(1)} %copy-done.1, ...), custom_call_target="tpu_custom_call" | custom-call | flops 786432 | bytes 1966080 | tf_op jit(solution)/shard_map/finish_rows/pallas_call | solution.py:441
  (2 shorter events, 0.0 us)
Async XLA Ops:
  2.9 18.3 %all-to-all-start = ((bf16[8,24,2176]{2,1,0:T(8,128)(2,1)}), bf16[8,24,2176]{2,1,0:T(8,128)(2,1)S(1)}, u32[]{:S(2)}, u32[]{:S(2)}) async-start(bf16[8,24,2176]{2,1,0:T(8,128)(2,1)} %bitcast.8), calls=%async_computation | async-start | bytes 1671168 | tf_op jit(solution)/shard_map/all_to_all | solution.py:495
  8.1 15.8 %copy-start = (bf16[96,2048]{1,0:T(8,128)(2,1)S(1)}, bf16[96,2048]{1,0:T(8,128)(2,1)}, u32[]{:S(2)}) copy-start(bf16[96,2048]{1,0:T(8,128)(2,1)} %refs_0_) | copy-start | bytes 1179652
  8.1 23.9 %collective-permute-start = (bf16[96,2048]{1,0:T(8,128)(2,1)}, bf16[96,2048]{1,0:T(8,128)(2,1)}, u32[]{:S(2)}, u32[]{:S(2)}) collective-permute-start(bf16[96,2048]{1,0:T(8,128)(2,1)} %refs_0_), channel_id=1, source_target_pairs={{0,1},{1,0},{2,3},{3,2},{4,5},{5,4},{6,7},{7,6},{8,9},{9,8},{10,11... | collective-permute-start | bytes 1179656 | tf_op jit(solution)/shard_map/ppermute | solution.py:462
  9.8 22.3 %collective-permute-start.1 = (bf16[96,2048]{1,0:T(8,128)(2,1)}, bf16[96,2048]{1,0:T(8,128)(2,1)}, u32[]{:S(2)}, u32[]{:S(2)}) collective-permute-start(bf16[96,2048]{1,0:T(8,128)(2,1)} %refs_0_), channel_id=1, source_target_pairs={{0,2},{1,3},{2,0},{3,1},{4,6},{5,7},{6,4},{7,5},{8,10},{9,11},{10,... | collective-permute-start | bytes 1179656 | tf_op jit(solution)/shard_map/ppermute | solution.py:462
  22.2 7.0 %collective-permute-start.2 = (bf16[192,128]{1,0:T(8,128)(2,1)S(1)}, bf16[192,128]{1,0:T(8,128)(2,1)S(1)}, u32[]{:S(2)}, u32[]{:S(2)}) collective-permute-start(bf16[192,128]{1,0:T(8,128)(2,1)S(1)} %get-tuple-element.31), channel_id=1, source_target_pairs={{0,1},{1,0},{2,3},{3,2},{4,5},{5,4},{6,7},{7,6},{8,9},{9,8},{10,11... | collective-permute-start | bytes 147464 | tf_op jit(solution)/shard_map/ppermute | solution.py:462
  29.2 5.7 %collective-permute-start.4 = (bf16[192,128]{1,0:T(8,128)(2,1)S(1)}, bf16[192,128]{1,0:T(8,128)(2,1)S(1)}, u32[]{:S(2)}, u32[]{:S(2)}) collective-permute-start(bf16[192,128]{1,0:T(8,128)(2,1)S(1)} %get-tuple-element.49), channel_id=1, source_target_pairs={{0,2},{1,3},{2,0},{3,1},{4,6},{5,7},{6,4},{7,5},{8,10},{9,11},{10,... | collective-permute-start | bytes 147464 | tf_op jit(solution)/shard_map/ppermute | solution.py:462
  32.1 12.9 %collective-permute-start.3 = (bf16[96,2048]{1,0:T(8,128)(2,1)}, bf16[96,2048]{1,0:T(8,128)(2,1)S(1)}, u32[]{:S(2)}, u32[]{:S(2)}) collective-permute-start(bf16[96,2048]{1,0:T(8,128)(2,1)} %collective-permute-done.1.refs_1_), channel_id=1, source_target_pairs={{0,1},{1,0},{2,3},{3,2},{4,5},{5,4},{6,7},{7,6},{8,9},{9,8},{10,11... | collective-permute-start | bytes 1179656 | tf_op jit(solution)/shard_map/ppermute | solution.py:462
  35.9 9.7 %all-to-all-start.1 = ((bf16[8,24,512]{2,1,0:T(8,128)(2,1)}), bf16[8,24,512]{2,1,0:T(8,128)(2,1)S(1)}, u32[]{:S(2)}, u32[]{:S(2)}) async-start(bf16[8,24,512]{2,1,0:T(8,128)(2,1)} %bitcast.3), calls=%async_computation.1 | async-start | bytes 393216 | tf_op jit(solution)/shard_map/all_to_all | solution.py:495
  43.3 2.3 %copy-start.1 = (bf16[96,2048]{1,0:T(8,128)(2,1)S(1)}, bf16[96,2048]{1,0:T(8,128)(2,1)}, u32[]{:S(2)}) copy-start(bf16[96,2048]{1,0:T(8,128)(2,1)} %query_ref.1) | copy-start | bytes 1179652
  43.3 2.3 %copy-start.2 = (bf16[96,192]{1,0:T(8,128)(2,1)S(1)}, bf16[96,192]{1,0:T(8,128)(2,1)}, u32[]{:S(2)}) copy-start(bf16[96,192]{1,0:T(8,128)(2,1)} %get-tuple-element.46.pick_ref) | copy-start | bytes 110596

commit v6 on v5

--- a/solution.py
+++ b/solution.py
@@ -506,17 +506,16 @@
     matrices = (base_key_matrix, base_value_matrix)
     if parts == 4:
         pieces = [hidden_in, one]
-        received = swap(sent, 1, parts)
+        received = [swap(sent, mask, parts) for mask in (1, 2, 3)]
     else:
         pieces = [hidden_in] + others(hidden_in, parts)
     early = 1
     sent, *first = lax.optimization_barrier((sent, *pieces[:early]))
     base, up_here = early_products(first, parts, *matrices, pooled_up_weights)
     if parts == 4:
-        received, base = lax.optimization_barrier((received, base))
-        paired = partial_rows + received.astype(jnp.float32)
-        sums = [paired, swap(paired.astype(jnp.bfloat16), 2, parts)]
-        one, two, _ = lax.optimization_barrier((one, two, paired))
+        received[0], base = lax.optimization_barrier((received[0], base))
+        sums = [partial_rows] + received
+        one, two, _ = lax.optimization_barrier((one, two, received[0]))
         pieces = [hidden_in, one, two, swap(two, 1, parts)]
     else:
         sums = [partial_rows] + others(sent, parts)

time: 47.5 us -> 46.7 us (0.983)
  waiting for transfers between devices: 5.96 us -> 2.32 us
  starting transfers between devices: 18 us -> 20.3 us
  Pallas kernels: 20.7 us -> 21.3 us
    ppermute x5 -> x6, waiting for transfers between devices: 5.42 us -> 1.78 us  [swap(): return lax.ppermute(x, 'tp', [(i, i ^ mask) for i in range(size)])]
    ppermute x5 -> x6, starting transfers between devices: 9.35 us -> 11.3 us  [swap(): return lax.ppermute(x, 'tp', [(i, i ^ mask) for i in range(size)])]
    pallas_call x1, Pallas kernels: 0.97 us -> 1.61 us  [shrink(): pl.pallas_call(shrink_kernel, name='shrink_rows', out_shape=(jax.ShapeDty...]
  transfers between devices with their start and end apart: 7 -> 8, of which waited for: 4 -> 4; matrix products, arithmetic and copies ran while one was open for 4% -> 4% of each run, Pallas kernels for 36% -> 38%
where the time goes in v6:
time: 46.7 us; the launch traced here: 46.4 us
  Pallas kernels  21.3 us (46%)
  starting transfers between devices  20.3 us (43%)
  waiting for transfers between devices  2.32 us (5%)
  matrix products  1.7 us (4%)
  between operations  0.73 us (2%)
    ppermute x6, starting transfers between devices, swap(): return lax.ppermute(x, 'tp', [(i, i ^ mask) for i in range(size)])  11.3 us
    all_to_all x2, starting transfers between devices, all_to_all(): lax.all_to_all(x, 'rep', split_axis=0, concat_axis=0, tiled=True)  8.98 us
    pallas_call x1, Pallas kernels, cached_attention(): pl.pallas_call(functools.partial(cached_kernel, heads, group), name='cach...  8.45 us
    pallas_call x1, Pallas kernels, base_products(): pl.pallas_call(functools.partial(base_kernel, total - 1 - count, total),...  3.88 us
    pallas_call x1, Pallas kernels, pack(): pl.pallas_call(functools.partial(pack_kernel, capacity), name='pack_rows'...  2.31 us
    pallas_call x1, Pallas kernels, early_products(): pl.pallas_call(functools.partial(early_kernel, count, total), name='early...  2.08 us
    ppermute x6, waiting for transfers between devices, swap(): return lax.ppermute(x, 'tp', [(i, i ^ mask) for i in range(size)])  1.78 us
    dot_general x1, matrix products, shards(): more = jnp.dot(between[0], key_rows, preferred_element_type=jnp.float32)  1.7 us
  transfers between devices with their start and end apart: 8, of which 4 were waited for; matrix products, arithmetic and copies ran while one was open for 4% of the time, Pallas kernels for 38%

profile of v6, /device:TPU:0, one launch (start us, length us, event | category | flops | bytes accessed | tf_op | source)
XLA Modules:
  0.0 46.4 jit_solution(11375113830240582403)
XLA Ops:
  0.6 2.3 %pack_rows.1 = (bf16[192,2176]{1,0:T(8,128)(2,1)}, bf16[96,192]{1,0:T(8,128)(2,1)}) custom-call(s32[24]{0:T(128)} %bitcast.9, s32[24]{0:T(128)} %slot_ref.1, bf16[96,2048]{1,0:T(8,128)(2,1)} %refs_0_), custom_call_target="tpu_custom_call" | custom-call | flops 75497472 | bytes 1179648 | tf_op jit(solution)/shard_map/pack_rows/pallas_call | solution.py:81
  2.9 5.2 %all-to-all-start = ((bf16[8,24,2176]{2,1,0:T(8,128)(2,1)}), bf16[8,24,2176]{2,1,0:T(8,128)(2,1)S(1)}, u32[]{:S(2)}, u32[]{:S(2)}) async-start(bf16[8,24,2176]{2,1,0:T(8,128)(2,1)} %bitcast.8), calls=%async_computation | async-start | bytes 1671168 | tf_op jit(solution)/shard_map/all_to_all | solution.py:495
  8.1 0.0 copy-start
  8.1 1.6 %collective-permute-start = (bf16[96,2048]{1,0:T(8,128)(2,1)}, bf16[96,2048]{1,0:T(8,128)(2,1)}, u32[]{:S(2)}, u32[]{:S(2)}) collective-permute-start(bf16[96,2048]{1,0:T(8,128)(2,1)} %refs_0_), channel_id=1, source_target_pairs={{0,1},{1,0},{2,3},{3,2},{4,5},{5,4},{6,7},{7,6},{8,9},{9,8},{10,11... | collective-permute-start | bytes 1179656 | tf_op jit(solution)/shard_map/ppermute | solution.py:462
  9.8 2.6 %collective-permute-start.1 = (bf16[96,2048]{1,0:T(8,128)(2,1)}, bf16[96,2048]{1,0:T(8,128)(2,1)}, u32[]{:S(2)}, u32[]{:S(2)}) collective-permute-start(bf16[96,2048]{1,0:T(8,128)(2,1)} %refs_0_), channel_id=1, source_target_pairs={{0,2},{1,3},{2,0},{3,1},{4,6},{5,7},{6,4},{7,5},{8,10},{9,11},{10,... | collective-permute-start | bytes 1179656 | tf_op jit(solution)/shard_map/ppermute | solution.py:462
  12.4 8.4 %cached_attention.1 = (f32[96,2048]{1,0:T(8,128)}, f32[96,128]{1,0:T(8,128)S(1)}, bf16[4,2048,128]{2,1,0:T(8,128)(2,1)S(1)}) custom-call(s32[96]{0:T(128)} %length_hbm.1, bf16[96,2048]{1,0:T(8,128)(2,1)} %query_ref.1, bf16[96,128,256]{2,1,0:T(8,128)(2,1)} %key_hbm.1, bf16[96,128,256]{2,1,0:T(8,128)(2,1)} %value_hbm.1, bf16[4,2048,128]{2,1,0:T(8,128)(2,1)} %shrink_hbm.1), custom_call_target="tpu_custom_call" | custom-call | flops 201326592 | bytes 13762560 | tf_op jit(solution)/shard_map/cached_attention/pallas_call | solution.py:258
  20.8 0.4 all-to-all-done
  21.3 1.6 %shrink_rows.1 = (f32[192,128]{1,0:T(8,128)S(1)}, bf16[192,128]{1,0:T(8,128)(2,1)}, bf16[192,128]{1,0:T(8,128)(2,1)S(1)}) custom-call(bf16[192,2176]{1,0:T(8,128)(2,1)S(1)} %bitcast.6, bf16[4,2048,128]{2,1,0:T(8,128)(2,1)S(1)} %get-tuple-element.29.shrink_ref), custom_call_target="tpu_custom_call" | custom-call | flops 402653184 | bytes 2883584 | tf_op jit(solution)/shard_map/shrink_rows/pallas_call | solution.py:115
  22.9 1.6 %collective-permute-start.2 = (bf16[192,128]{1,0:T(8,128)(2,1)}, bf16[192,128]{1,0:T(8,128)(2,1)S(1)}, u32[]{:S(2)}, u32[]{:S(2)}) collective-permute-start(bf16[192,128]{1,0:T(8,128)(2,1)} %get-tuple-element.30), channel_id=1, source_target_pairs={{0,1},{1,0},{2,3},{3,2},{4,5},{5,4},{6,7},{7,6},{8,9},{9,8},{10,11... | collective-permute-start | bytes 147464 | tf_op jit(solution)/shard_map/ppermute | solution.py:462
  24.4 2.6 %collective-permute-start.4 = (bf16[192,128]{1,0:T(8,128)(2,1)}, bf16[192,128]{1,0:T(8,128)(2,1)S(1)}, u32[]{:S(2)}, u32[]{:S(2)}) collective-permute-start(bf16[192,128]{1,0:T(8,128)(2,1)} %get-tuple-element.30), channel_id=1, source_target_pairs={{0,2},{1,3},{2,0},{3,1},{4,6},{5,7},{6,4},{7,5},{8,10},{9,11},{10,... | collective-permute-start | bytes 147464 | tf_op jit(solution)/shard_map/ppermute | solution.py:462
  27.0 0.2 collective-permute-start.5
  27.2 0.0 copy-done
  27.3 2.1 %early_products.1 = (f32[96,512]{1,0:T(8,128)S(1)}, bf16[4,2,64,256]{3,2,1,0:T(8,128)(2,1)S(1)}) custom-call(bf16[96,2048]{1,0:T(8,128)(2,1)S(1)} %copy-done, bf16[8192,256]{1,0:T(8,128)(2,1)} %refs_3_.3, bf16[8192,256]{1,0:T(8,128)(2,1)} %refs_4_.1, bf16[4,2,64,256]{3,2,1,0:T(8,128)(2,1)} %refs_3_.2), custom_call_target="tpu_custom_call" | custom-call | flops 201326592 | bytes 2097152 | tf_op jit(solution)/shard_map/early_products/pallas_call | solution.py:314
  29.3 0.0 collective-permute-done.2.refs_1_
  29.4 0.0 collective-permute-done.refs_0_
  29.4 1.1 %collective-permute-done.1.refs_1_ = bf16[96,2048]{1,0:T(8,128)(2,1)} collective-permute-done((bf16[96,2048]{1,0:T(8,128)(2,1)}, bf16[96,2048]{1,0:T(8,128)(2,1)}, u32[]{:S(2)}, u32[]{:S(2)}) %collective-permute-start.1) | collective-permute-done | bytes 393248 | tf_op jit(solution)/shard_map/ppermute | solution.py:462
  30.5 2.7 %collective-permute-start.3 = (bf16[96,2048]{1,0:T(8,128)(2,1)}, bf16[96,2048]{1,0:T(8,128)(2,1)S(1)}, u32[]{:S(2)}, u32[]{:S(2)}) collective-permute-start(bf16[96,2048]{1,0:T(8,128)(2,1)} %collective-permute-done.1.refs_1_), channel_id=1, source_target_pairs={{0,1},{1,0},{2,3},{3,2},{4,5},{5,4},{6,7},{7,6},{8,9},{9,8},{10,11... | collective-permute-start | bytes 1179656 | tf_op jit(solution)/shard_map/ppermute | solution.py:462
  33.2 0.6 %collective-permute-done.4.refs_2_ = bf16[192,128]{1,0:T(8,128)(2,1)S(1)} collective-permute-done((bf16[192,128]{1,0:T(8,128)(2,1)}, bf16[192,128]{1,0:T(8,128)(2,1)S(1)}, u32[]{:S(2)}, u32[]{:S(2)}) %collective-permute-start.4) | collective-permute-done | bytes 49184 | tf_op jit(solution)/shard_map/ppermute | solution.py:462
  33.8 0.0 collective-permute-done.5.refs_3_
  33.8 1.0 %expand_rows.1 = bf16[192,512]{1,0:T(8,128)(2,1)} custom-call(f32[192,128]{1,0:T(8,128)S(1)} %get-tuple-element.35.refs_0_, bf16[192,128]{1,0:T(8,128)(2,1)S(1)} %collective-permute-done.2.refs_1_, bf16[192,128]{1,0:T(8,128)(2,1)S(1)} %collective-permute-done.4.refs_2_, bf16[192,128]{1,0:T(8,128)(2,1)S(1)} %collective-permute-done.5.refs_3_, ...), custom_call_target="tpu_custom_call" | custom-call | flops 50331648 | bytes 458752 | tf_op jit(solution)/shard_map/expand_rows/pallas_call | solution.py:149
  34.8 3.8 %all-to-all-start.1 = ((bf16[8,24,512]{2,1,0:T(8,128)(2,1)}), bf16[8,24,512]{2,1,0:T(8,128)(2,1)S(1)}, u32[]{:S(2)}, u32[]{:S(2)}) async-start(bf16[8,24,512]{2,1,0:T(8,128)(2,1)} %bitcast.3), calls=%async_computation.1 | async-start | bytes 393216 | tf_op jit(solution)/shard_map/all_to_all | solution.py:495
  38.7 3.9 %base_products.1 = (f32[96,512]{1,0:T(8,128)S(1)}, bf16[2048,256]{1,0:T(8,128)(2,1)S(1)}, bf16[2048,256]{1,0:T(8,128)(2,1)S(1)}, f32[96,2048]{1,0:T(8,128)S(1)}) custom-call(bf16[96,2048]{1,0:T(8,128)(2,1)} %collective-permute-done.refs_0_, bf16[96,2048]{1,0:T(8,128)(2,1)} %collective-permute-done.1.refs_1_, f32[96,512]{1,0:T(8,128)S(1)} %get-tuple-element.41.refs_2_, ...), custom_call_target="tpu_custom_call" | custom-call | flops 402653184 | bytes 4980736 | tf_op jit(solution)/shard_map/base_products/pallas_call | solution.py:362
  42.5 0.0 copy-start.1
  42.6 0.0 copy-start.2
  42.6 1.7 %fusion = f32[96,256]{1,0:T(8,128)S(1)} fusion(bf16[96,2048]{1,0:T(8,128)(2,1)} %collective-permute-done.refs_0_, bf16[8192,256]{1,0:T(8,128)(2,1)} %refs_3_.3, s32[]{:T(128)S(6)} %select_n.3), kind=kOutput, calls=%fused_computation | convolution fusion | flops 100663296 | bytes 1540100 | tf_op jit(solution)/shard_map/dot_general | solution.py:528
  44.3 0.0 collective-permute-done.3.piece_ref
  44.3 0.5 %last_product.1.base_ref = f32[96,512]{1,0:T(8,128)S(1)} custom-call(bf16[96,2048]{1,0:T(8,128)(2,1)S(1)} %collective-permute-done.3.piece_ref, bf16[2048,256]{1,0:T(8,128)(2,1)S(1)} %get-tuple-element.43.keys, bf16[2048,256]{1,0:T(8,128)(2,1)S(1)} %get-tuple-element.44.values, f32[96,512]{1,0:T(8,128)S(1)} %pad_add_fusion.base_ref), custom_call_target="tpu_custom_call" | custom-call | flops 201326592 | bytes 2097152 | tf_op jit(solution)/shard_map/last_product/pallas_call | solution.py:392
  44.8 0.1 all-to-all-done.1
  44.9 0.0 copy-done.1
  44.9 0.0 copy-done.2
  44.9 1.5 %finish_rows.1 = (bf16[96,256]{1,0:T(8,128)(2,1)}, bf16[96,256]{1,0:T(8,128)(2,1)}, bf16[96,2048]{1,0:T(8,128)(2,1)}) custom-call(f32[96,512]{1,0:T(8,128)S(1)} %last_product.1.base_ref, bf16[192,512]{1,0:T(8,128)(2,1)S(1)} %bitcast.7, bf16[96,192]{1,0:T(8,128)(2,1)S(1)} %copy-done.2, bf16[96,2048]{1,0:T(8,128)(2,1)S(1)} %copy-done.1, ...), custom_call_target="tpu_custom_call" | custom-call | flops 786432 | bytes 1966080 | tf_op jit(solution)/shard_map/finish_rows/pallas_call | solution.py:441
  (1 shorter events, 0.0 us)
Async XLA Ops:
  2.9 18.3 %all-to-all-start = ((bf16[8,24,2176]{2,1,0:T(8,128)(2,1)}), bf16[8,24,2176]{2,1,0:T(8,128)(2,1)S(1)}, u32[]{:S(2)}, u32[]{:S(2)}) async-start(bf16[8,24,2176]{2,1,0:T(8,128)(2,1)} %bitcast.8), calls=%async_computation | async-start | bytes 1671168 | tf_op jit(solution)/shard_map/all_to_all | solution.py:495
  8.1 19.1 %copy-start = (bf16[96,2048]{1,0:T(8,128)(2,1)S(1)}, bf16[96,2048]{1,0:T(8,128)(2,1)}, u32[]{:S(2)}) copy-start(bf16[96,2048]{1,0:T(8,128)(2,1)} %refs_0_) | copy-start | bytes 1179652
  8.1 21.2 %collective-permute-start = (bf16[96,2048]{1,0:T(8,128)(2,1)}, bf16[96,2048]{1,0:T(8,128)(2,1)}, u32[]{:S(2)}, u32[]{:S(2)}) collective-permute-start(bf16[96,2048]{1,0:T(8,128)(2,1)} %refs_0_), channel_id=1, source_target_pairs={{0,1},{1,0},{2,3},{3,2},{4,5},{5,4},{6,7},{7,6},{8,9},{9,8},{10,11... | collective-permute-start | bytes 1179656 | tf_op jit(solution)/shard_map/ppermute | solution.py:462
  9.8 20.7 %collective-permute-start.1 = (bf16[96,2048]{1,0:T(8,128)(2,1)}, bf16[96,2048]{1,0:T(8,128)(2,1)}, u32[]{:S(2)}, u32[]{:S(2)}) collective-permute-start(bf16[96,2048]{1,0:T(8,128)(2,1)} %refs_0_), channel_id=1, source_target_pairs={{0,2},{1,3},{2,0},{3,1},{4,6},{5,7},{6,4},{7,5},{8,10},{9,11},{10,... | collective-permute-start | bytes 1179656 | tf_op jit(solution)/shard_map/ppermute | solution.py:462
  22.9 6.5 %collective-permute-start.2 = (bf16[192,128]{1,0:T(8,128)(2,1)}, bf16[192,128]{1,0:T(8,128)(2,1)S(1)}, u32[]{:S(2)}, u32[]{:S(2)}) collective-permute-start(bf16[192,128]{1,0:T(8,128)(2,1)} %get-tuple-element.30), channel_id=1, source_target_pairs={{0,1},{1,0},{2,3},{3,2},{4,5},{5,4},{6,7},{7,6},{8,9},{9,8},{10,11... | collective-permute-start | bytes 147464 | tf_op jit(solution)/shard_map/ppermute | solution.py:462
  24.4 9.4 %collective-permute-start.4 = (bf16[192,128]{1,0:T(8,128)(2,1)}, bf16[192,128]{1,0:T(8,128)(2,1)S(1)}, u32[]{:S(2)}, u32[]{:S(2)}) collective-permute-start(bf16[192,128]{1,0:T(8,128)(2,1)} %get-tuple-element.30), channel_id=1, source_target_pairs={{0,2},{1,3},{2,0},{3,1},{4,6},{5,7},{6,4},{7,5},{8,10},{9,11},{10,... | collective-permute-start | bytes 147464 | tf_op jit(solution)/shard_map/ppermute | solution.py:462
  27.0 6.8 %collective-permute-start.5 = (bf16[192,128]{1,0:T(8,128)(2,1)}, bf16[192,128]{1,0:T(8,128)(2,1)S(1)}, u32[]{:S(2)}, u32[]{:S(2)}) collective-permute-start(bf16[192,128]{1,0:T(8,128)(2,1)} %get-tuple-element.30), channel_id=1, source_target_pairs={{0,3},{1,2},{2,1},{3,0},{4,7},{5,6},{6,5},{7,4},{8,11},{9,10},{10,... | collective-permute-start | bytes 147464 | tf_op jit(solution)/shard_map/ppermute | solution.py:462
  30.5 13.8 %collective-permute-start.3 = (bf16[96,2048]{1,0:T(8,128)(2,1)}, bf16[96,2048]{1,0:T(8,128)(2,1)S(1)}, u32[]{:S(2)}, u32[]{:S(2)}) collective-permute-start(bf16[96,2048]{1,0:T(8,128)(2,1)} %collective-permute-done.1.refs_1_), channel_id=1, source_target_pairs={{0,1},{1,0},{2,3},{3,2},{4,5},{5,4},{6,7},{7,6},{8,9},{9,8},{10,11... | collective-permute-start | bytes 1179656 | tf_op jit(solution)/shard_map/ppermute | solution.py:462
  34.8 10.0 %all-to-all-start.1 = ((bf16[8,24,512]{2,1,0:T(8,128)(2,1)}), bf16[8,24,512]{2,1,0:T(8,128)(2,1)S(1)}, u32[]{:S(2)}, u32[]{:S(2)}) async-start(bf16[8,24,512]{2,1,0:T(8,128)(2,1)} %bitcast.3), calls=%async_computation.1 | async-start | bytes 393216 | tf_op jit(solution)/shard_map/all_to_all | solution.py:495
  42.5 2.3 %copy-start.1 = (bf16[96,2048]{1,0:T(8,128)(2,1)S(1)}, bf16[96,2048]{1,0:T(8,128)(2,1)}, u32[]{:S(2)}) copy-start(bf16[96,2048]{1,0:T(8,128)(2,1)} %query_ref.1) | copy-start | bytes 1179652
  42.6 2.3 %copy-start.2 = (bf16[96,192]{1,0:T(8,128)(2,1)S(1)}, bf16[96,192]{1,0:T(8,128)(2,1)}, u32[]{:S(2)}) copy-start(bf16[96,192]{1,0:T(8,128)(2,1)} %get-tuple-element.46.pick_ref) | copy-start | bytes 110596

commit v7 on v6

--- a/solution.py
+++ b/solution.py
@@ -281,17 +281,22 @@
     )(*(pinned(x) for x in (lengths, queries, keys, values, weights)))
 
 
-def owner_of(place, p, parts):
-    return place ^ p if parts == 4 else lax.rem(place + parts - p, parts)
+def owner_of(p, parts):
+    place = lax.axis_index("tp")
+    if parts != 4:
+        return lax.rem(place + parts - p, parts)
+    if p in (0, 3):
+        return place ^ p
+    odd = lax.rem(lax.axis_index("rep"), 2)
+    return place ^ (p + odd if p == 1 else p - odd)
 
 
 def early_kernel(count, total, *refs):
     pieces, (key_hbm, value_hbm, up_hbm, out_ref, up_ref, keys, values, sems) = refs[:count], refs[count:]
     shard, width = keys.shape[1:]
-    place = lax.axis_index("tp")
     copies = []
     for p in range(count):
-        rows = pl.ds(pl.multiple_of(owner_of(place, p, total) * shard, shard), shard)
+        rows = pl.ds(pl.multiple_of(owner_of(p, total) * shard, shard), shard)
         copies.append(pltpu.make_async_copy(key_hbm.at[rows], keys.at[p], sems.at[0, p]))
         copies.append(pltpu.make_async_copy(value_hbm.at[rows], values.at[p], sems.at[1, p]))
     copies.append(pltpu.make_async_copy(up_hbm, up_ref, sems.at[0, count]))
@@ -329,10 +334,9 @@
     pieces, refs = refs[:count], refs[count:]
     so_far, key_hbm, value_hbm, mean_hbm, out_ref, last_keys, last_values, mean_ref, keys, values, sems = refs
     shard, width = last_keys.shape
-    place = lax.axis_index("tp")
 
     def copies(p):
-        rows = pl.ds(pl.multiple_of(owner_of(place, p + first, total) * shard, shard), shard)
+        rows = pl.ds(pl.multiple_of(owner_of(p + first, total) * shard, shard), shard)
         key_to, value_to = (last_keys, last_values) if p == count else (keys.at[p], values.at[p])
         key_copy = pltpu.make_async_copy(key_hbm.at[rows], key_to, sems.at[0, p]) if p > 0 else None
         return key_copy, pltpu.make_async_copy(value_hbm.at[rows], value_to, sems.at[1, p])
@@ -462,6 +466,11 @@
     return lax.ppermute(x, "tp", [(i, i ^ mask) for i in range(size)])
 
 
+def cross(x, masks, size):
+    pairs = [(r * size + i, r * size + (i ^ masks[r % 2])) for r in range(lax.axis_size("rep")) for i in range(size)]
+    return lax.ppermute(x, ("rep", "tp"), pairs)
+
+
 def turn(x, shift, size):
     return lax.ppermute(x, "tp", [(i, (i + shift) % size) for i in range(size)])
 
@@ -498,8 +507,8 @@
     arrived = all_to_all(outgoing)
 
     if parts == 4:
-        one = swap(hidden_in, 1, parts)
-        two = swap(hidden_in, 2, parts)
+        one = cross(hidden_in, (1, 2), parts)
+        two = cross(hidden_in, (2, 1), parts)
     mean, lse, shrink_here = cached_attention(cache_lengths, queries, cache_keys, cached_value_rows, shrink_weights)
     arrived, lse = lax.optimization_barrier((arrived, lse))
     partial_rows, sent, flags = shrink(arrived, shrink_here)
@@ -516,14 +525,16 @@
         received[0], base = lax.optimization_barrier((received[0], base))
         sums = [partial_rows] + received
         one, two, _ = lax.optimization_barrier((one, two, received[0]))
-        pieces = [hidden_in, one, two, swap(two, 1, parts)]
+        far = jnp.where(lax.rem(lax.axis_index("rep"), 2) == 1, one, two)
+        far, sums[0] = lax.optimization_barrier((far, partial_rows))
+        pieces = [hidden_in, one, two, swap(far, 1, parts)]
     else:
         sums = [partial_rows] + others(sent, parts)
     deltas = expand(sums, flags, up_here)
     back = all_to_all(deltas)
     deltas, *between = lax.optimization_barrier((deltas, *pieces[early:-1]))
     base, *last, mean = base_products(between, parts, base, *matrices, mean)
-    owner = owner_of(lax.axis_index("tp"), early, parts)
+    owner = owner_of(early, parts)
     key_rows = lax.dynamic_slice_in_dim(base_key_matrix, owner * shard_width, shard_width, 0)
     more = jnp.dot(between[0], key_rows, preferred_element_type=jnp.float32)
     base = base + jnp.concatenate([more, jnp.zeros_like(more)], axis=1)

time: 46.7 us -> 46.5 us (level)
  starting transfers between devices: 20.3 us -> 18.6 us
  other arithmetic: 0.02 us -> 1.07 us
  local copies, waits for them, and re-layouts: 0.02 us -> 1.01 us
  waiting for transfers between devices: 2.32 us -> 1.83 us
    ppermute x6 -> x4, starting transfers between devices: 11.3 us -> 5.46 us  [swap(): return lax.ppermute(x, 'tp', [(i, i ^ mask) for i in range(size)])]
    ppermute x0 -> x2, starting transfers between devices: none -> 4.17 us  [cross(): return lax.ppermute(x, ('rep', 'tp'), pairs)]
    select_n x0 -> x1, other arithmetic: none -> 1.05 us  [shards(): far = jnp.where(lax.rem(lax.axis_index('rep'), 2) == 1, one, two)]
    unnamed x6, local copies, waits for them, and re-layouts: 0.02 us -> 1.01 us
    ppermute x6 -> x4, waiting for transfers between devices: 1.78 us -> 0.98 us  [swap(): return lax.ppermute(x, 'tp', [(i, i ^ mask) for i in range(size)])]
  transfers between devices with their start and end apart: 8 -> 8, of which waited for: 4 -> 3; matrix products, arithmetic and copies ran while one was open for 4% -> 6% of each run, Pallas kernels for 38% -> 38%
where the time goes in v7:
time: 46.5 us; the launch traced here: 46 us
  Pallas kernels  21.2 us (46%)
  starting transfers between devices  18.6 us (40%)
  waiting for transfers between devices  1.83 us (4%)
  matrix products  1.58 us (3%)
  other arithmetic  1.07 us (2%)
  local copies, waits for them, and re-layouts  1.01 us (2%)
  between operations  0.73 us (2%)
    all_to_all x2, starting transfers between devices, all_to_all(): lax.all_to_all(x, 'rep', split_axis=0, concat_axis=0, tiled=True)  8.98 us
    pallas_call x1, Pallas kernels, cached_attention(): pl.pallas_call(functools.partial(cached_kernel, heads, group), name='cach...  8.45 us
    ppermute x4, starting transfers between devices, swap(): return lax.ppermute(x, 'tp', [(i, i ^ mask) for i in range(size)])  5.46 us
    ppermute x2, starting transfers between devices, cross(): return lax.ppermute(x, ('rep', 'tp'), pairs)  4.17 us
    pallas_call x1, Pallas kernels, base_products(): pl.pallas_call(functools.partial(base_kernel, total - 1 - count, total),...  3.76 us
    pallas_call x1, Pallas kernels, pack(): pl.pallas_call(functools.partial(pack_kernel, capacity), name='pack_rows'...  2.31 us
    pallas_call x1, Pallas kernels, early_products(): pl.pallas_call(functools.partial(early_kernel, count, total), name='early...  2.08 us
    pallas_call x1, Pallas kernels, shrink(): pl.pallas_call(shrink_kernel, name='shrink_rows', out_shape=(jax.ShapeDty...  1.61 us
  transfers between devices with their start and end apart: 8, of which 3 were waited for; matrix products, arithmetic and copies ran while one was open for 6% of the time, Pallas kernels for 38%

profile of v7, /device:TPU:0, one launch (start us, length us, event | category | flops | bytes accessed | tf_op | source)
XLA Modules:
  0.0 46.0 jit_solution(1881339191022022184)
XLA Ops:
  0.6 2.3 %pack_rows.1 = (bf16[192,2176]{1,0:T(8,128)(2,1)}, bf16[96,192]{1,0:T(8,128)(2,1)}) custom-call(s32[24]{0:T(128)} %bitcast.9, s32[24]{0:T(128)} %slot_ref.1, bf16[96,2048]{1,0:T(8,128)(2,1)} %refs_0_), custom_call_target="tpu_custom_call" | custom-call | flops 75497472 | bytes 1179648 | tf_op jit(solution)/shard_map/pack_rows/pallas_call | solution.py:81
  2.9 5.2 %all-to-all-start = ((bf16[8,24,2176]{2,1,0:T(8,128)(2,1)}), bf16[8,24,2176]{2,1,0:T(8,128)(2,1)S(1)}, u32[]{:S(2)}, u32[]{:S(2)}) async-start(bf16[8,24,2176]{2,1,0:T(8,128)(2,1)} %bitcast.8), calls=%async_computation | async-start | bytes 1671168 | tf_op jit(solution)/shard_map/all_to_all | solution.py:504
  8.1 1.6 %collective-permute-start = (bf16[96,2048]{1,0:T(8,128)(2,1)}, bf16[96,2048]{1,0:T(8,128)(2,1)S(1)}, u32[]{:S(2)}, u32[]{:S(2)}) collective-permute-start(bf16[96,2048]{1,0:T(8,128)(2,1)} %refs_0_), channel_id=1, source_target_pairs={{0,1},{1,0},{2,3},{3,2},{4,6},{5,7},{6,4},{7,5},{8,9},{9,8},{10,11... | collective-permute-start | bytes 1179656 | tf_op jit(solution)/shard_map/ppermute | solution.py:471
  9.7 2.6 %collective-permute-start.1 = (bf16[96,2048]{1,0:T(8,128)(2,1)}, bf16[96,2048]{1,0:T(8,128)(2,1)}, u32[]{:S(2)}, u32[]{:S(2)}) collective-permute-start(bf16[96,2048]{1,0:T(8,128)(2,1)} %refs_0_), channel_id=1, source_target_pairs={{0,2},{1,3},{2,0},{3,1},{4,5},{5,4},{6,7},{7,6},{8,10},{9,11},{10,... | collective-permute-start | bytes 1179656 | tf_op jit(solution)/shard_map/ppermute | solution.py:471
  12.3 8.4 %cached_attention.1 = (f32[96,2048]{1,0:T(8,128)}, f32[96,128]{1,0:T(8,128)S(1)}, bf16[4,2048,128]{2,1,0:T(8,128)(2,1)S(1)}) custom-call(s32[96]{0:T(128)} %length_hbm.1, bf16[96,2048]{1,0:T(8,128)(2,1)} %query_ref.1, bf16[96,128,256]{2,1,0:T(8,128)(2,1)} %key_hbm.1, bf16[96,128,256]{2,1,0:T(8,128)(2,1)} %value_hbm.1, bf16[4,2048,128]{2,1,0:T(8,128)(2,1)} %shrink_hbm.1), custom_call_target="tpu_custom_call" | custom-call | flops 201326592 | bytes 13762560 | tf_op jit(solution)/shard_map/cached_attention/pallas_call | solution.py:258
  20.7 0.5 %all-to-all-done = bf16[8,24,2176]{2,1,0:T(8,128)(2,1)S(1)} async-done(((bf16[8,24,2176]{2,1,0:T(8,128)(2,1)}), bf16[8,24,2176]{2,1,0:T(8,128)(2,1)S(1)}, u32[]{:S(2)}, u32[]{:S(2)}) %all-to-all-start) | async-done | bytes 835616 | tf_op jit(solution)/shard_map/all_to_all | solution.py:504
  21.3 1.6 %shrink_rows.1 = (f32[192,128]{1,0:T(8,128)S(1)}, bf16[192,128]{1,0:T(8,128)(2,1)}, bf16[192,128]{1,0:T(8,128)(2,1)S(1)}) custom-call(bf16[192,2176]{1,0:T(8,128)(2,1)S(1)} %bitcast.6, bf16[4,2048,128]{2,1,0:T(8,128)(2,1)S(1)} %get-tuple-element.31.shrink_ref), custom_call_target="tpu_custom_call" | custom-call | flops 402653184 | bytes 2883584 | tf_op jit(solution)/shard_map/shrink_rows/pallas_call | solution.py:115
  22.9 1.6 %collective-permute-start.2 = (bf16[192,128]{1,0:T(8,128)(2,1)}, bf16[192,128]{1,0:T(8,128)(2,1)S(1)}, u32[]{:S(2)}, u32[]{:S(2)}) collective-permute-start(bf16[192,128]{1,0:T(8,128)(2,1)} %get-tuple-element.32), channel_id=1, source_target_pairs={{0,1},{1,0},{2,3},{3,2},{4,5},{5,4},{6,7},{7,6},{8,9},{9,8},{10,11... | collective-permute-start | bytes 147464 | tf_op jit(solution)/shard_map/ppermute | solution.py:466
  24.4 2.6 %collective-permute-start.4 = (bf16[192,128]{1,0:T(8,128)(2,1)}, bf16[192,128]{1,0:T(8,128)(2,1)S(1)}, u32[]{:S(2)}, u32[]{:S(2)}) collective-permute-start(bf16[192,128]{1,0:T(8,128)(2,1)} %get-tuple-element.32), channel_id=1, source_target_pairs={{0,2},{1,3},{2,0},{3,1},{4,6},{5,7},{6,4},{7,5},{8,10},{9,11},{10,... | collective-permute-start | bytes 147464 | tf_op jit(solution)/shard_map/ppermute | solution.py:466
  27.0 0.2 collective-permute-start.5
  27.2 0.0 copy-start
  27.3 1.0 %copy-done = bf16[96,2048]{1,0:T(8,128)(2,1)S(1)} copy-done((bf16[96,2048]{1,0:T(8,128)(2,1)S(1)}, bf16[96,2048]{1,0:T(8,128)(2,1)}, u32[]{:S(2)}) %copy-start) | copy-done | bytes 393240
  28.2 2.1 %early_products.1 = (f32[96,512]{1,0:T(8,128)S(1)}, bf16[4,2,64,256]{3,2,1,0:T(8,128)(2,1)S(1)}) custom-call(bf16[96,2048]{1,0:T(8,128)(2,1)S(1)} %copy-done, bf16[8192,256]{1,0:T(8,128)(2,1)} %refs_3_.3, bf16[8192,256]{1,0:T(8,128)(2,1)} %refs_4_.1, bf16[4,2,64,256]{3,2,1,0:T(8,128)(2,1)} %refs_3_.2), custom_call_target="tpu_custom_call" | custom-call | flops 201326592 | bytes 2097152 | tf_op jit(solution)/shard_map/early_products/pallas_call | solution.py:319
  30.3 0.0 collective-permute-done.2.refs_1_
  30.3 0.0 collective-permute-done.refs_0_
  30.4 0.0 collective-permute-done.1.refs_1_
  30.4 1.0 %broadcast_select_fusion = bf16[96,2048]{1,0:T(8,128)(2,1)S(1)} fusion(bf16[96,2048]{1,0:T(8,128)(2,1)S(1)} %collective-permute-done.refs_0_, bf16[96,2048]{1,0:T(8,128)(2,1)} %collective-permute-done.1.refs_1_, pred[]{:T(512)S(6)} %eq.3), kind=kLoop, calls=%fused_computation.2 | loop fusion | flops 196608 | bytes 1179649 | tf_op jit(solution)/shard_map/jit(_where)/select_n | solution.py:528
  31.4 1.1 %collective-permute-start.3 = (bf16[96,2048]{1,0:T(8,128)(2,1)S(1)}, bf16[96,2048]{1,0:T(8,128)(2,1)S(1)}, u32[]{:S(2)}, u32[]{:S(2)}) collective-permute-start(bf16[96,2048]{1,0:T(8,128)(2,1)S(1)} %broadcast_select_fusion), channel_id=1, source_target_pairs={{0,1},{1,0},{2,3},{3,2},{4,5},{5,4},{6,7},{7,6},{8,9},{9,8},{10,11... | collective-permute-start | bytes 1179656 | tf_op jit(solution)/shard_map/ppermute | solution.py:466
  32.5 0.0 collective-permute-done.4.refs_2_
  32.5 1.0 %collective-permute-done.5.refs_3_ = bf16[192,128]{1,0:T(8,128)(2,1)S(1)} collective-permute-done((bf16[192,128]{1,0:T(8,128)(2,1)}, bf16[192,128]{1,0:T(8,128)(2,1)S(1)}, u32[]{:S(2)}, u32[]{:S(2)}) %collective-permute-start.5) | collective-permute-done | bytes 49184 | tf_op jit(solution)/shard_map/ppermute | solution.py:466
  33.5 1.0 %expand_rows.1 = bf16[192,512]{1,0:T(8,128)(2,1)} custom-call(f32[192,128]{1,0:T(8,128)S(1)} %get-tuple-element.40.refs_0_, bf16[192,128]{1,0:T(8,128)(2,1)S(1)} %collective-permute-done.2.refs_1_, bf16[192,128]{1,0:T(8,128)(2,1)S(1)} %collective-permute-done.4.refs_2_, bf16[192,128]{1,0:T(8,128)(2,1)S(1)} %collective-permute-done.5.refs_3_, ...), custom_call_target="tpu_custom_call" | custom-call | flops 50331648 | bytes 458752 | tf_op jit(solution)/shard_map/expand_rows/pallas_call | solution.py:149
  34.5 3.8 %all-to-all-start.1 = ((bf16[8,24,512]{2,1,0:T(8,128)(2,1)}), bf16[8,24,512]{2,1,0:T(8,128)(2,1)S(1)}, u32[]{:S(2)}, u32[]{:S(2)}) async-start(bf16[8,24,512]{2,1,0:T(8,128)(2,1)} %bitcast.3), calls=%async_computation.1 | async-start | bytes 393216 | tf_op jit(solution)/shard_map/all_to_all | solution.py:504
  38.3 3.8 %base_products.1 = (f32[96,512]{1,0:T(8,128)S(1)}, bf16[2048,256]{1,0:T(8,128)(2,1)S(1)}, bf16[2048,256]{1,0:T(8,128)(2,1)S(1)}, f32[96,2048]{1,0:T(8,128)S(1)}) custom-call(bf16[96,2048]{1,0:T(8,128)(2,1)S(1)} %collective-permute-done.refs_0_, bf16[96,2048]{1,0:T(8,128)(2,1)} %collective-permute-done.1.refs_1_, f32[96,512]{1,0:T(8,128)S(1)} %get-tuple-element.45.refs_2_, ...), custom_call_target="tpu_custom_call" | custom-call | flops 402653184 | bytes 4980736 | tf_op jit(solution)/shard_map/base_products/pallas_call | solution.py:366
  42.1 0.0 copy-start.1
  42.1 0.0 copy-start.2
  42.1 1.6 %fusion = f32[96,256]{1,0:T(8,128)S(1)} fusion(bf16[96,2048]{1,0:T(8,128)(2,1)S(1)} %collective-permute-done.refs_0_, bf16[8192,256]{1,0:T(8,128)(2,1)} %refs_3_.3, s32[]{:T(128)S(6)} %select_n.13), kind=kOutput, calls=%fused_computation | convolution fusion | flops 100663296 | bytes 1540100 | tf_op jit(solution)/shard_map/dot_general | solution.py:539
  43.7 0.0 collective-permute-done.3.piece_ref
  43.7 0.5 %last_product.1.base_ref = f32[96,512]{1,0:T(8,128)S(1)} custom-call(bf16[96,2048]{1,0:T(8,128)(2,1)S(1)} %collective-permute-done.3.piece_ref, bf16[2048,256]{1,0:T(8,128)(2,1)S(1)} %get-tuple-element.47.keys, bf16[2048,256]{1,0:T(8,128)(2,1)S(1)} %get-tuple-element.48.values, f32[96,512]{1,0:T(8,128)S(1)} %pad_add_fusion.base_ref), custom_call_target="tpu_custom_call" | custom-call | flops 201326592 | bytes 2097152 | tf_op jit(solution)/shard_map/last_product/pallas_call | solution.py:396
  44.2 0.3 all-to-all-done.1
  44.5 0.0 copy-done.1
  44.5 0.0 copy-done.2
  44.5 1.5 %finish_rows.1 = (bf16[96,256]{1,0:T(8,128)(2,1)}, bf16[96,256]{1,0:T(8,128)(2,1)}, bf16[96,2048]{1,0:T(8,128)(2,1)}) custom-call(f32[96,512]{1,0:T(8,128)S(1)} %last_product.1.base_ref, bf16[192,512]{1,0:T(8,128)(2,1)S(1)} %bitcast.7, bf16[96,192]{1,0:T(8,128)(2,1)S(1)} %copy-done.2, bf16[96,2048]{1,0:T(8,128)(2,1)S(1)} %copy-done.1, ...), custom_call_target="tpu_custom_call" | custom-call | flops 786432 | bytes 1966080 | tf_op jit(solution)/shard_map/finish_rows/pallas_call | solution.py:445
  (1 shorter events, 0.0 us)
Async XLA Ops:
  2.9 18.3 %all-to-all-start = ((bf16[8,24,2176]{2,1,0:T(8,128)(2,1)}), bf16[8,24,2176]{2,1,0:T(8,128)(2,1)S(1)}, u32[]{:S(2)}, u32[]{:S(2)}) async-start(bf16[8,24,2176]{2,1,0:T(8,128)(2,1)} %bitcast.8), calls=%async_computation | async-start | bytes 1671168 | tf_op jit(solution)/shard_map/all_to_all | solution.py:504
  8.1 22.2 %collective-permute-start = (bf16[96,2048]{1,0:T(8,128)(2,1)}, bf16[96,2048]{1,0:T(8,128)(2,1)S(1)}, u32[]{:S(2)}, u32[]{:S(2)}) collective-permute-start(bf16[96,2048]{1,0:T(8,128)(2,1)} %refs_0_), channel_id=1, source_target_pairs={{0,1},{1,0},{2,3},{3,2},{4,6},{5,7},{6,4},{7,5},{8,9},{9,8},{10,11... | collective-permute-start | bytes 1179656 | tf_op jit(solution)/shard_map/ppermute | solution.py:471
  9.7 20.7 %collective-permute-start.1 = (bf16[96,2048]{1,0:T(8,128)(2,1)}, bf16[96,2048]{1,0:T(8,128)(2,1)}, u32[]{:S(2)}, u32[]{:S(2)}) collective-permute-start(bf16[96,2048]{1,0:T(8,128)(2,1)} %refs_0_), channel_id=1, source_target_pairs={{0,2},{1,3},{2,0},{3,1},{4,5},{5,4},{6,7},{7,6},{8,10},{9,11},{10,... | collective-permute-start | bytes 1179656 | tf_op jit(solution)/shard_map/ppermute | solution.py:471
  22.9 7.5 %collective-permute-start.2 = (bf16[192,128]{1,0:T(8,128)(2,1)}, bf16[192,128]{1,0:T(8,128)(2,1)S(1)}, u32[]{:S(2)}, u32[]{:S(2)}) collective-permute-start(bf16[192,128]{1,0:T(8,128)(2,1)} %get-tuple-element.32), channel_id=1, source_target_pairs={{0,1},{1,0},{2,3},{3,2},{4,5},{5,4},{6,7},{7,6},{8,9},{9,8},{10,11... | collective-permute-start | bytes 147464 | tf_op jit(solution)/shard_map/ppermute | solution.py:466
  24.4 8.1 %collective-permute-start.4 = (bf16[192,128]{1,0:T(8,128)(2,1)}, bf16[192,128]{1,0:T(8,128)(2,1)S(1)}, u32[]{:S(2)}, u32[]{:S(2)}) collective-permute-start(bf16[192,128]{1,0:T(8,128)(2,1)} %get-tuple-element.32), channel_id=1, source_target_pairs={{0,2},{1,3},{2,0},{3,1},{4,6},{5,7},{6,4},{7,5},{8,10},{9,11},{10,... | collective-permute-start | bytes 147464 | tf_op jit(solution)/shard_map/ppermute | solution.py:466
  27.0 6.4 %collective-permute-start.5 = (bf16[192,128]{1,0:T(8,128)(2,1)}, bf16[192,128]{1,0:T(8,128)(2,1)S(1)}, u32[]{:S(2)}, u32[]{:S(2)}) collective-permute-start(bf16[192,128]{1,0:T(8,128)(2,1)} %get-tuple-element.32), channel_id=1, source_target_pairs={{0,3},{1,2},{2,1},{3,0},{4,7},{5,6},{6,5},{7,4},{8,11},{9,10},{10,... | collective-permute-start | bytes 147464 | tf_op jit(solution)/shard_map/ppermute | solution.py:466
  27.2 1.0 %copy-start = (bf16[96,2048]{1,0:T(8,128)(2,1)S(1)}, bf16[96,2048]{1,0:T(8,128)(2,1)}, u32[]{:S(2)}) copy-start(bf16[96,2048]{1,0:T(8,128)(2,1)} %refs_0_) | copy-start | bytes 1179652
  31.4 12.3 %collective-permute-start.3 = (bf16[96,2048]{1,0:T(8,128)(2,1)S(1)}, bf16[96,2048]{1,0:T(8,128)(2,1)S(1)}, u32[]{:S(2)}, u32[]{:S(2)}) collective-permute-start(bf16[96,2048]{1,0:T(8,128)(2,1)S(1)} %broadcast_select_fusion), channel_id=1, source_target_pairs={{0,1},{1,0},{2,3},{3,2},{4,5},{5,4},{6,7},{7,6},{8,9},{9,8},{10,11... | collective-permute-start | bytes 1179656 | tf_op jit(solution)/shard_map/ppermute | solution.py:466
  34.5 10.0 %all-to-all-start.1 = ((bf16[8,24,512]{2,1,0:T(8,128)(2,1)}), bf16[8,24,512]{2,1,0:T(8,128)(2,1)S(1)}, u32[]{:S(2)}, u32[]{:S(2)}) async-start(bf16[8,24,512]{2,1,0:T(8,128)(2,1)} %bitcast.3), calls=%async_computation.1 | async-start | bytes 393216 | tf_op jit(solution)/shard_map/all_to_all | solution.py:504
  42.1 2.5 %copy-start.1 = (bf16[96,2048]{1,0:T(8,128)(2,1)S(1)}, bf16[96,2048]{1,0:T(8,128)(2,1)}, u32[]{:S(2)}) copy-start(bf16[96,2048]{1,0:T(8,128)(2,1)} %query_ref.1) | copy-start | bytes 1179652
  42.1 2.5 %copy-start.2 = (bf16[96,192]{1,0:T(8,128)(2,1)S(1)}, bf16[96,192]{1,0:T(8,128)(2,1)}, u32[]{:S(2)}) copy-start(bf16[96,192]{1,0:T(8,128)(2,1)} %get-tuple-element.50.pick_ref) | copy-start | bytes 110596
